TPU v7x, 128 devices: a whole 4x4x4 slice. The times are simulated.
128 devices in a mesh: col: 16 (over y, z), dp: 4 (over x_lo, core), strip: 2 (over x_hi).
Axes of the slice: x: 4 (x_hi: 2, x_lo: 2; x = x_hi * 2 + x_lo), y: 4, z: 4, core: 2. Of those that a mesh axis runs over, the one named last changes fastest.
Arguments:
- stem: bfloat16 [16, 4, 32, 360], P('dp', 'strip'), may hold values from -6 to 6
- labels: int32 [16, 4, 32], P('dp', 'strip'), may hold values from 0 to 149
- up_proj: bfloat16 [16, 720, 360], P('col'), may hold values from -0.21875 to 0.21875
- mix_proj: bfloat16 [16, 360, 360], P('col'), may hold values from -0.3125 to 0.3125
- down_proj: bfloat16 [16, 360, 720], P('col'), may hold values from -0.3125 to 0.3125
- dw_kernel: bfloat16 [16, 9, 360], P('col'), may hold values from -2 to 2
- gain1: float32 [16, 360], P('col'), may hold values from 0.7498942 to 1
- gain2: float32 [16, 720], P('col'), may hold values from 0.7498942 to 1
- lat_one: bfloat16 [360, 512], replicated, may hold values from -0.3125 to 0.3125
- lat_two: bfloat16 [720, 512], replicated, may hold values from -0.21875 to 0.21875
- classifier: bfloat16 [512, 150], replicated, may hold values from -1.0546875 to 1.0546875
Outputs:
- grad_up: float32 [16, 720, 360], P('col', ('dp', 'strip'))
- grad_mix: float32 [16, 360, 360], P('col', ('dp', 'strip'))
- grad_down: float32 [16, 360, 720], P('col', ('dp', 'strip'))
- grad_kernel: float32 [16, 9, 360], P('col', None, ('dp', 'strip'))
- grad_stem: float32 [16, 4, 32, 360], P('dp', 'strip', 'col')
All inputs are finite; a program needn't handle non-finite values.
Results may differ from a plain program's by a relative error of at most 0.034.
Values sent between devices are 32-bit elements; how exact they have to be, the bound alone decides.
No kernel may reach another device: no remote copies, remote signals or barrier semaphores. Data moves between devices by JAX's collectives and lax.ppermute only.
A program may use at most 64 MiB of HBM per device.

v0:
```python
import jax
import jax.numpy as jnp
from jax import lax
from jax.sharding import PartitionSpec as P

loss_scale = 64.0
root_coef = 0.7978845608028654
cube_coef = 0.044715


def extended(block, sides, width):
    for axis, dim in sides:
        count = lax.axis_size(axis)
        forward = [(i, i + 1) for i in range(count - 1)]
        backward = [(target, source) for source, target in forward]
        low = lax.ppermute(
            lax.slice_in_dim(block, block.shape[dim] - width, None, axis=dim), axis, forward
        )
        high = lax.ppermute(lax.slice_in_dim(block, 0, width, axis=dim), axis, backward)
        block = jnp.concatenate([low, block, high], axis=dim)
    return block


def passed_along(block, axis, distance):
    devices = range(lax.axis_size(axis))
    route = [(i - distance, i) for i in devices if i - distance in devices]
    return lax.ppermute(block, axis, route)


def gelu_pair(values):
    inner = root_coef * (values + cube_coef * values * values * values)
    tangent = jnp.tanh(inner)
    result = 0.5 * values * (1.0 + tangent)
    slope = 0.5 * (1.0 + tangent) + 0.5 * values * (1.0 - tangent * tangent) * root_coef * (
        1.0 + 3.0 * cube_coef * values * values
    )
    return (result, slope)


def project(left, matrix):
    flat = left.reshape(-1, left.shape[-1])
    out = jnp.dot(flat, matrix, preferred_element_type=jnp.float32)
    return out.reshape(left.shape[:-1] + (matrix.shape[1],))


def project_back(left, matrix):
    flat = left.reshape(-1, left.shape[-1])
    out = lax.dot_general(
        flat, matrix, (((1,), (1,)), ((), ())), preferred_element_type=jnp.float32
    )
    return out.reshape(left.shape[:-1] + (matrix.shape[0],))


def outer_sum(left, right):
    return lax.dot_general(
        left.reshape(-1, left.shape[-1]),
        right.reshape(-1, right.shape[-1]),
        (((0,), (0,)), ((), ())),
        preferred_element_type=jnp.float32,
    )


def upsample(values):
    return jnp.repeat(jnp.repeat(values, 2, axis=-3), 2, axis=-2)


def pool_sum(values):
    shape = values.shape
    return values.reshape(shape[:-3] + (shape[-3] // 2, 2, shape[-2] // 2, 2, shape[-1])).sum(
        axis=(-4, -2)
    )


def depthwise_apply(padded, kernel):
    row_count = padded.shape[-3] - 2
    col_count = padded.shape[-2] - 2
    total = jnp.zeros(padded.shape[:-3] + (row_count, col_count, padded.shape[-1]), jnp.float32)
    for tap_index in range(9):
        row_shift = tap_index // 3 - 1
        col_shift = tap_index % 3 - 1
        total = (
            total
            + kernel[tap_index]
            * padded[
                ...,
                1 + row_shift : 1 + row_shift + row_count,
                1 + col_shift : 1 + col_shift + col_count,
                :,
            ]
        )
    return total


def depthwise_adjoint(padded, kernel):
    row_count = padded.shape[-3] - 2
    col_count = padded.shape[-2] - 2
    total = jnp.zeros(padded.shape[:-3] + (row_count, col_count, padded.shape[-1]), jnp.float32)
    for tap_index in range(9):
        row_shift = tap_index // 3 - 1
        col_shift = tap_index % 3 - 1
        total = (
            total
            + kernel[tap_index]
            * padded[
                ...,
                1 - row_shift : 1 - row_shift + row_count,
                1 - col_shift : 1 - col_shift + col_count,
                :,
            ]
        )
    return total


def kernel_terms(padded, grad_depth):
    row_count = grad_depth.shape[-3]
    col_count = grad_depth.shape[-2]
    axes = tuple(range(grad_depth.ndim - 1))
    pieces = []
    for tap_index in range(9):
        row_shift = tap_index // 3 - 1
        col_shift = tap_index % 3 - 1
        window = padded[
            ...,
            1 + row_shift : 1 + row_shift + row_count,
            1 + col_shift : 1 + col_shift + col_count,
            :,
        ]
        pieces.append(jnp.sum(window * grad_depth, axis=axes))
    return jnp.stack(pieces, axis=0)


def head_grads(level_one, level_two, lat_one, lat_two, classifier, labels, npix):
    lateral = project(level_one.astype(jnp.bfloat16), lat_one) + upsample(
        project(level_two.astype(jnp.bfloat16), lat_two)
    )
    active, slope = gelu_pair(lateral)
    hidden = active.astype(jnp.bfloat16)
    logits = project(hidden, classifier)
    probs = jax.nn.softmax(logits, axis=-1)
    onehot = (labels[..., None] == jnp.arange(classifier.shape[1], dtype=jnp.int32)).astype(
        jnp.float32
    )
    grad_logits = (probs - onehot) * (loss_scale / npix)
    grad_lat = project_back(grad_logits.astype(jnp.bfloat16), classifier) * slope
    cot_one = project_back(grad_lat.astype(jnp.bfloat16), lat_one)
    cot_two = project_back(pool_sum(grad_lat).astype(jnp.bfloat16), lat_two)
    return (cot_one, cot_two)


def widen(values):
    return jnp.pad(values, ((0, 0), (1, 1), (0, 0)))


def pick(buffer, slot_index):
    return lax.dynamic_index_in_dim(buffer, slot_index, 0, keepdims=False)


def place(buffer, slot_index, values, active):
    previous = pick(buffer, slot_index)
    return lax.dynamic_update_index_in_dim(
        buffer, jnp.where(active, values, previous), slot_index, 0
    )


def shards(
    stem,
    labels,
    up_proj,
    mix_proj,
    down_proj,
    dw_kernel,
    gain1,
    gain2,
    lat_one,
    lat_two,
    classifier,
):
    batches, row_count, col_count, chan_one = stem.shape
    chan_two = up_proj.shape[1]
    sections = lax.axis_size("col")
    section_index = lax.axis_index("col")
    tick_count = batches + sections - 1
    proj_up = up_proj[0]
    proj_mix = mix_proj[0]
    proj_down = down_proj[0]
    kernel = dw_kernel[0].astype(jnp.float32)
    decay1 = gain1[0]
    decay2 = gain2[0]
    is_first = section_index == 0
    is_final = section_index == sections - 1
    zeros_one = jnp.zeros((row_count, col_count, chan_one), jnp.float32)
    zeros_two = jnp.zeros((row_count // 2, col_count // 2, chan_two), jnp.float32)
    buffer_one = jnp.zeros((batches,) + zeros_one.shape, jnp.float32)
    buffer_two = jnp.zeros((batches,) + zeros_two.shape, jnp.float32)

    def front(lower_two, slot_index):
        stem_piece = pick(stem, slot_index).astype(jnp.float32)
        narrow = lower_two.astype(jnp.bfloat16)
        return (narrow, stem_piece + upsample(project(narrow, proj_up)))

    def middle(padded):
        depth = depthwise_apply(padded, kernel)
        active, slope_one = gelu_pair(depth)
        hidden = active.astype(jnp.bfloat16)
        return (hidden, slope_one, project(hidden, proj_mix))

    def upper(level_one):
        pooled = (pool_sum(level_one) * 0.25).astype(jnp.bfloat16)
        lifted, slope_two = gelu_pair(project(pooled, proj_down))
        return (pooled, lifted, slope_two)

    def forward_tick(step_count, state_tuple):
        inbox1, inbox2, saved1, saved2, stored1, stored2 = state_tuple
        micro = step_count - section_index
        active = (micro >= 0) & (micro < batches)
        slot_index = jnp.clip(micro, 0, batches - 1)
        narrow, mixture = front(inbox2, slot_index)
        bordered = extended(mixture, (("strip", 0),), 1)
        hidden, slope_one, branch = middle(widen(bordered))
        state1 = decay1 * inbox1 + branch
        pooled, lifted, slope_two = upper(state1)
        state2 = decay2 * inbox2 + lifted
        saved1 = place(saved1, slot_index, state1, active)
        saved2 = place(saved2, slot_index, state2, active)
        inbox1, inbox2 = passed_along((state1, state2), "col", 1)
        return (inbox1, inbox2, saved1, saved2, stored1, stored2)

    outcome = lax.fori_loop(
        0,
        tick_count,
        forward_tick,
        (zeros_one, zeros_two, buffer_one, buffer_two, buffer_one, buffer_two),
    )
    saved1, saved2, stored1, stored2 = (outcome[2], outcome[3], outcome[4], outcome[5])
    npix = float(batches * lax.axis_size("dp") * row_count * lax.axis_size("strip") * col_count)
    head_one, head_two = head_grads(saved1, saved2, lat_one, lat_two, classifier, labels, npix)

    def backward_tick(step_count, state_tuple):
        message, acc_up, acc_mix, acc_down, acc_kernel, acc_stem = state_tuple
        micro = step_count - (sections - 1 - section_index)
        active = (micro >= 0) & (micro < batches)
        slot_index = jnp.clip(micro, 0, batches - 1)
        from_head1 = pick(head_one, slot_index)
        from_head2 = pick(head_two, slot_index)
        own1 = pick(saved1, slot_index)
        own2 = pick(saved2, slot_index)
        upper1 = jnp.where(is_final, own1, message[0])
        cot1 = jnp.where(is_final, from_head1, message[1])
        cot2 = jnp.where(is_final, from_head2, message[2])
        own_pooled, own_lifted, own_slope = upper(own1)
        lower2 = jnp.where(is_first, 0.0, (own2 - own_lifted) / decay2)
        pooled, lifted, slope_two = upper(upper1)
        narrow, mixture = front(lower2, slot_index)
        bordered = extended(mixture, (("strip", 0),), 1)
        padded = widen(bordered)
        hidden, slope_one, branch = middle(padded)
        lower1 = jnp.where(is_first, 0.0, (own1 - branch) / decay1)
        cot1 = jnp.where(active, cot1, 0.0)
        cot2 = jnp.where(active, cot2, 0.0)
        grad_lift = (cot2 * slope_two).astype(jnp.bfloat16)
        acc_down = acc_down + outer_sum(pooled, grad_lift)
        total_one = cot1 + upsample(project_back(grad_lift, proj_down)) * 0.25
        total_narrow = total_one.astype(jnp.bfloat16)
        acc_mix = acc_mix + outer_sum(hidden, total_narrow)
        grad_depth = project_back(total_narrow, proj_mix) * slope_one
        grad_border = extended(grad_depth, (("strip", 0),), 1)
        grad_mixture = depthwise_adjoint(widen(grad_border), kernel)
        acc_kernel = acc_kernel + kernel_terms(padded, grad_depth)
        acc_stem = lax.dynamic_update_index_in_dim(
            acc_stem, pick(acc_stem, slot_index) + grad_mixture, slot_index, 0
        )
        grad_narrow = pool_sum(grad_mixture).astype(jnp.bfloat16)
        acc_up = acc_up + outer_sum(narrow, grad_narrow)
        send_two = decay2 * cot2 + project_back(grad_narrow, proj_up)
        send_one = decay1 * total_one
        message = passed_along((lower1, send_one, send_two), "col", -1)
        return (message, acc_up, acc_mix, acc_down, acc_kernel, acc_stem)

    start_message = (zeros_one, zeros_one, zeros_two)
    start = (
        start_message,
        jnp.zeros((chan_two, chan_one), jnp.float32),
        jnp.zeros((chan_one, chan_one), jnp.float32),
        jnp.zeros((chan_one, chan_two), jnp.float32),
        jnp.zeros((9, chan_one), jnp.float32),
        buffer_one,
    )
    result = lax.fori_loop(0, tick_count, backward_tick, start)
    grad_up, grad_mix, grad_down, grad_kernel = (
        lax.psum_scatter(result[1], ("dp", "strip"), scatter_dimension=0, tiled=True),
        lax.psum_scatter(result[2], ("dp", "strip"), scatter_dimension=0, tiled=True),
        lax.psum_scatter(result[3], ("dp", "strip"), scatter_dimension=0, tiled=True),
        lax.psum_scatter(result[4], ("dp", "strip"), scatter_dimension=1, tiled=True),
    )
    grad_stem = lax.psum_scatter(result[5], "col", scatter_dimension=2, tiled=True)
    return (grad_up[None], grad_mix[None], grad_down[None], grad_kernel[None], grad_stem)


def solution(mesh):
    placed = (
        P("dp", "strip", None, None),
        P("dp", "strip", None),
        P("col", None, None),
        P("col", None, None),
        P("col", None, None),
        P("col", None, None),
        P("col", None),
        P("col", None),
        P(),
        P(),
        P(),
    )
    return jax.shard_map(
        shards,
        mesh=mesh,
        in_specs=placed,
        out_specs=(
            P("col", ("dp", "strip"), None),
            P("col", ("dp", "strip"), None),
            P("col", ("dp", "strip"), None),
            P("col", None, ("dp", "strip")),
            P("dp", "strip", "col", None),
        ),
        check_vma=False,
    )
```

profile of v0, /device:TPU:25, one launch (start us, length us, event | category | flops | bytes accessed | tf_op | source)
XLA Modules:
  0.0 1702.2 jit_solution(4548003098856464248)
XLA Ops:
  9.4 454.9 %while.51 = (s32[]{:T(128)}, f32[2,32,360]{2,1,0:T(8,128)}, f32[1,16,720]{2,1,0:T(8,128)S(1)}, f32[4,2,32,360]{3,2,1,0:T(8,128)S(1)}, f32[4,1,16,720]{3,2,1,0:T(...) while((s32[]{:T(128)}, f32[2,32,360]{2,1,0:T(8,128)}, ...), condition=%wide.region_3.4_spmd, body=%wide.region_0.3_spmd.sunk | while | flops 34496644 | bytes 7706652 | solution.py:228
  12.8 5.5 collective-permute-start.1
  38.2 5.5 collective-permute-start.1
  62.0 5.5 collective-permute-start.1
  85.8 5.5 collective-permute-start.1
  109.5 5.5 collective-permute-start.1
  133.3 5.5 collective-permute-start.1
  157.1 5.5 collective-permute-start.1
  180.9 5.5 collective-permute-start.1
  204.6 5.5 collective-permute-start.1
  228.7 5.5 collective-permute-start.1
  252.5 5.5 collective-permute-start.1
  276.2 5.5 collective-permute-start.1
  300.0 5.5 collective-permute-start.1
  323.8 5.5 collective-permute-start.1
  347.6 5.5 collective-permute-start.1
  372.4 5.5 collective-permute-start.1
  396.5 5.5 collective-permute-start.1
  420.2 5.5 collective-permute-start.1
  444.0 5.5 collective-permute-start.1
  474.6 989.0 %while.52 = (s32[]{:T(128)}, f32[2,32,360]{2,1,0:T(8,128)}, f32[2,32,360]{2,1,0:T(8,128)}, f32[1,16,720]{2,1,0:T(8,128)}, f32[720,360]{1,0:T(8,128)S(1)}, /*inde...) while((s32[]{:T(128)}, f32[2,32,360]{2,1,0:T(8,128)}, ...), condition=%wide.region_24.25_spmd.clone, body=%wide.region_8.24_spmd.clone.sunk | while | flops 113066288 | bytes 23087148 | solution.py:288
  480.1 6.7 collective-permute-start.5
  508.1 5.5 collective-permute-start.9
  530.9 6.7 collective-permute-start.5
  560.2 5.5 collective-permute-start.9
  585.4 6.7 collective-permute-start.5
  613.4 5.5 collective-permute-start.9
  639.7 6.7 collective-permute-start.5
  667.7 5.5 collective-permute-start.9
  691.5 6.7 collective-permute-start.5
  719.6 5.5 collective-permute-start.9
  743.5 6.7 collective-permute-start.5
  771.4 5.5 collective-permute-start.9
  795.3 6.7 collective-permute-start.5
  823.2 5.5 collective-permute-start.9
  847.1 6.7 collective-permute-start.5
  875.0 5.5 collective-permute-start.9
  898.8 6.7 collective-permute-start.5
  926.8 5.5 collective-permute-start.9
  950.6 6.7 collective-permute-start.5
  978.5 5.5 collective-permute-start.9
  1002.3 6.7 collective-permute-start.5
  1030.3 5.5 collective-permute-start.9
  1054.1 6.7 collective-permute-start.5
  1082.9 5.5 collective-permute-start.9
  1106.7 6.7 collective-permute-start.5
  1134.7 5.5 collective-permute-start.9
  1158.5 6.7 collective-permute-start.5
  1186.4 5.5 collective-permute-start.9
  1210.2 6.7 collective-permute-start.5
  1238.2 5.5 collective-permute-start.9
  1262.0 6.7 collective-permute-start.5
  1289.9 5.5 collective-permute-start.9
  1313.8 6.7 collective-permute-start.5
  1341.7 5.5 collective-permute-start.9
  1365.6 6.7 collective-permute-start.5
  1393.5 5.5 collective-permute-start.9
  1417.3 6.7 collective-permute-start.5
  1445.3 5.5 collective-permute-start.9
  1463.6 132.4 %fusion.162 = (f32[96,360]{1,0:T(8,128)S(1)}, f32[48,360]{1,0:T(8,128)S(1)}, f32[48,720]{1,0:T(8,128)S(1)}) fusion(f32[720,360]{1,0:T(8,128)S(1)} %get-tuple-element.1663, f32[360,360]{1,0:T(8,128)} %get-tuple-element.1664, f32[360,720]{1,0:T(8,128)} %get-tuple-element.1665), kind=kCustom, calls=%all-reduce-scatter.3 | all-reduce-scatter fusion | flops 691202 | bytes 2938112
  1596.1 5.9 collective-permute-start.13
  1602.1 4.3 collective-permute-start.12
  1610.3 28.7 %all-reduce.6 = f32[9,360]{1,0:T(8,128)S(1)} all-reduce(f32[9,360]{1,0:T(8,128)S(1)} %copy-done.17), channel_id=5, replica_groups=mesh['col'=16,'dp'=4,'strip'=2] {'dp','strip'}, use_global_device_ids=true, to_apply=%region_28.29.clone | all-reduce | flops 3240 | bytes 25920
  1646.6 47.4 %all-reduce.14.cloned.1.call-done = f32[4,2,32,360]{3,0,1,2:T(4,128)} async-done(((f32[4,2,32,360]{3,0,1,2:T(4,128)}), f32[4,2,32,360]{3,0,1,2:T(4,128)}) %all-reduce.14.cloned.1.call-update) | async-done | bytes 368656
  (2314 shorter events, 1119.2 us)
Async XLA Ops:
  7.2 1686.8 %all-reduce.14.cloned.1.call-start = ((), (), s32[]{:S(2)}) async-start(), calls=%async_computation | async-start | bytes 786432
  478.8 23.3 %collective-permute-start.4 = (f32[1,32,360]{2,1,0:T(8,128)}, f32[1,32,360]{2,1,0:T(8,128)}, u32[]{:S(2)}, u32[]{:S(2)}) collective-permute-start(f32[1,32,360]{2,1,0:T(8,128)} %get-tuple-element.1468), channel_id=1, source_target_pairs={{1,0},{3,2},{5,4},{7,6},{9,8},{11,10},{13,12},{15,14},{17,16},{19,... | collective-permute-start | bytes 138248 | tf_op jit(solution)/shard_map/while/body/eval_jaxpr/ppermute | solution.py:19
  480.1 22.0 %collective-permute-start.5 = (f32[1,32,360]{2,1,0:T(8,128)}, f32[1,32,360]{2,1,0:T(8,128)}, u32[]{:S(2)}, u32[]{:S(2)}) collective-permute-start(f32[1,32,360]{2,1,0:T(8,128)} %get-tuple-element.1469), channel_id=1, source_target_pairs={{0,1},{2,3},{4,5},{6,7},{8,9},{10,11},{12,13},{14,15},{16,17},{18,... | collective-permute-start | bytes 138248 | tf_op jit(solution)/shard_map/while/body/eval_jaxpr/ppermute | solution.py:16
  493.3 31.5 %collective-permute-start.7 = (f32[2,32,360]{2,1,0:T(8,128)}, f32[2,32,360]{2,1,0:T(8,128)}, u32[]{:S(2)}, u32[]{:S(2)}) collective-permute-start(f32[2,32,360]{2,1,0:T(8,128)} %get-tuple-element.1479), channel_id=1, source_target_pairs={{8,0},{16,8},{24,16},{32,24},{40,32},{48,40},{56,48},{64,56},{72,6... | collective-permute-start | bytes 276488 | tf_op jit(solution)/shard_map/while/body/eval_jaxpr/ppermute | solution.py:27
  529.6 24.6 %collective-permute-start.4 = (f32[1,32,360]{2,1,0:T(8,128)}, f32[1,32,360]{2,1,0:T(8,128)}, u32[]{:S(2)}, u32[]{:S(2)}) collective-permute-start(f32[1,32,360]{2,1,0:T(8,128)} %get-tuple-element.1468), channel_id=1, source_target_pairs={{1,0},{3,2},{5,4},{7,6},{9,8},{11,10},{13,12},{15,14},{17,16},{19,... | collective-permute-start | bytes 138248 | tf_op jit(solution)/shard_map/while/body/eval_jaxpr/ppermute | solution.py:19
  530.9 23.4 %collective-permute-start.5 = (f32[1,32,360]{2,1,0:T(8,128)}, f32[1,32,360]{2,1,0:T(8,128)}, u32[]{:S(2)}, u32[]{:S(2)}) collective-permute-start(f32[1,32,360]{2,1,0:T(8,128)} %get-tuple-element.1469), channel_id=1, source_target_pairs={{0,1},{2,3},{4,5},{6,7},{8,9},{10,11},{12,13},{14,15},{16,17},{18,... | collective-permute-start | bytes 138248 | tf_op jit(solution)/shard_map/while/body/eval_jaxpr/ppermute | solution.py:16
  544.1 35.3 %collective-permute-start.7 = (f32[2,32,360]{2,1,0:T(8,128)}, f32[2,32,360]{2,1,0:T(8,128)}, u32[]{:S(2)}, u32[]{:S(2)}) collective-permute-start(f32[2,32,360]{2,1,0:T(8,128)} %get-tuple-element.1479), channel_id=1, source_target_pairs={{8,0},{16,8},{24,16},{32,24},{40,32},{48,40},{56,48},{64,56},{72,6... | collective-permute-start | bytes 276488 | tf_op jit(solution)/shard_map/while/body/eval_jaxpr/ppermute | solution.py:27
  558.9 12.4 collective-permute-start.8
  584.2 23.3 %collective-permute-start.4 = (f32[1,32,360]{2,1,0:T(8,128)}, f32[1,32,360]{2,1,0:T(8,128)}, u32[]{:S(2)}, u32[]{:S(2)}) collective-permute-start(f32[1,32,360]{2,1,0:T(8,128)} %get-tuple-element.1468), channel_id=1, source_target_pairs={{1,0},{3,2},{5,4},{7,6},{9,8},{11,10},{13,12},{15,14},{17,16},{19,... | collective-permute-start | bytes 138248 | tf_op jit(solution)/shard_map/while/body/eval_jaxpr/ppermute | solution.py:19
  585.4 22.0 %collective-permute-start.5 = (f32[1,32,360]{2,1,0:T(8,128)}, f32[1,32,360]{2,1,0:T(8,128)}, u32[]{:S(2)}, u32[]{:S(2)}) collective-permute-start(f32[1,32,360]{2,1,0:T(8,128)} %get-tuple-element.1469), channel_id=1, source_target_pairs={{0,1},{2,3},{4,5},{6,7},{8,9},{10,11},{12,13},{14,15},{16,17},{18,... | collective-permute-start | bytes 138248 | tf_op jit(solution)/shard_map/while/body/eval_jaxpr/ppermute | solution.py:16
  598.6 35.0 %collective-permute-start.7 = (f32[2,32,360]{2,1,0:T(8,128)}, f32[2,32,360]{2,1,0:T(8,128)}, u32[]{:S(2)}, u32[]{:S(2)}) collective-permute-start(f32[2,32,360]{2,1,0:T(8,128)} %get-tuple-element.1479), channel_id=1, source_target_pairs={{8,0},{16,8},{24,16},{32,24},{40,32},{48,40},{56,48},{64,56},{72,6... | collective-permute-start | bytes 276488 | tf_op jit(solution)/shard_map/while/body/eval_jaxpr/ppermute | solution.py:27
  612.1 12.1 collective-permute-start.8
  621.0 12.5 collective-permute-start.6
  638.4 23.3 %collective-permute-start.4 = (f32[1,32,360]{2,1,0:T(8,128)}, f32[1,32,360]{2,1,0:T(8,128)}, u32[]{:S(2)}, u32[]{:S(2)}) collective-permute-start(f32[1,32,360]{2,1,0:T(8,128)} %get-tuple-element.1468), channel_id=1, source_target_pairs={{1,0},{3,2},{5,4},{7,6},{9,8},{11,10},{13,12},{15,14},{17,16},{19,... | collective-permute-start | bytes 138248 | tf_op jit(solution)/shard_map/while/body/eval_jaxpr/ppermute | solution.py:19
  639.7 22.0 %collective-permute-start.5 = (f32[1,32,360]{2,1,0:T(8,128)}, f32[1,32,360]{2,1,0:T(8,128)}, u32[]{:S(2)}, u32[]{:S(2)}) collective-permute-start(f32[1,32,360]{2,1,0:T(8,128)} %get-tuple-element.1469), channel_id=1, source_target_pairs={{0,1},{2,3},{4,5},{6,7},{8,9},{10,11},{12,13},{14,15},{16,17},{18,... | collective-permute-start | bytes 138248 | tf_op jit(solution)/shard_map/while/body/eval_jaxpr/ppermute | solution.py:16
  652.9 32.4 %collective-permute-start.7 = (f32[2,32,360]{2,1,0:T(8,128)}, f32[2,32,360]{2,1,0:T(8,128)}, u32[]{:S(2)}, u32[]{:S(2)}) collective-permute-start(f32[2,32,360]{2,1,0:T(8,128)} %get-tuple-element.1479), channel_id=1, source_target_pairs={{8,0},{16,8},{24,16},{32,24},{40,32},{48,40},{56,48},{64,56},{72,6... | collective-permute-start | bytes 276488 | tf_op jit(solution)/shard_map/while/body/eval_jaxpr/ppermute | solution.py:27
  690.2 23.5 %collective-permute-start.4 = (f32[1,32,360]{2,1,0:T(8,128)}, f32[1,32,360]{2,1,0:T(8,128)}, u32[]{:S(2)}, u32[]{:S(2)}) collective-permute-start(f32[1,32,360]{2,1,0:T(8,128)} %get-tuple-element.1468), channel_id=1, source_target_pairs={{1,0},{3,2},{5,4},{7,6},{9,8},{11,10},{13,12},{15,14},{17,16},{19,... | collective-permute-start | bytes 138248 | tf_op jit(solution)/shard_map/while/body/eval_jaxpr/ppermute | solution.py:19
  691.5 22.2 %collective-permute-start.5 = (f32[1,32,360]{2,1,0:T(8,128)}, f32[1,32,360]{2,1,0:T(8,128)}, u32[]{:S(2)}, u32[]{:S(2)}) collective-permute-start(f32[1,32,360]{2,1,0:T(8,128)} %get-tuple-element.1469), channel_id=1, source_target_pairs={{0,1},{2,3},{4,5},{6,7},{8,9},{10,11},{12,13},{14,15},{16,17},{18,... | collective-permute-start | bytes 138248 | tf_op jit(solution)/shard_map/while/body/eval_jaxpr/ppermute | solution.py:16
  704.7 32.6 %collective-permute-start.7 = (f32[2,32,360]{2,1,0:T(8,128)}, f32[2,32,360]{2,1,0:T(8,128)}, u32[]{:S(2)}, u32[]{:S(2)}) collective-permute-start(f32[2,32,360]{2,1,0:T(8,128)} %get-tuple-element.1479), channel_id=1, source_target_pairs={{8,0},{16,8},{24,16},{32,24},{40,32},{48,40},{56,48},{64,56},{72,6... | collective-permute-start | bytes 276488 | tf_op jit(solution)/shard_map/while/body/eval_jaxpr/ppermute | solution.py:27
  742.2 23.3 %collective-permute-start.4 = (f32[1,32,360]{2,1,0:T(8,128)}, f32[1,32,360]{2,1,0:T(8,128)}, u32[]{:S(2)}, u32[]{:S(2)}) collective-permute-start(f32[1,32,360]{2,1,0:T(8,128)} %get-tuple-element.1468), channel_id=1, source_target_pairs={{1,0},{3,2},{5,4},{7,6},{9,8},{11,10},{13,12},{15,14},{17,16},{19,... | collective-permute-start | bytes 138248 | tf_op jit(solution)/shard_map/while/body/eval_jaxpr/ppermute | solution.py:19
  743.5 22.0 %collective-permute-start.5 = (f32[1,32,360]{2,1,0:T(8,128)}, f32[1,32,360]{2,1,0:T(8,128)}, u32[]{:S(2)}, u32[]{:S(2)}) collective-permute-start(f32[1,32,360]{2,1,0:T(8,128)} %get-tuple-element.1469), channel_id=1, source_target_pairs={{0,1},{2,3},{4,5},{6,7},{8,9},{10,11},{12,13},{14,15},{16,17},{18,... | collective-permute-start | bytes 138248 | tf_op jit(solution)/shard_map/while/body/eval_jaxpr/ppermute | solution.py:16
  756.7 32.5 %collective-permute-start.7 = (f32[2,32,360]{2,1,0:T(8,128)}, f32[2,32,360]{2,1,0:T(8,128)}, u32[]{:S(2)}, u32[]{:S(2)}) collective-permute-start(f32[2,32,360]{2,1,0:T(8,128)} %get-tuple-element.1479), channel_id=1, source_target_pairs={{8,0},{16,8},{24,16},{32,24},{40,32},{48,40},{56,48},{64,56},{72,6... | collective-permute-start | bytes 276488 | tf_op jit(solution)/shard_map/while/body/eval_jaxpr/ppermute | solution.py:27
  794.0 23.3 %collective-permute-start.4 = (f32[1,32,360]{2,1,0:T(8,128)}, f32[1,32,360]{2,1,0:T(8,128)}, u32[]{:S(2)}, u32[]{:S(2)}) collective-permute-start(f32[1,32,360]{2,1,0:T(8,128)} %get-tuple-element.1468), channel_id=1, source_target_pairs={{1,0},{3,2},{5,4},{7,6},{9,8},{11,10},{13,12},{15,14},{17,16},{19,... | collective-permute-start | bytes 138248 | tf_op jit(solution)/shard_map/while/body/eval_jaxpr/ppermute | solution.py:19
  795.3 22.0 %collective-permute-start.5 = (f32[1,32,360]{2,1,0:T(8,128)}, f32[1,32,360]{2,1,0:T(8,128)}, u32[]{:S(2)}, u32[]{:S(2)}) collective-permute-start(f32[1,32,360]{2,1,0:T(8,128)} %get-tuple-element.1469), channel_id=1, source_target_pairs={{0,1},{2,3},{4,5},{6,7},{8,9},{10,11},{12,13},{14,15},{16,17},{18,... | collective-permute-start | bytes 138248 | tf_op jit(solution)/shard_map/while/body/eval_jaxpr/ppermute | solution.py:16
  808.5 32.5 %collective-permute-start.7 = (f32[2,32,360]{2,1,0:T(8,128)}, f32[2,32,360]{2,1,0:T(8,128)}, u32[]{:S(2)}, u32[]{:S(2)}) collective-permute-start(f32[2,32,360]{2,1,0:T(8,128)} %get-tuple-element.1479), channel_id=1, source_target_pairs={{8,0},{16,8},{24,16},{32,24},{40,32},{48,40},{56,48},{64,56},{72,6... | collective-permute-start | bytes 276488 | tf_op jit(solution)/shard_map/while/body/eval_jaxpr/ppermute | solution.py:27
  845.8 23.3 %collective-permute-start.4 = (f32[1,32,360]{2,1,0:T(8,128)}, f32[1,32,360]{2,1,0:T(8,128)}, u32[]{:S(2)}, u32[]{:S(2)}) collective-permute-start(f32[1,32,360]{2,1,0:T(8,128)} %get-tuple-element.1468), channel_id=1, source_target_pairs={{1,0},{3,2},{5,4},{7,6},{9,8},{11,10},{13,12},{15,14},{17,16},{19,... | collective-permute-start | bytes 138248 | tf_op jit(solution)/shard_map/while/body/eval_jaxpr/ppermute | solution.py:19
  847.1 22.0 %collective-permute-start.5 = (f32[1,32,360]{2,1,0:T(8,128)}, f32[1,32,360]{2,1,0:T(8,128)}, u32[]{:S(2)}, u32[]{:S(2)}) collective-permute-start(f32[1,32,360]{2,1,0:T(8,128)} %get-tuple-element.1469), channel_id=1, source_target_pairs={{0,1},{2,3},{4,5},{6,7},{8,9},{10,11},{12,13},{14,15},{16,17},{18,... | collective-permute-start | bytes 138248 | tf_op jit(solution)/shard_map/while/body/eval_jaxpr/ppermute | solution.py:16
  860.2 32.4 %collective-permute-start.7 = (f32[2,32,360]{2,1,0:T(8,128)}, f32[2,32,360]{2,1,0:T(8,128)}, u32[]{:S(2)}, u32[]{:S(2)}) collective-permute-start(f32[2,32,360]{2,1,0:T(8,128)} %get-tuple-element.1479), channel_id=1, source_target_pairs={{8,0},{16,8},{24,16},{32,24},{40,32},{48,40},{56,48},{64,56},{72,6... | collective-permute-start | bytes 276488 | tf_op jit(solution)/shard_map/while/body/eval_jaxpr/ppermute | solution.py:27
  897.5 23.3 %collective-permute-start.4 = (f32[1,32,360]{2,1,0:T(8,128)}, f32[1,32,360]{2,1,0:T(8,128)}, u32[]{:S(2)}, u32[]{:S(2)}) collective-permute-start(f32[1,32,360]{2,1,0:T(8,128)} %get-tuple-element.1468), channel_id=1, source_target_pairs={{1,0},{3,2},{5,4},{7,6},{9,8},{11,10},{13,12},{15,14},{17,16},{19,... | collective-permute-start | bytes 138248 | tf_op jit(solution)/shard_map/while/body/eval_jaxpr/ppermute | solution.py:19
  898.8 22.0 %collective-permute-start.5 = (f32[1,32,360]{2,1,0:T(8,128)}, f32[1,32,360]{2,1,0:T(8,128)}, u32[]{:S(2)}, u32[]{:S(2)}) collective-permute-start(f32[1,32,360]{2,1,0:T(8,128)} %get-tuple-element.1469), channel_id=1, source_target_pairs={{0,1},{2,3},{4,5},{6,7},{8,9},{10,11},{12,13},{14,15},{16,17},{18,... | collective-permute-start | bytes 138248 | tf_op jit(solution)/shard_map/while/body/eval_jaxpr/ppermute | solution.py:16
  912.0 32.4 %collective-permute-start.7 = (f32[2,32,360]{2,1,0:T(8,128)}, f32[2,32,360]{2,1,0:T(8,128)}, u32[]{:S(2)}, u32[]{:S(2)}) collective-permute-start(f32[2,32,360]{2,1,0:T(8,128)} %get-tuple-element.1479), channel_id=1, source_target_pairs={{8,0},{16,8},{24,16},{32,24},{40,32},{48,40},{56,48},{64,56},{72,6... | collective-permute-start | bytes 276488 | tf_op jit(solution)/shard_map/while/body/eval_jaxpr/ppermute | solution.py:27
  949.3 23.3 %collective-permute-start.4 = (f32[1,32,360]{2,1,0:T(8,128)}, f32[1,32,360]{2,1,0:T(8,128)}, u32[]{:S(2)}, u32[]{:S(2)}) collective-permute-start(f32[1,32,360]{2,1,0:T(8,128)} %get-tuple-element.1468), channel_id=1, source_target_pairs={{1,0},{3,2},{5,4},{7,6},{9,8},{11,10},{13,12},{15,14},{17,16},{19,... | collective-permute-start | bytes 138248 | tf_op jit(solution)/shard_map/while/body/eval_jaxpr/ppermute | solution.py:19
  950.6 22.0 %collective-permute-start.5 = (f32[1,32,360]{2,1,0:T(8,128)}, f32[1,32,360]{2,1,0:T(8,128)}, u32[]{:S(2)}, u32[]{:S(2)}) collective-permute-start(f32[1,32,360]{2,1,0:T(8,128)} %get-tuple-element.1469), channel_id=1, source_target_pairs={{0,1},{2,3},{4,5},{6,7},{8,9},{10,11},{12,13},{14,15},{16,17},{18,... | collective-permute-start | bytes 138248 | tf_op jit(solution)/shard_map/while/body/eval_jaxpr/ppermute | solution.py:16
  963.8 32.4 %collective-permute-start.7 = (f32[2,32,360]{2,1,0:T(8,128)}, f32[2,32,360]{2,1,0:T(8,128)}, u32[]{:S(2)}, u32[]{:S(2)}) collective-permute-start(f32[2,32,360]{2,1,0:T(8,128)} %get-tuple-element.1479), channel_id=1, source_target_pairs={{8,0},{16,8},{24,16},{32,24},{40,32},{48,40},{56,48},{64,56},{72,6... | collective-permute-start | bytes 276488 | tf_op jit(solution)/shard_map/while/body/eval_jaxpr/ppermute | solution.py:27
  1001.1 23.3 %collective-permute-start.4 = (f32[1,32,360]{2,1,0:T(8,128)}, f32[1,32,360]{2,1,0:T(8,128)}, u32[]{:S(2)}, u32[]{:S(2)}) collective-permute-start(f32[1,32,360]{2,1,0:T(8,128)} %get-tuple-element.1468), channel_id=1, source_target_pairs={{1,0},{3,2},{5,4},{7,6},{9,8},{11,10},{13,12},{15,14},{17,16},{19,... | collective-permute-start | bytes 138248 | tf_op jit(solution)/shard_map/while/body/eval_jaxpr/ppermute | solution.py:19
  1002.3 22.0 %collective-permute-start.5 = (f32[1,32,360]{2,1,0:T(8,128)}, f32[1,32,360]{2,1,0:T(8,128)}, u32[]{:S(2)}, u32[]{:S(2)}) collective-permute-start(f32[1,32,360]{2,1,0:T(8,128)} %get-tuple-element.1469), channel_id=1, source_target_pairs={{0,1},{2,3},{4,5},{6,7},{8,9},{10,11},{12,13},{14,15},{16,17},{18,... | collective-permute-start | bytes 138248 | tf_op jit(solution)/shard_map/while/body/eval_jaxpr/ppermute | solution.py:16
  1015.5 32.4 %collective-permute-start.7 = (f32[2,32,360]{2,1,0:T(8,128)}, f32[2,32,360]{2,1,0:T(8,128)}, u32[]{:S(2)}, u32[]{:S(2)}) collective-permute-start(f32[2,32,360]{2,1,0:T(8,128)} %get-tuple-element.1479), channel_id=1, source_target_pairs={{8,0},{16,8},{24,16},{32,24},{40,32},{48,40},{56,48},{64,56},{72,6... | collective-permute-start | bytes 276488 | tf_op jit(solution)/shard_map/while/body/eval_jaxpr/ppermute | solution.py:27
  1052.8 24.1 %collective-permute-start.4 = (f32[1,32,360]{2,1,0:T(8,128)}, f32[1,32,360]{2,1,0:T(8,128)}, u32[]{:S(2)}, u32[]{:S(2)}) collective-permute-start(f32[1,32,360]{2,1,0:T(8,128)} %get-tuple-element.1468), channel_id=1, source_target_pairs={{1,0},{3,2},{5,4},{7,6},{9,8},{11,10},{13,12},{15,14},{17,16},{19,... | collective-permute-start | bytes 138248 | tf_op jit(solution)/shard_map/while/body/eval_jaxpr/ppermute | solution.py:19
  1054.1 22.8 %collective-permute-start.5 = (f32[1,32,360]{2,1,0:T(8,128)}, f32[1,32,360]{2,1,0:T(8,128)}, u32[]{:S(2)}, u32[]{:S(2)}) collective-permute-start(f32[1,32,360]{2,1,0:T(8,128)} %get-tuple-element.1469), channel_id=1, source_target_pairs={{0,1},{2,3},{4,5},{6,7},{8,9},{10,11},{12,13},{14,15},{16,17},{18,... | collective-permute-start | bytes 138248 | tf_op jit(solution)/shard_map/while/body/eval_jaxpr/ppermute | solution.py:16
  1067.3 33.3 %collective-permute-start.7 = (f32[2,32,360]{2,1,0:T(8,128)}, f32[2,32,360]{2,1,0:T(8,128)}, u32[]{:S(2)}, u32[]{:S(2)}) collective-permute-start(f32[2,32,360]{2,1,0:T(8,128)} %get-tuple-element.1479), channel_id=1, source_target_pairs={{8,0},{16,8},{24,16},{32,24},{40,32},{48,40},{56,48},{64,56},{72,6... | collective-permute-start | bytes 276488 | tf_op jit(solution)/shard_map/while/body/eval_jaxpr/ppermute | solution.py:27
  1105.4 23.3 %collective-permute-start.4 = (f32[1,32,360]{2,1,0:T(8,128)}, f32[1,32,360]{2,1,0:T(8,128)}, u32[]{:S(2)}, u32[]{:S(2)}) collective-permute-start(f32[1,32,360]{2,1,0:T(8,128)} %get-tuple-element.1468), channel_id=1, source_target_pairs={{1,0},{3,2},{5,4},{7,6},{9,8},{11,10},{13,12},{15,14},{17,16},{19,... | collective-permute-start | bytes 138248 | tf_op jit(solution)/shard_map/while/body/eval_jaxpr/ppermute | solution.py:19
  1106.7 22.0 %collective-permute-start.5 = (f32[1,32,360]{2,1,0:T(8,128)}, f32[1,32,360]{2,1,0:T(8,128)}, u32[]{:S(2)}, u32[]{:S(2)}) collective-permute-start(f32[1,32,360]{2,1,0:T(8,128)} %get-tuple-element.1469), channel_id=1, source_target_pairs={{0,1},{2,3},{4,5},{6,7},{8,9},{10,11},{12,13},{14,15},{16,17},{18,... | collective-permute-start | bytes 138248 | tf_op jit(solution)/shard_map/while/body/eval_jaxpr/ppermute | solution.py:16
  1119.9 32.4 %collective-permute-start.7 = (f32[2,32,360]{2,1,0:T(8,128)}, f32[2,32,360]{2,1,0:T(8,128)}, u32[]{:S(2)}, u32[]{:S(2)}) collective-permute-start(f32[2,32,360]{2,1,0:T(8,128)} %get-tuple-element.1479), channel_id=1, source_target_pairs={{8,0},{16,8},{24,16},{32,24},{40,32},{48,40},{56,48},{64,56},{72,6... | collective-permute-start | bytes 276488 | tf_op jit(solution)/shard_map/while/body/eval_jaxpr/ppermute | solution.py:27
  1157.2 23.3 %collective-permute-start.4 = (f32[1,32,360]{2,1,0:T(8,128)}, f32[1,32,360]{2,1,0:T(8,128)}, u32[]{:S(2)}, u32[]{:S(2)}) collective-permute-start(f32[1,32,360]{2,1,0:T(8,128)} %get-tuple-element.1468), channel_id=1, source_target_pairs={{1,0},{3,2},{5,4},{7,6},{9,8},{11,10},{13,12},{15,14},{17,16},{19,... | collective-permute-start | bytes 138248 | tf_op jit(solution)/shard_map/while/body/eval_jaxpr/ppermute | solution.py:19
  1158.5 22.0 %collective-permute-start.5 = (f32[1,32,360]{2,1,0:T(8,128)}, f32[1,32,360]{2,1,0:T(8,128)}, u32[]{:S(2)}, u32[]{:S(2)}) collective-permute-start(f32[1,32,360]{2,1,0:T(8,128)} %get-tuple-element.1469), channel_id=1, source_target_pairs={{0,1},{2,3},{4,5},{6,7},{8,9},{10,11},{12,13},{14,15},{16,17},{18,... | collective-permute-start | bytes 138248 | tf_op jit(solution)/shard_map/while/body/eval_jaxpr/ppermute | solution.py:16
  1171.7 32.4 %collective-permute-start.7 = (f32[2,32,360]{2,1,0:T(8,128)}, f32[2,32,360]{2,1,0:T(8,128)}, u32[]{:S(2)}, u32[]{:S(2)}) collective-permute-start(f32[2,32,360]{2,1,0:T(8,128)} %get-tuple-element.1479), channel_id=1, source_target_pairs={{8,0},{16,8},{24,16},{32,24},{40,32},{48,40},{56,48},{64,56},{72,6... | collective-permute-start | bytes 276488 | tf_op jit(solution)/shard_map/while/body/eval_jaxpr/ppermute | solution.py:27
  1209.0 23.3 %collective-permute-start.4 = (f32[1,32,360]{2,1,0:T(8,128)}, f32[1,32,360]{2,1,0:T(8,128)}, u32[]{:S(2)}, u32[]{:S(2)}) collective-permute-start(f32[1,32,360]{2,1,0:T(8,128)} %get-tuple-element.1468), channel_id=1, source_target_pairs={{1,0},{3,2},{5,4},{7,6},{9,8},{11,10},{13,12},{15,14},{17,16},{19,... | collective-permute-start | bytes 138248 | tf_op jit(solution)/shard_map/while/body/eval_jaxpr/ppermute | solution.py:19
  1210.2 22.0 %collective-permute-start.5 = (f32[1,32,360]{2,1,0:T(8,128)}, f32[1,32,360]{2,1,0:T(8,128)}, u32[]{:S(2)}, u32[]{:S(2)}) collective-permute-start(f32[1,32,360]{2,1,0:T(8,128)} %get-tuple-element.1469), channel_id=1, source_target_pairs={{0,1},{2,3},{4,5},{6,7},{8,9},{10,11},{12,13},{14,15},{16,17},{18,... | collective-permute-start | bytes 138248 | tf_op jit(solution)/shard_map/while/body/eval_jaxpr/ppermute | solution.py:16
  1223.4 32.4 %collective-permute-start.7 = (f32[2,32,360]{2,1,0:T(8,128)}, f32[2,32,360]{2,1,0:T(8,128)}, u32[]{:S(2)}, u32[]{:S(2)}) collective-permute-start(f32[2,32,360]{2,1,0:T(8,128)} %get-tuple-element.1479), channel_id=1, source_target_pairs={{8,0},{16,8},{24,16},{32,24},{40,32},{48,40},{56,48},{64,56},{72,6... | collective-permute-start | bytes 276488 | tf_op jit(solution)/shard_map/while/body/eval_jaxpr/ppermute | solution.py:27
  1260.7 23.3 %collective-permute-start.4 = (f32[1,32,360]{2,1,0:T(8,128)}, f32[1,32,360]{2,1,0:T(8,128)}, u32[]{:S(2)}, u32[]{:S(2)}) collective-permute-start(f32[1,32,360]{2,1,0:T(8,128)} %get-tuple-element.1468), channel_id=1, source_target_pairs={{1,0},{3,2},{5,4},{7,6},{9,8},{11,10},{13,12},{15,14},{17,16},{19,... | collective-permute-start | bytes 138248 | tf_op jit(solution)/shard_map/while/body/eval_jaxpr/ppermute | solution.py:19
  1262.0 22.0 %collective-permute-start.5 = (f32[1,32,360]{2,1,0:T(8,128)}, f32[1,32,360]{2,1,0:T(8,128)}, u32[]{:S(2)}, u32[]{:S(2)}) collective-permute-start(f32[1,32,360]{2,1,0:T(8,128)} %get-tuple-element.1469), channel_id=1, source_target_pairs={{0,1},{2,3},{4,5},{6,7},{8,9},{10,11},{12,13},{14,15},{16,17},{18,... | collective-permute-start | bytes 138248 | tf_op jit(solution)/shard_map/while/body/eval_jaxpr/ppermute | solution.py:16
  1275.2 32.4 %collective-permute-start.7 = (f32[2,32,360]{2,1,0:T(8,128)}, f32[2,32,360]{2,1,0:T(8,128)}, u32[]{:S(2)}, u32[]{:S(2)}) collective-permute-start(f32[2,32,360]{2,1,0:T(8,128)} %get-tuple-element.1479), channel_id=1, source_target_pairs={{8,0},{16,8},{24,16},{32,24},{40,32},{48,40},{56,48},{64,56},{72,6... | collective-permute-start | bytes 276488 | tf_op jit(solution)/shard_map/while/body/eval_jaxpr/ppermute | solution.py:27
  1312.5 23.3 %collective-permute-start.4 = (f32[1,32,360]{2,1,0:T(8,128)}, f32[1,32,360]{2,1,0:T(8,128)}, u32[]{:S(2)}, u32[]{:S(2)}) collective-permute-start(f32[1,32,360]{2,1,0:T(8,128)} %get-tuple-element.1468), channel_id=1, source_target_pairs={{1,0},{3,2},{5,4},{7,6},{9,8},{11,10},{13,12},{15,14},{17,16},{19,... | collective-permute-start | bytes 138248 | tf_op jit(solution)/shard_map/while/body/eval_jaxpr/ppermute | solution.py:19
  1313.8 22.0 %collective-permute-start.5 = (f32[1,32,360]{2,1,0:T(8,128)}, f32[1,32,360]{2,1,0:T(8,128)}, u32[]{:S(2)}, u32[]{:S(2)}) collective-permute-start(f32[1,32,360]{2,1,0:T(8,128)} %get-tuple-element.1469), channel_id=1, source_target_pairs={{0,1},{2,3},{4,5},{6,7},{8,9},{10,11},{12,13},{14,15},{16,17},{18,... | collective-permute-start | bytes 138248 | tf_op jit(solution)/shard_map/while/body/eval_jaxpr/ppermute | solution.py:16
  1327.0 32.4 %collective-permute-start.7 = (f32[2,32,360]{2,1,0:T(8,128)}, f32[2,32,360]{2,1,0:T(8,128)}, u32[]{:S(2)}, u32[]{:S(2)}) collective-permute-start(f32[2,32,360]{2,1,0:T(8,128)} %get-tuple-element.1479), channel_id=1, source_target_pairs={{8,0},{16,8},{24,16},{32,24},{40,32},{48,40},{56,48},{64,56},{72,6... | collective-permute-start | bytes 276488 | tf_op jit(solution)/shard_map/while/body/eval_jaxpr/ppermute | solution.py:27
  1364.3 23.3 %collective-permute-start.4 = (f32[1,32,360]{2,1,0:T(8,128)}, f32[1,32,360]{2,1,0:T(8,128)}, u32[]{:S(2)}, u32[]{:S(2)}) collective-permute-start(f32[1,32,360]{2,1,0:T(8,128)} %get-tuple-element.1468), channel_id=1, source_target_pairs={{1,0},{3,2},{5,4},{7,6},{9,8},{11,10},{13,12},{15,14},{17,16},{19,... | collective-permute-start | bytes 138248 | tf_op jit(solution)/shard_map/while/body/eval_jaxpr/ppermute | solution.py:19
  1365.6 22.0 %collective-permute-start.5 = (f32[1,32,360]{2,1,0:T(8,128)}, f32[1,32,360]{2,1,0:T(8,128)}, u32[]{:S(2)}, u32[]{:S(2)}) collective-permute-start(f32[1,32,360]{2,1,0:T(8,128)} %get-tuple-element.1469), channel_id=1, source_target_pairs={{0,1},{2,3},{4,5},{6,7},{8,9},{10,11},{12,13},{14,15},{16,17},{18,... | collective-permute-start | bytes 138248 | tf_op jit(solution)/shard_map/while/body/eval_jaxpr/ppermute | solution.py:16
  1378.7 32.4 %collective-permute-start.7 = (f32[2,32,360]{2,1,0:T(8,128)}, f32[2,32,360]{2,1,0:T(8,128)}, u32[]{:S(2)}, u32[]{:S(2)}) collective-permute-start(f32[2,32,360]{2,1,0:T(8,128)} %get-tuple-element.1479), channel_id=1, source_target_pairs={{8,0},{16,8},{24,16},{32,24},{40,32},{48,40},{56,48},{64,56},{72,6... | collective-permute-start | bytes 276488 | tf_op jit(solution)/shard_map/while/body/eval_jaxpr/ppermute | solution.py:27
  1416.0 23.3 %collective-permute-start.4 = (f32[1,32,360]{2,1,0:T(8,128)}, f32[1,32,360]{2,1,0:T(8,128)}, u32[]{:S(2)}, u32[]{:S(2)}) collective-permute-start(f32[1,32,360]{2,1,0:T(8,128)} %get-tuple-element.1468), channel_id=1, source_target_pairs={{1,0},{3,2},{5,4},{7,6},{9,8},{11,10},{13,12},{15,14},{17,16},{19,... | collective-permute-start | bytes 138248 | tf_op jit(solution)/shard_map/while/body/eval_jaxpr/ppermute | solution.py:19
  1417.3 22.0 %collective-permute-start.5 = (f32[1,32,360]{2,1,0:T(8,128)}, f32[1,32,360]{2,1,0:T(8,128)}, u32[]{:S(2)}, u32[]{:S(2)}) collective-permute-start(f32[1,32,360]{2,1,0:T(8,128)} %get-tuple-element.1469), channel_id=1, source_target_pairs={{0,1},{2,3},{4,5},{6,7},{8,9},{10,11},{12,13},{14,15},{16,17},{18,... | collective-permute-start | bytes 138248 | tf_op jit(solution)/shard_map/while/body/eval_jaxpr/ppermute | solution.py:16
  1430.5 32.4 %collective-permute-start.7 = (f32[2,32,360]{2,1,0:T(8,128)}, f32[2,32,360]{2,1,0:T(8,128)}, u32[]{:S(2)}, u32[]{:S(2)}) collective-permute-start(f32[2,32,360]{2,1,0:T(8,128)} %get-tuple-element.1479), channel_id=1, source_target_pairs={{8,0},{16,8},{24,16},{32,24},{40,32},{48,40},{56,48},{64,56},{72,6... | collective-permute-start | bytes 276488 | tf_op jit(solution)/shard_map/while/body/eval_jaxpr/ppermute | solution.py:27
  1596.1 48.4 %collective-permute-start.13 = (f32[21,720]{1,0:T(8,128)S(1)}, f32[21,720]{1,0:T(8,128)S(1)}, u32[]{:S(2)}, u32[]{:S(2)}) collective-permute-start(f32[21,720]{1,0:T(8,128)S(1)} %slice.577), channel_id=1, source_target_pairs={{0,1},{1,2},{2,3},{3,4},{4,5},{5,6},{6,7},{8,9},{9,10},{10,11},{11... | collective-permute-start | bytes 181448
  1602.1 41.4 %collective-permute-start.12 = (f32[21,360]{1,0:T(8,128)S(1)}, f32[21,360]{1,0:T(8,128)S(1)}, u32[]{:S(2)}, u32[]{:S(2)}) collective-permute-start(f32[21,360]{1,0:T(8,128)S(1)} %slice.576), channel_id=1, source_target_pairs={{0,1},{1,2},{2,3},{3,4},{4,5},{5,6},{6,7},{8,9},{9,10},{10,11},{11... | collective-permute-start | bytes 90728
  1606.4 39.1 %collective-permute-start.11 = (f32[42,360]{1,0:T(8,128)S(1)}, f32[42,360]{1,0:T(8,128)S(1)}, u32[]{:S(2)}, u32[]{:S(2)}) collective-permute-start(f32[42,360]{1,0:T(8,128)S(1)} %slice.575), channel_id=1, source_target_pairs={{0,1},{1,2},{2,3},{3,4},{4,5},{5,6},{6,7},{8,9},{9,10},{10,11},{11... | collective-permute-start | bytes 181448
  (485 other events, 4051.6 us)
Sparse Core Ops, SparseCore 0:
  1610.4 83.4 all-reduce.13
where the time goes:
time: 1730 us; the launch traced here: 1700 us
  starting transfers between devices  633 us (37%)
  local copies, waits for them, and re-layouts  279 us (16%)
  matrix products  243 us (14%)
  other arithmetic  205 us (12%)
  blocking collectives  161 us (9%)
  waiting for transfers between devices  152 us (9%)
    ppermute x57, starting transfers between devices, extended(): lax.ppermute(lax.slice_in_dim(block, block.shape[dim] - width, None, axis...  336 us
    ppermute x95, starting transfers between devices, passed_along(): return lax.ppermute(block, axis, route)  210 us
    unnamed x2, blocking collectives  161 us
    dot_general x136, matrix products, project(): out = jnp.dot(flat, matrix, preferred_element_type=jnp.float32)  109 us
    ppermute x95, waiting for transfers between devices, passed_along(): return lax.ppermute(block, axis, route)  104 us
    dot_general x57, matrix products, outer_sum(): lax.dot_general(left.reshape(-1, left.shape[-1]), right.reshape(-1, right...  98.9 us
    ppermute x57, starting transfers between devices, extended(): lax.ppermute(lax.slice_in_dim(block, 0, width, axis=dim), axis, backward)  73.4 us
    slice x38, local copies, waits for them, and re-layouts, depthwise_apply(): kernel[tap_index]  63.1 us
  transfers between devices with their start and end apart: 213, of which 39 were waited for; matrix products, arithmetic and copies ran while one was open for 31% of the time, Pallas kernels for 0%

commit v1 on v0

v1 whole, which is shorter than its diff:
```python
import jax
import jax.numpy as jnp
from jax import lax
from jax.experimental import pallas as pl
from jax.experimental.pallas import tpu as pltpu
from jax.sharding import Mesh, PartitionSpec as P

loss_scale = 64.0
root_coef = 0.7978845608028654
cube_coef = 0.044715

C1 = 360
C2 = 720
PAD1 = 384
HEAD = 512
CLASSES = 150
F32 = jnp.float32
BF16 = jnp.bfloat16
VMEM_LIMIT = 30 * 2**20

WROWS = 464
LROWS = 224
RROWS = 240
GROWS = 256


def params():
    return pltpu.CompilerParams(vmem_limit_bytes=VMEM_LIMIT)


def gelu_pair(values):
    inner = root_coef * (values + cube_coef * values * values * values)
    tangent = jnp.tanh(inner)
    result = 0.5 * values * (1.0 + tangent)
    slope = 0.5 * (1.0 + tangent) + 0.5 * values * (1.0 - tangent * tangent) * root_coef * (
        1.0 + 3.0 * cube_coef * values * values
    )
    return result, slope


def gelu_only(values):
    inner = root_coef * (values + cube_coef * values * values * values)
    return 0.5 * values * (1.0 + jnp.tanh(inner))


def dot(left, right):
    return jnp.dot(left, right, preferred_element_type=F32)


def dot_nt(left, right):
    return lax.dot_general(left, right, (((1,), (1,)), ((), ())), preferred_element_type=F32)


def dot_tn(left, right):
    return lax.dot_general(left, right, (((0,), (0,)), ((), ())), preferred_element_type=F32)


def shifted(even, odd):
    spot = lax.broadcasted_iota(jnp.int32, even.shape, 0)
    after = jnp.where(spot == 15, 0.0, pltpu.roll(even, 15, 0))
    before = jnp.where(spot == 0, 0.0, pltpu.roll(odd, 1, 0))
    return after, before


def neighbours(blocks):
    rows = []
    for r in range(4):
        even, odd = blocks[2 * r], blocks[2 * r + 1]
        after, before = shifted(even, odd)
        rows.append(((before, even, odd), (even, odd, after)))
    return rows


def stencil(rows, taps):
    out = []
    for r in range(4):
        for b in range(2):
            total = None
            for i in (-1, 0, 1):
                if 0 <= r + i < 4:
                    for j in range(3):
                        term = taps[3 * (i + 1) + j] * rows[r + i][b][j]
                        total = term if total is None else total + term
            out.append(total)
    return out


def tap_sums(rows, grads):
    sums = []
    for i in (-1, 0, 1):
        for j in range(3):
            total = None
            for r in range(4):
                if 0 <= r + i < 4:
                    for b in range(2):
                        term = rows[r + i][b][j] * grads[2 * r + b]
                        total = term if total is None else total + term
            sums.append(jnp.sum(total, axis=0, keepdims=True))
    return sums


def pool(blocks):
    parts = [blocks[4 * q] + blocks[4 * q + 1] + blocks[4 * q + 2] + blocks[4 * q + 3] for q in range(2)]
    return jnp.concatenate(parts, axis=0)


def split(values):
    return [values[16 * q : 16 * q + 16] for q in range(8)]


def join(blocks):
    return jnp.concatenate(blocks, axis=0)


def up2(values):
    return [values[16 * (q // 4) : 16 * (q // 4) + 16] for q in range(8)]


def decode_aux(aux):
    taps = [aux[t : t + 1, 0:C1] for t in range(8)] + [aux[0:1, PAD1 : PAD1 + C1]]
    gain1 = aux[1:2, PAD1 : PAD1 + C1]
    gain2 = jnp.concatenate([aux[2:3, PAD1 : 2 * PAD1], aux[3:4, PAD1:C2]], axis=1)
    return taps, gain1, gain2


def put(ref, row, values):
    width = values.shape[1]
    if width < PAD1:
        values = jnp.concatenate([values, jnp.zeros((values.shape[0], PAD1 - width), F32)], axis=1)
    ref[row : row + values.shape[0], :] = values


def put_two(ref, row, values):
    put(ref, row, values[:, 0:PAD1])
    put(ref, row + values.shape[0], values[:, PAD1:C2])


def get_two(ref, row):
    return jnp.concatenate([ref[row : row + 32, :], ref[row + 32 : row + 64, 0 : C2 - PAD1]], axis=1)


def pack_kernel(where, up_ref, mix_ref, down_ref, tap_ref, g1_ref, g2_ref, out_ref):
    core = where[2]
    mix = mix_ref[0].astype(F32)

    @pl.when(core == 0)
    def _():
        up = up_ref[0].astype(F32)
        out_ref[0:368, 0:C1] = up[0:368]
        out_ref[0:352, PAD1 : PAD1 + C1] = up[368:720]
        out_ref[368:464, 0:C1] = mix[0:96]
        out_ref[368:464, PAD1 : PAD1 + C1] = mix[96:192]

    @pl.when(core == 1)
    def _():
        down = down_ref[0].astype(F32)
        taps = tap_ref[0].astype(F32)
        out_ref[0:360, 0:C2] = down
        out_ref[360:368, 0:C1] = taps[0:8]
        out_ref[360:361, PAD1 : PAD1 + C1] = taps[8:9]
        out_ref[361:362, PAD1 : PAD1 + C1] = g1_ref[...]
        out_ref[362:363, PAD1 : 2 * PAD1] = g2_ref[:, 0:PAD1]
        out_ref[363:364, PAD1:C2] = g2_ref[:, PAD1:C2]
        out_ref[368:464, 0:C1] = mix[192:288]
        out_ref[368:440, PAD1 : PAD1 + C1] = mix[288:360]


def unpack_kernel(where, o0, o1, r1, r2, r3, s1, s2, s3, up_ref, mix_ref, down_ref, aux_ref):
    z, core = where[1], where[2]

    def write(first, second, column):
        up = jnp.concatenate([first[0:368, 0:C1], first[0:352, PAD1 : PAD1 + C1]], axis=0)
        up_ref[column] = up.astype(BF16)
        mix = jnp.concatenate(
            [
                first[368:464, 0:C1],
                first[368:464, PAD1 : PAD1 + C1],
                second[368:464, 0:C1],
                second[368:440, PAD1 : PAD1 + C1],
            ],
            axis=0,
        )
        mix_ref[column] = mix.astype(BF16)
        down_ref[column] = second[0:360, 0:C2].astype(BF16)
        aux_ref[column] = second[360:368, :]

    last, following, opposite = lax.rem(z + 3, 4), lax.rem(z + 1, 4), lax.rem(z + 2, 4)

    @pl.when(core == 0)
    def _():
        write(o0, o1, z)
        write(r1, s2, last)
        write(r2, s1, following)
        write(r3, s3, opposite)

    @pl.when(core == 1)
    def _():
        write(o1, o0, z)
        write(s1, r2, last)
        write(s2, r1, following)
        write(s3, r3, opposite)


def forward_kernel(full, where, msg_ref, stem_ref, up_ref, mix_ref, down_ref, aux_ref, out_ref, *rest):
    if full:
        mixture_ref, slope1_ref, slope2_ref, left_ref, half_ref, state1, state2 = rest
    else:
        state1, state2 = rest
    step = pl.program_id(0)

    @pl.when(step == 0)
    def _():
        state1[...] = msg_ref[0:128, 0:C1]
        state2[...] = get_two(msg_ref, 128)

    taps, gain1, gain2 = decode_aux(aux_ref[0])
    narrow = state2[...].astype(BF16)
    lifted_up = dot(narrow, up_ref[0])
    ups = up2(lifted_up)
    mixture = [stem_ref[16 * q : 16 * q + 16, 0:C1] + ups[q] for q in range(8)]
    depth = join(stencil(neighbours(mixture), taps))
    if full:
        active, slope1 = gelu_pair(depth)
    else:
        active = gelu_only(depth)
    hidden = active.astype(BF16)
    next1 = gain1 * state1[...] + dot(hidden, mix_ref[0])
    pooled = (pool(split(next1)) * 0.25).astype(BF16)
    lifted = dot(pooled, down_ref[0])
    if full:
        active2, slope2 = gelu_pair(lifted)
    else:
        active2 = gelu_only(lifted)
    next2 = gain2 * state2[...] + active2
    state1[...] = next1
    state2[...] = next2
    if full:
        core = where[2]
        mixture_ref[0] = join(mixture)
        slope1_ref[0] = slope1
        slope2_ref[0] = slope2
        here = left_ref.at[0]
        put(here, 0, hidden.astype(F32))
        put(here, 128, pooled.astype(F32))
        put_two(here, 160, narrow.astype(F32))
        half = LROWS // 2
        half_ref[0] = left_ref[0, pl.ds(pl.multiple_of(core * half, 8), half), :]

    @pl.when(step == 3)
    def _():
        put(out_ref, 0, next1)
        put_two(out_ref, 128, next2)


def head_kernel(where, msg_ref, stem_ref, one_ref, two_ref, cls_ref, out_ref, first, second):
    state1 = msg_ref[0:128, 0:C1].astype(BF16)
    state2 = get_two(msg_ref, 128).astype(BF16)
    labels = stem_ref[:, C1 : C1 + 1].astype(jnp.int32)
    second[...] = dot(state2, two_ref[...])
    first[...] = dot(state1, one_ref[...])
    lateral = first[...] + join(up2(second[...]))
    active, slope = gelu_pair(lateral)
    logits = dot(active.astype(BF16), cls_ref[...])
    classes = lax.broadcasted_iota(jnp.int32, logits.shape, 1)
    logits = jnp.where(classes < CLASSES, logits, -jnp.inf)
    logits = logits - jnp.max(logits, axis=-1, keepdims=True)
    powers = jnp.exp(logits)
    probs = powers / jnp.sum(powers, axis=-1, keepdims=True)
    onehot = (classes == labels).astype(F32)
    grad_logits = (probs - onehot) * (loss_scale / 2048.0)
    grad_lat = dot_nt(grad_logits.astype(BF16), cls_ref[...]) * slope
    put(out_ref, 0, dot_nt(grad_lat.astype(BF16), one_ref[...]))
    put_two(out_ref, 128, dot_nt(pool(split(grad_lat)).astype(BF16), two_ref[...]))


def backward_kernel(
    full, where, msg_ref, head_ref, slope1_ref, slope2_ref, up_ref, mix_ref, down_ref, aux_ref, *rest
):
    if full:
        mixture_ref, out_ref, right_ref, half_ref, stem_out, cot1, cot2, stem_sum = rest
    else:
        out_ref, cot1, cot2 = rest
    step = pl.program_id(0)

    @pl.when(step == 0)
    def _():
        @pl.when(where[0] == 3)
        def _():
            cot1[...] = head_ref[0:128, 0:C1]
            cot2[...] = get_two(head_ref, 128)

        @pl.when(where[0] != 3)
        def _():
            cot1[...] = msg_ref[0:128, 0:C1]
            cot2[...] = get_two(msg_ref, 128)

    taps, gain1, gain2 = decode_aux(aux_ref[0])
    old2 = cot2[...]
    grad_s = (old2 * slope2_ref[0]).astype(BF16)
    back = dot_nt(grad_s, down_ref[0]) * 0.25
    total1 = cot1[...] + join(up2(back))
    narrow_total = total1.astype(BF16)
    grad_depth = dot_nt(narrow_total, mix_ref[0]) * slope1_ref[0]
    grads = split(grad_depth)
    grad_mixture = stencil(neighbours(grads), taps[::-1])
    grad_narrow = pool(grad_mixture).astype(BF16)
    next2 = gain2 * old2 + dot_nt(grad_narrow, up_ref[0])
    next1 = gain1 * total1
    cot1[...] = next1
    cot2[...] = next2
    if full:
        core = where[2]
        here = right_ref.at[0]
        put(here, 0, narrow_total.astype(F32))
        put(here, 128, grad_narrow.astype(F32))
        put_two(here, 160, grad_s.astype(F32))
        sums = tap_sums(neighbours(split(mixture_ref[0])), grads)
        put(here, 224, jnp.concatenate(sums + [jnp.zeros((7, C1), F32)], axis=0))
        half = RROWS // 2
        half_ref[0] = right_ref[0, pl.ds(pl.multiple_of(core * half, 8), half), :]
        mixed = join(grad_mixture)

        @pl.when(step == 0)
        def _():
            stem_sum[...] = mixed

        @pl.when(step != 0)
        def _():
            stem_sum[...] = stem_sum[...] + mixed

    @pl.when(step == 3)
    def _():
        put(out_ref, 0, next1)
        put_two(out_ref, 128, next2)
        if full:
            mine = stem_sum[pl.ds(pl.multiple_of(where[2] * 64, 8), 64), :]
            stem_out[:, 0:C1] = mine
            stem_out[:, C1:PAD1] = jnp.zeros((64, PAD1 - C1), F32)


def weight_kernel(where, lo, l1, l2, l3, m1, m2, m3, ro, r1, r2, r3, s1, s2, s3, out_ref, left, right):
    core, block = where[2], where[3]
    for full_ref, own, pairs, rows in (
        (left, lo, ((l1, m2), (l2, m1), (l3, m3)), LROWS),
        (right, ro, ((r1, s2), (r2, s1), (r3, s3)), RROWS),
    ):
        half = rows // 2
        mine = pl.ds(pl.multiple_of(core * half, 8), half)
        other = pl.ds(pl.multiple_of((1 - core) * half, 8), half)
        full_ref[0] = own[0]
        for at, (near, far) in enumerate(pairs):
            full_ref[at + 1, mine, :] = near[0]
            full_ref[at + 1, other, :] = far[0]

    def stack(ref, row, count):
        return jnp.concatenate([ref[q, row : row + count, :] for q in range(4)], axis=0)

    back1 = lax.rem(PAD1 - 45 * block, PAD1)
    back2 = lax.rem(2 * PAD1 - 90 * block, 2 * PAD1)
    hidden = pltpu.roll(stack(left, 0, 128), back1, 1)[:, 0:128].astype(BF16)
    pooled = pltpu.roll(stack(left, 128, 32), back1, 1)[:, 0:128].astype(BF16)
    narrow = jnp.concatenate([stack(left, 160, 32), stack(left, 192, 32)], axis=1)
    narrow = pltpu.roll(narrow, back2, 1)[:, 0:128].astype(BF16)
    grad_mix = dot_tn(hidden, stack(right, 0, 128).astype(BF16))
    grad_up = dot_tn(narrow, stack(right, 128, 32).astype(BF16))
    grad_lo = dot_tn(pooled, stack(right, 160, 32).astype(BF16))
    grad_hi = dot_tn(pooled, stack(right, 192, 32).astype(BF16))
    taps = right[0, 224:240, :] + right[1, 224:240, :] + right[2, 224:240, :] + right[3, 224:240, :]
    out_ref[0, 0:96, :] = grad_up[0:96]
    out_ref[0, 96:144, :] = grad_mix[0:48]
    out_ref[0, 144:192, :] = grad_lo[0:48]
    out_ref[0, 192:240, :] = grad_hi[0:48]
    out_ref[0, 240:256, :] = pltpu.roll(taps, back1, 1)


def final_kernel(own, near, far, up_ref, mix_ref, down_ref, tap_ref):
    total = own[0] + near[...] + far[...]
    up_ref[0] = total[0:90, 0:C1]
    mix_ref[0] = total[96:141, 0:C1]
    down_ref[0, :, 0:PAD1] = total[144:189]
    down_ref[0, :, PAD1:C2] = total[192:237, 0 : C2 - PAD1]
    tap_ref[0] = total[240:249, 0:45]


def shape(*dims, kind=F32):
    return jax.ShapeDtypeStruct(dims, kind)


SMEM = pl.BlockSpec(memory_space=pltpu.SMEM)
WHOLE = pl.BlockSpec(memory_space=pltpu.VMEM)


def shards(stem, labels, up_proj, mix_proj, down_proj, dw_kernel, gain1, gain2, lat_one, lat_two, classifier):
    y, z = lax.axis_index("y"), lax.axis_index("z")
    core = lax.axis_index("core")
    block = lax.axis_index("xl") * 4 + core * 2 + lax.axis_index("xh")
    where = jnp.stack([y, z, core, block]).astype(jnp.int32)
    sign = 1 - 2 * core

    def z_ring(step):
        return [
            (2 * at + c, 2 * ((at + (step if c == 0 else -step)) % 4) + c) for at in range(4) for c in range(2)
        ]

    def x_spot(x, c):
        return ((x % 2) * 2 + c) * 2 + x // 2

    def x_ring(step):
        return [
            (x_spot(x, c), x_spot((x + (step if c == 0 else -step)) % 4, c)) for x in range(4) for c in range(2)
        ]

    z_axes, x_axes = ("z", "core"), ("xl", "core", "xh")

    def swap(values):
        return lax.ppermute(values, "core", [(0, 1), (1, 0)])

    def gather(half, axes, ring):
        near = lax.ppermute(half, axes, ring(1))
        away = lax.ppermute(half, axes, ring(-1))
        opposite = lax.ppermute(near, axes, ring(1))
        return near, away, opposite, swap(near), swap(away), swap(opposite)

    piece = lax.dynamic_index_in_dim(stem, z, 0, keepdims=False).astype(F32)
    marks = lax.dynamic_index_in_dim(labels, z, 0, keepdims=False).astype(F32)
    piece = jnp.concatenate([piece, marks[..., None], jnp.zeros((2, 32, PAD1 - C1 - 1), F32)], axis=-1)
    piece = piece.reshape(2, 16, 2, PAD1).transpose(0, 2, 1, 3).reshape(64, PAD1)
    pairs = [(c, s) for c in range(2) for s in range(2)]
    same = lax.ppermute(piece, ("core", "xh"), [(2 * c + s, 2 * s + c) for c, s in pairs])
    cross = lax.ppermute(piece, ("core", "xh"), [(2 * c + s, 2 * (1 - s) + c) for c, s in pairs])
    crop = jnp.where(core == 0, jnp.concatenate([same, cross], 0), jnp.concatenate([cross, same], 0))

    half = pl.pallas_call(
        pack_kernel,
        out_shape=shape(WROWS, 2 * PAD1),
        in_specs=[SMEM] + [WHOLE] * 6,
        out_specs=WHOLE,
        compiler_params=params(),
        name="pack",
    )(where, up_proj, mix_proj, down_proj, dw_kernel, gain1, gain2)
    pieces = gather(half, z_axes, z_ring)
    weights = pl.pallas_call(
        unpack_kernel,
        out_shape=(
            shape(4, C2, C1, kind=BF16),
            shape(4, C1, C1, kind=BF16),
            shape(4, C1, C2, kind=BF16),
            shape(4, 8, 2 * PAD1),
        ),
        in_specs=[SMEM] + [WHOLE] * 8,
        out_specs=(WHOLE,) * 4,
        compiler_params=params(),
        name="unpack",
    )(where, half, swap(half), *pieces)

    def per(*dims, flip=False):
        zeros = (0,) * len(dims)
        if flip:
            return pl.BlockSpec((1,) + dims, lambda j: (3 - j,) + zeros)
        return pl.BlockSpec((1,) + dims, lambda j: (j,) + zeros)

    def fixed(*dims):
        return pl.BlockSpec(dims, lambda j: (0,) * len(dims))

    def weight_specs(flip):
        return [per(C2, C1, flip=flip), per(C1, C1, flip=flip), per(C1, C2, flip=flip), per(8, 2 * PAD1, flip=flip)]

    def forward(msg, full):
        outs, specs = [shape(192, PAD1)], [fixed(192, PAD1)]
        if full:
            for dims in ((128, C1), (128, C1), (32, C2), (LROWS, PAD1), (LROWS // 2, PAD1)):
                outs.append(shape(4, *dims))
                specs.append(per(*dims))
        return pl.pallas_call(
            lambda *refs: forward_kernel(full, *refs),
            grid=(4,),
            out_shape=tuple(outs),
            in_specs=[SMEM, fixed(192, PAD1), fixed(128, PAD1)] + weight_specs(False),
            out_specs=tuple(specs),
            scratch_shapes=[pltpu.VMEM((128, C1), F32), pltpu.VMEM((32, C2), F32)],
            compiler_params=params(),
            name="forward_full" if full else "forward_light",
        )(where, msg, crop, *weights)

    msg = jnp.zeros((192, PAD1), F32)
    for tick in range(3):
        msg = lax.ppermute(forward(msg, False)[0], "y", [(0, 1), (1, 2), (2, 3)])
    msg, mixture, slope1, slope2, left, left_half = forward(msg, True)
    lefts = gather(left_half, x_axes, x_ring)

    head = pl.pallas_call(
        head_kernel,
        out_shape=shape(192, PAD1),
        in_specs=[SMEM] + [WHOLE] * 5,
        out_specs=WHOLE,
        scratch_shapes=[pltpu.VMEM((128, HEAD), F32), pltpu.VMEM((32, HEAD), F32)],
        compiler_params=params(),
        name="head",
    )(where, msg, crop, lat_one, lat_two, jnp.pad(classifier, ((0, 0), (0, 256 - CLASSES))))

    def backward(msg, full):
        outs, specs = [shape(192, PAD1)], [fixed(192, PAD1)]
        operands = [where, msg, head, slope1, slope2, *weights]
        in_specs = [SMEM, fixed(192, PAD1), fixed(192, PAD1), per(128, C1, flip=True), per(32, C2, flip=True)]
        in_specs += weight_specs(True)
        scratch = [pltpu.VMEM((128, C1), F32), pltpu.VMEM((32, C2), F32)]
        if full:
            operands.append(mixture)
            in_specs.append(per(128, C1, flip=True))
            for dims in ((RROWS, PAD1), (RROWS // 2, PAD1)):
                outs.append(shape(4, *dims))
                specs.append(per(*dims, flip=True))
            outs.append(shape(64, PAD1))
            specs.append(fixed(64, PAD1))
            scratch.append(pltpu.VMEM((128, C1), F32))
        return pl.pallas_call(
            lambda *refs: backward_kernel(full, *refs),
            grid=(4,),
            out_shape=tuple(outs),
            in_specs=in_specs,
            out_specs=tuple(specs),
            scratch_shapes=scratch,
            compiler_params=params(),
            name="backward_full" if full else "backward_light",
        )(*operands)

    cots = head
    for tick in range(3):
        cots = lax.ppermute(backward(cots, False)[0], "y", [(1, 0), (2, 1), (3, 2)])
    _, right, right_half, stem_part = backward(cots, True)
    rights = gather(right_half, x_axes, x_ring)

    order = jnp.stack([z + sign + 4, z - sign + 4, z + 2, z]) % 4
    spots = jnp.concatenate([where, order.astype(jnp.int32)])

    def pick(*dims):
        return pl.BlockSpec((1,) + dims, lambda j, at: (at[4 + j], 0, 0))

    partial = pl.pallas_call(
        weight_kernel,
        grid_spec=pltpu.PrefetchScalarGridSpec(
            num_scalar_prefetch=1,
            grid=(4,),
            in_specs=[pick(LROWS, PAD1)]
            + [pick(LROWS // 2, PAD1)] * 6
            + [pick(RROWS, PAD1)]
            + [pick(RROWS // 2, PAD1)] * 6,
            out_specs=pl.BlockSpec((1, GROWS, PAD1), lambda j, at: (j, 0, 0)),
            scratch_shapes=[pltpu.VMEM((4, LROWS, PAD1), F32), pltpu.VMEM((4, RROWS, PAD1), F32)],
        ),
        out_shape=shape(4, GROWS, PAD1),
        compiler_params=params(),
        name="weight_grads",
    )(spots, left, *lefts, right, *rights)
    relay = lax.ppermute(partial[2], z_axes, z_ring(1))
    away = lax.ppermute(partial[1], z_axes, z_ring(-1))
    near = lax.ppermute(partial[0] + relay, z_axes, z_ring(1))
    grads = pl.pallas_call(
        final_kernel,
        out_shape=(shape(1, 90, C1), shape(1, 45, C1), shape(1, 45, C2), shape(1, 9, 45)),
        in_specs=[WHOLE] * 3,
        out_specs=(WHOLE,) * 4,
        compiler_params=params(),
        name="final",
    )(partial[3:4], near, away)

    cells = stem_part.reshape(4, 16, PAD1).transpose(1, 0, 2)
    cells = lax.all_to_all(cells, ("y", "z"), 0, 0, tiled=True)
    cells = cells.reshape(4, 4, 4, PAD1).sum(axis=0)
    cells = lax.ppermute(cells, ("core", "xh"), [(2 * k + h, 2 * h + k) for k, h in pairs])
    grad_stem = cells[..., 0:C1].reshape(4, 2, 2, C1)
    return (*grads, grad_stem)


def solution(mesh):
    fine = Mesh(mesh.devices.reshape(4, 4, 2, 2, 2), ("y", "z", "xl", "core", "xh"))
    col, dp, strip, both = ("y", "z"), ("xl", "core"), "xh", ("xl", "core", "xh")
    return jax.shard_map(
        shards,
        mesh=fine,
        in_specs=(
            P(dp, strip, None, None),
            P(dp, strip, None),
            P(col, None, None),
            P(col, None, None),
            P(col, None, None),
            P(col, None, None),
            P(col, None),
            P(col, None),
            P(),
            P(),
            P(),
        ),
        out_specs=(
            P(col, both, None),
            P(col, both, None),
            P(col, both, None),
            P(col, None, both),
            P(dp, strip, col, None),
        ),
        check_vma=False,
    )
```

time: 1730 us -> 277 us (0.16); the launches traced: 1700 us -> 273 us
  starting transfers between devices: 633 us -> 76.7 us
  local copies, waits for them, and re-layouts: 279 us -> 27.5 us
  matrix products: 243 us -> 0 us
  other arithmetic: 205 us -> 1.84 us
  blocking collectives: 161 us -> 10.4 us
  Pallas kernels: 0 us -> 45.3 us
  waiting for transfers between devices: 152 us -> 110 us
    ppermute x209 -> x31, starting transfers between devices: 619 us -> 76.7 us  [the longest x10 21.7 us: swap(): return lax.ppermute(values, 'core', [(0, 1), (1, 0)])]
    dot_general x253 -> x0, matrix products: 243 us -> none  [the longest x136 109 us: project(): out = jnp.dot(flat, matrix, preferred_element_type=jnp.float32)]
    unnamed x2 -> x0, blocking collectives: 161 us -> none
    slice x95 -> x0, local copies, waits for them, and re-layouts: 75.5 us -> none  [the longest x38 63.1 us: depthwise_apply(): kernel[tap_index]]
    dynamic_update_slice x38 -> x0, local copies, waits for them, and re-layouts: 61.7 us -> none  [backward_tick(): lax.dynamic_update_index_in_dim(acc_stem, pick(acc_stem, slot_index) + gr...]
    while x646 -> x0, local copies, waits for them, and re-layouts: 50.9 us -> none
    add x76 -> x1, other arithmetic: 48.6 us -> 0.06 us  [shards(): near = lax.ppermute(partial[0] + relay, z_axes, z_ring(1))]
    unnamed x5 -> x0, waiting for transfers between devices: 47.4 us -> none
  transfers between devices with their start and end apart: 213 -> 31, of which waited for: 39 -> 17; matrix products, arithmetic and copies ran while one was open for 31% -> 2% of each run, Pallas kernels for 0% -> 0%
where the time goes in v1:
time: 277 us; the launch traced here: 273 us
  waiting for transfers between devices  110 us (40%)
  starting transfers between devices  76.7 us (28%)
  Pallas kernels  45.3 us (16%)
  local copies, waits for them, and re-layouts  27.5 us (10%)
  blocking collectives  10.4 us (4%)
    ppermute x3, waiting for transfers between devices, gather(): near = lax.ppermute(half, axes, ring(1))  48.6 us
    unnamed x59, local copies, waits for them, and re-layouts  25.8 us
    ppermute x10, starting transfers between devices, swap(): return lax.ppermute(values, 'core', [(0, 1), (1, 0)])  21.7 us
    pallas_call x4, Pallas kernels, backward(): pl.pallas_call(lambda *refs: backward_kernel(full, *refs), grid=(4,), out...  16.8 us
    ppermute x3, waiting for transfers between devices, gather(): opposite = lax.ppermute(near, axes, ring(1))  16.6 us
    ppermute x3, waiting for transfers between devices, shards(): msg = lax.ppermute(forward(msg, False)[0], 'y', [(0, 1), (1, 2), (2, 3)])  16.1 us
    pallas_call x4, Pallas kernels, forward(): pl.pallas_call(lambda *refs: forward_kernel(full, *refs), grid=(4,), out_...  16.1 us
    ppermute x3, starting transfers between devices, gather(): near = lax.ppermute(half, axes, ring(1))  15 us
  transfers between devices with their start and end apart: 31, of which 17 were waited for; matrix products, arithmetic and copies ran while one was open for 2% of the time, Pallas kernels for 0%

profile of v1, /device:TPU:25, one launch (start us, length us, event | category | flops | bytes accessed | tf_op | source)
XLA Modules:
  0.0 273.2 jit_solution(5107205128251004925)
XLA Ops:
  0.7 1.1 copy-done.19
  1.8 1.0 copy-done.20
  6.5 3.8 %collective-permute-start.3 = (f32[464,768]{1,0:T(8,128)S(1)}, f32[464,768]{1,0:T(8,128)S(1)}, u32[]{:S(2)}, u32[]{:S(2)}) collective-permute-start(f32[464,768]{1,0:T(8,128)S(1)} %pack.1.o0), channel_id=1, source_target_pairs={{0,8},{2,26},{8,16},{10,2},{16,24},{18,10},{24,0},{26,18},{1,9},{3... | collective-permute-start | bytes 4276232 | tf_op jit(solution)/shard_map/ppermute | solution.py:419
  10.3 29.8 %collective-permute-done.3.r1 = f32[464,768]{1,0:T(8,128)S(1)} collective-permute-done((f32[464,768]{1,0:T(8,128)S(1)}, f32[464,768]{1,0:T(8,128)S(1)}, u32[]{:S(2)}, u32[]{:S(2)}) %collective-permute-start.3) | collective-permute-done | bytes 1425440 | tf_op jit(solution)/shard_map/ppermute | solution.py:419
  40.1 3.5 %collective-permute-start.5 = (f32[464,768]{1,0:T(8,128)S(1)}, f32[464,768]{1,0:T(8,128)}, u32[]{:S(2)}, u32[]{:S(2)}) collective-permute-start(f32[464,768]{1,0:T(8,128)S(1)} %collective-permute-done.3.r1), channel_id=1, source_target_pairs={{0,8},{2,26},{8,16},{10,2},{16,24},{18,10},{24,0},{26,18},{1,9},{3... | collective-permute-start | bytes 4276232 | tf_op jit(solution)/shard_map/ppermute | solution.py:421
  43.7 1.1 copy-done.6
  45.3 1.1 copy-done.10
  46.4 13.1 %collective-permute-done.5.r3 = f32[464,768]{1,0:T(8,128)} collective-permute-done((f32[464,768]{1,0:T(8,128)S(1)}, f32[464,768]{1,0:T(8,128)}, u32[]{:S(2)}, u32[]{:S(2)}) %collective-permute-start.5) | collective-permute-done | bytes 1425440 | tf_op jit(solution)/shard_map/ppermute | solution.py:421
  59.4 2.2 collective-permute-start.8
  63.8 4.5 %collective-permute-start = (f32[64,384]{1,0:T(8,128)S(1)}, f32[64,384]{1,0:T(8,128)S(1)}, u32[]{:S(2)}, u32[]{:S(2)}) collective-permute-start(f32[64,384]{1,0:T(8,128)S(1)} %bitcast.30), channel_id=1, source_target_pairs={{0,0},{1,2},{2,1},{3,3},{4,4},{5,6},{6,5},{7,7},{8,8},{9,10},{10,9... | collective-permute-start | bytes 294920 | tf_op jit(solution)/shard_map/ppermute | solution.py:429
  68.3 2.9 %collective-permute-done = f32[64,384]{1,0:T(8,128)S(1)} collective-permute-done((f32[64,384]{1,0:T(8,128)S(1)}, f32[64,384]{1,0:T(8,128)S(1)}, u32[]{:S(2)}, u32[]{:S(2)}) %collective-permute-start) | collective-permute-done | bytes 98336 | tf_op jit(solution)/shard_map/ppermute | solution.py:429
  71.2 1.6 collective-permute-done.1
  72.9 1.3 copy-done.7
  74.3 1.4 copy-done.11
  75.6 4.1 %unpack.1 = (bf16[4,720,360]{2,1,0:T(8,128)(2,1)S(1)}, bf16[4,360,360]{2,1,0:T(8,128)(2,1)S(1)}, bf16[4,360,720]{2,1,0:T(8,128)(2,1)S(1)}, f32[4,8,768]{2,1,0:T(8,128)S(1)}) custom-call(s32[4]{0:T(128)S(1)} %pad_add_fusion.where.refs_0_, f32[464,768]{1,0:T(8,128)S(1)} %copy-done.7, f32[464,768]{1,0:T(8,128)} %collective-permute-done.2.o1, ...), custom_call_target="tpu_custom_call" | custom-call | tf_op jit(solution)/shard_map/unpack/pallas_call | solution.py:442
  79.8 3.6 %forward_light.3 = f32[192,384]{1,0:T(8,128)S(1)} custom-call(s32[4]{0:T(128)S(1)} %pad_add_fusion.where.refs_0_, f32[192,384]{1,0:T(8,128)S(1)} %broadcast_in_dim.7.refs_1_, f32[128,384]{1,0:T(8,128)S(1)} %maximum_select_fusion.refs_2_.stem_ref, bf16[4,720,360]{2,1,0:T(8,128)(2,1)S(1)} %get-tuple-element.22.refs_3_.refs_5_, ...), custom_call_target="tpu_custom_call" | custom-call | tf_op jit(solution)/shard_map/forward_light/pallas_call | solution.py:474
  83.4 1.3 collective-permute-start.9
  84.7 6.2 %collective-permute-done.9.refs_1_ = f32[192,384]{1,0:T(8,128)S(1)} collective-permute-done((f32[192,384]{1,0:T(8,128)S(1)}, f32[192,384]{1,0:T(8,128)S(1)}, u32[]{:S(2)}, u32[]{:S(2)}) %collective-permute-start.9) | collective-permute-done | bytes 294944 | tf_op jit(solution)/shard_map/ppermute | solution.py:487
  90.9 3.6 %forward_light.4 = f32[192,384]{1,0:T(8,128)S(1)} custom-call(s32[4]{0:T(128)S(1)} %pad_add_fusion.where.refs_0_, f32[192,384]{1,0:T(8,128)S(1)} %collective-permute-done.9.refs_1_, f32[128,384]{1,0:T(8,128)S(1)} %maximum_select_fusion.refs_2_.stem_ref, bf16[4,720,360]{2,1,0:T(8,128)(2,1)S(1)} %get-tuple-element.22.refs_3_.refs_5_, ...), custom_call_target="tpu_custom_call" | custom-call | tf_op jit(solution)/shard_map/forward_light/pallas_call | solution.py:474
  94.5 1.3 collective-permute-start.10
  95.8 6.2 %collective-permute-done.10.refs_1_ = f32[192,384]{1,0:T(8,128)S(1)} collective-permute-done((f32[192,384]{1,0:T(8,128)S(1)}, f32[192,384]{1,0:T(8,128)S(1)}, u32[]{:S(2)}, u32[]{:S(2)}) %collective-permute-start.10) | collective-permute-done | bytes 294944 | tf_op jit(solution)/shard_map/ppermute | solution.py:487
  101.9 4.3 %forward_light.5 = f32[192,384]{1,0:T(8,128)} custom-call(s32[4]{0:T(128)S(1)} %pad_add_fusion.where.refs_0_, f32[192,384]{1,0:T(8,128)S(1)} %collective-permute-done.10.refs_1_, f32[128,384]{1,0:T(8,128)S(1)} %maximum_select_fusion.refs_2_.stem_ref, bf16[4,720,360]{2,1,0:T(8,128)(2,1)S(1)} %get-tuple-element.22.refs_3_.refs_5_, ...), custom_call_target="tpu_custom_call" | custom-call | tf_op jit(solution)/shard_map/forward_light/pallas_call | solution.py:474
  106.3 1.3 collective-permute-start.11
  107.6 1.8 copy.32
  109.3 1.0 pad.4.cls_ref
  110.3 3.7 %collective-permute-done.11.refs_1_ = f32[192,384]{1,0:T(8,128)} collective-permute-done((f32[192,384]{1,0:T(8,128)}, f32[192,384]{1,0:T(8,128)}, u32[]{:S(2)}, u32[]{:S(2)}) %collective-permute-start.11) | collective-permute-done | bytes 294944 | tf_op jit(solution)/shard_map/ppermute | solution.py:487
  114.0 1.6 copy-done.1
  116.6 4.5 %forward_full.1 = (f32[192,384]{1,0:T(8,128)S(1)}, f32[4,128,360]{2,1,0:T(8,128)S(1)}, f32[4,128,360]{2,1,0:T(8,128)S(1)}, f32[4,32,720]{2,1,0:T(8,128)S(1)}, f3...) custom-call(s32[4]{0:T(128)S(1)} %pad_add_fusion.where.refs_0_, f32[192,384]{1,0:T(8,128)} %collective-permute-done.11.refs_1_, ...), custom_call_target="tpu_custom_call" | custom-call | tf_op jit(solution)/shard_map/forward_full/pallas_call | solution.py:474
  121.1 1.8 head.1.refs_1_.refs_2_
  122.9 3.9 %backward_light.3 = f32[192,384]{1,0:T(8,128)S(1)} custom-call(s32[4]{0:T(128)S(1)} %pad_add_fusion.where.refs_0_, f32[192,384]{1,0:T(8,128)S(1)} %head.1.refs_1_.refs_2_, f32[192,384]{1,0:T(8,128)S(1)} %head.1.refs_1_.refs_2_, f32[4,128,360]{2,1,0:T(8,128)S(1)} %get-tuple-element.29.refs_3_, f32[4,32,720]{2,1,0:T(8,128)S(1)} %get-tuple-element.30.refs_4_, ...), custom_call_target="tpu_custom_call" | custom-call | tf_op jit(solution)/shard_map/backward_light/pallas_call | solution.py:516
  126.8 2.4 collective-permute-start.18
  129.2 3.6 %collective-permute-done.18.refs_1_ = f32[192,384]{1,0:T(8,128)S(1)} collective-permute-done((f32[192,384]{1,0:T(8,128)S(1)}, f32[192,384]{1,0:T(8,128)S(1)}, u32[]{:S(2)}, u32[]{:S(2)}) %collective-permute-start.18) | collective-permute-done | bytes 294944 | tf_op jit(solution)/shard_map/ppermute | solution.py:529
  132.8 3.9 %backward_light.4 = f32[192,384]{1,0:T(8,128)S(1)} custom-call(s32[4]{0:T(128)S(1)} %pad_add_fusion.where.refs_0_, f32[192,384]{1,0:T(8,128)S(1)} %collective-permute-done.18.refs_1_, f32[192,384]{1,0:T(8,128)S(1)} %head.1.refs_1_.refs_2_, f32[4,128,360]{2,1,0:T(8,128)S(1)} %get-tuple-element.29.refs_3_, f32[4,32,720]{2,1,0:T(8,128)S(1)} %get-tuple-element.30.refs_4_, ...), custom_call_target="tpu_custom_call" | custom-call | tf_op jit(solution)/shard_map/backward_light/pallas_call | solution.py:516
  136.7 4.0 %collective-permute-start.19 = (f32[192,384]{1,0:T(8,128)S(1)}, f32[192,384]{1,0:T(8,128)S(1)}, u32[]{:S(2)}, u32[]{:S(2)}) collective-permute-start(f32[192,384]{1,0:T(8,128)S(1)} %backward_light.4), channel_id=1, source_target_pairs={{32,0},{64,32},{96,64},{33,1},{65,33},{97,65},{34,2},{66,34},{98,6... | collective-permute-start | bytes 884744 | tf_op jit(solution)/shard_map/ppermute | solution.py:529
  140.7 3.6 %collective-permute-done.19.refs_1_ = f32[192,384]{1,0:T(8,128)S(1)} collective-permute-done((f32[192,384]{1,0:T(8,128)S(1)}, f32[192,384]{1,0:T(8,128)S(1)}, u32[]{:S(2)}, u32[]{:S(2)}) %collective-permute-start.19) | collective-permute-done | bytes 294944 | tf_op jit(solution)/shard_map/ppermute | solution.py:529
  144.3 3.9 %backward_light.5 = f32[192,384]{1,0:T(8,128)S(1)} custom-call(s32[4]{0:T(128)S(1)} %pad_add_fusion.where.refs_0_, f32[192,384]{1,0:T(8,128)S(1)} %collective-permute-done.19.refs_1_, f32[192,384]{1,0:T(8,128)S(1)} %head.1.refs_1_.refs_2_, f32[4,128,360]{2,1,0:T(8,128)S(1)} %get-tuple-element.29.refs_3_, f32[4,32,720]{2,1,0:T(8,128)S(1)} %get-tuple-element.30.refs_4_, ...), custom_call_target="tpu_custom_call" | custom-call | tf_op jit(solution)/shard_map/backward_light/pallas_call | solution.py:516
  148.2 3.8 %collective-permute-start.20 = (f32[192,384]{1,0:T(8,128)S(1)}, f32[192,384]{1,0:T(8,128)S(1)}, u32[]{:S(2)}, u32[]{:S(2)}) collective-permute-start(f32[192,384]{1,0:T(8,128)S(1)} %backward_light.5), channel_id=1, source_target_pairs={{32,0},{64,32},{96,64},{33,1},{65,33},{97,65},{34,2},{66,34},{98,6... | collective-permute-start | bytes 884744 | tf_op jit(solution)/shard_map/ppermute | solution.py:529
  152.0 4.5 %collective-permute-done.20.refs_1_ = f32[192,384]{1,0:T(8,128)S(1)} collective-permute-done((f32[192,384]{1,0:T(8,128)S(1)}, f32[192,384]{1,0:T(8,128)S(1)}, u32[]{:S(2)}, u32[]{:S(2)}) %collective-permute-start.20) | collective-permute-done | bytes 294944 | tf_op jit(solution)/shard_map/ppermute | solution.py:529
  156.5 5.3 %backward_full.1 = (f32[192,384]{1,0:T(8,128)}, f32[4,240,384]{2,1,0:T(8,128)S(1)}, f32[4,120,384]{2,1,0:T(8,128)S(1)}, f32[64,384]{1,0:T(8,128)S(1)}) custom-call(s32[4]{0:T(128)S(1)} %pad_add_fusion.where.refs_0_, f32[192,384]{1,0:T(8,128)S(1)} %collective-permute-done.20.refs_1_, f32[192,384]{1,0:T(8,128)S(1)} %head.1.refs_1_.refs_2_, ...), custom_call_target="tpu_custom_call" | custom-call | tf_op jit(solution)/shard_map/backward_full/pallas_call | solution.py:516
  161.8 1.1 copy-done.8
  162.9 11.2 %collective-permute-start.21 = (f32[4,120,384]{2,1,0:T(8,128)S(1)}, f32[4,120,384]{2,1,0:T(8,128)S(1)}, u32[]{:S(2)}, u32[]{:S(2)}) collective-permute-start(f32[4,120,384]{2,1,0:T(8,128)S(1)} %get-tuple-element.33), channel_id=1, source_target_pairs={{0,4},{2,7},{4,1},{6,2},{1,5},{3,6},{5,0},{7,3},{8,12},{10,15},{12... | collective-permute-start | bytes 2211848 | tf_op jit(solution)/shard_map/ppermute | solution.py:419
  174.1 1.4 collective-permute-start.22
  175.5 9.3 %collective-permute-done.21.r1 = f32[4,120,384]{2,1,0:T(8,128)S(1)} collective-permute-done((f32[4,120,384]{2,1,0:T(8,128)S(1)}, f32[4,120,384]{2,1,0:T(8,128)S(1)}, u32[]{:S(2)}, u32[]{:S(2)}) %collective-permute-start.21) | collective-permute-done | bytes 737312 | tf_op jit(solution)/shard_map/ppermute | solution.py:419
  184.9 3.4 %collective-permute-start.23 = (f32[4,120,384]{2,1,0:T(8,128)S(1)}, f32[4,120,384]{2,1,0:T(8,128)S(1)}, u32[]{:S(2)}, u32[]{:S(2)}) collective-permute-start(f32[4,120,384]{2,1,0:T(8,128)S(1)} %collective-permute-done.21.r1), channel_id=1, source_target_pairs={{0,4},{2,7},{4,1},{6,2},{1,5},{3,6},{5,0},{7,3},{8,12},{10,15},{12... | collective-permute-start | bytes 2211848 | tf_op jit(solution)/shard_map/ppermute | solution.py:421
  188.3 9.5 %collective-permute-done.12.l1 = f32[4,112,384]{2,1,0:T(8,128)S(1)} collective-permute-done((f32[4,112,384]{2,1,0:T(8,128)S(1)}, f32[4,112,384]{2,1,0:T(8,128)S(1)}, u32[]{:S(2)}, u32[]{:S(2)}) %collective-permute-start.12) | collective-permute-done | bytes 688160 | tf_op jit(solution)/shard_map/ppermute | solution.py:419
  197.8 3.1 %collective-permute-start.14 = (f32[4,112,384]{2,1,0:T(8,128)S(1)}, f32[4,112,384]{2,1,0:T(8,128)}, u32[]{:S(2)}, u32[]{:S(2)}) collective-permute-start(f32[4,112,384]{2,1,0:T(8,128)S(1)} %collective-permute-done.12.l1), channel_id=1, source_target_pairs={{0,4},{2,7},{4,1},{6,2},{1,5},{3,6},{5,0},{7,3},{8,12},{10,15},{12... | collective-permute-start | bytes 2064392 | tf_op jit(solution)/shard_map/ppermute | solution.py:421
  200.9 8.1 %collective-permute-start.15 = (f32[4,112,384]{2,1,0:T(8,128)S(1)}, f32[4,112,384]{2,1,0:T(8,128)S(1)}, u32[]{:S(2)}, u32[]{:S(2)}) collective-permute-start(f32[4,112,384]{2,1,0:T(8,128)S(1)} %collective-permute-done.12.l1), channel_id=1, source_target_pairs={{0,2},{2,0},{1,3},{3,1},{4,6},{6,4},{5,7},{7,5},{8,10},{10,8},{9,1... | collective-permute-start | bytes 2064392 | tf_op jit(solution)/shard_map/ppermute | solution.py:416
  209.9 5.0 %collective-permute-start.24 = (f32[4,120,384]{2,1,0:T(8,128)S(1)}, f32[4,120,384]{2,1,0:T(8,128)S(1)}, u32[]{:S(2)}, u32[]{:S(2)}) collective-permute-start(f32[4,120,384]{2,1,0:T(8,128)S(1)} %collective-permute-done.21.r1), channel_id=1, source_target_pairs={{0,2},{2,0},{1,3},{3,1},{4,6},{6,4},{5,7},{7,5},{8,10},{10,8},{9,1... | collective-permute-start | bytes 2211848 | tf_op jit(solution)/shard_map/ppermute | solution.py:416
  214.9 1.9 collective-permute-start.26
  216.9 3.5 %collective-permute-done.14.l3 = f32[4,112,384]{2,1,0:T(8,128)} collective-permute-done((f32[4,112,384]{2,1,0:T(8,128)S(1)}, f32[4,112,384]{2,1,0:T(8,128)}, u32[]{:S(2)}, u32[]{:S(2)}) %collective-permute-start.14) | collective-permute-done | bytes 688160 | tf_op jit(solution)/shard_map/ppermute | solution.py:421
  220.4 3.9 %collective-permute-start.16 = (f32[4,112,384]{2,1,0:T(8,128)}, f32[4,112,384]{2,1,0:T(8,128)}, u32[]{:S(2)}, u32[]{:S(2)}) collective-permute-start(f32[4,112,384]{2,1,0:T(8,128)} %collective-permute-done.13.l2), channel_id=1, source_target_pairs={{0,2},{2,0},{1,3},{3,1},{4,6},{6,4},{5,7},{7,5},{8,10},{10,8},{9,1... | collective-permute-start | bytes 2064392 | tf_op jit(solution)/shard_map/ppermute | solution.py:416
  225.5 1.0 collective-permute-done.16.m2
  226.5 1.3 collective-permute-done.17.m3
  227.8 1.4 copy-done.9
  229.2 1.3 copy-done.13
  230.5 1.1 copy-done.16
  231.6 1.1 copy-done.18
  232.7 5.8 %weight_grads.1 = f32[4,256,384]{2,1,0:T(8,128)S(1)} custom-call(s32[8]{0:T(128)S(1)} %concatenate.14.where, f32[4,224,384]{2,1,0:T(8,128)S(1)} %copy-done.13, f32[4,112,384]{2,1,0:T(8,128)S(1)} %copy-done.16, f32[4,112,384]{2,1,0:T(8,128)} %collective-permute-done.13.l2, f32[4,112,384]{2,1,0:T(8,128)} %collective-permute-done.14.l3, ...), custom_call_target="tpu_custom_call" | custom-call | tf_op jit(solution)/shard_map/weight_grads/pallas_call | solution.py:539
  238.6 1.4 collective-permute-start.27
  240.1 9.0 %collective-permute-done.27 = f32[256,384]{1,0:T(8,128)S(1)} collective-permute-done((f32[256,384]{1,0:T(8,128)S(1)}, f32[256,384]{1,0:T(8,128)S(1)}, u32[]{:S(2)}, u32[]{:S(2)}) %collective-permute-start.27) | collective-permute-done | bytes 393248 | tf_op jit(solution)/shard_map/ppermute | solution.py:555
  249.2 1.0 collective-permute-start.28
  250.3 10.4 %all_to_all.5 = f32[16,4,384]{2,1,0:T(4,128)S(1)} all-to-all(f32[16,4,384]{2,1,0:T(4,128)S(1)} %bitcast.28), channel_id=1, replica_groups=mesh['y'=4,'z'=4,'xl'=2,'core'=2,'xh'=2] {'y','z'}, dimensions={0} | all-to-all | bytes 196608 | tf_op jit(solution)/shard_map/all_to_all | solution.py:568
  260.8 7.3 %collective-permute-start.30 = (f32[4,4,384]{2,0,1:T(4,128)S(1)}, f32[4,4,384]{2,0,1:T(4,128)S(1)}, u32[]{:S(2)}, u32[]{:S(2)}) collective-permute-start(f32[4,4,384]{2,0,1:T(4,128)S(1)} %copy.40), channel_id=1, source_target_pairs={{0,0},{1,2},{2,1},{3,3},{4,4},{5,6},{6,5},{7,7},{8,8},{9,10},{10,9... | collective-permute-start | bytes 73736 | tf_op jit(solution)/shard_map/ppermute | solution.py:570
  268.1 1.5 collective-permute-done.30
  (90 shorter events, 13.3 us)
Async XLA Ops:
  0.7 1.1 copy-start.19
  1.8 1.1 copy-start.20
  2.8 1.0 copy-start.22
  3.8 0.7 copy-start.23
  4.5 0.7 copy-start.24
  5.2 0.7 copy-start.25
  6.5 33.6 %collective-permute-start.3 = (f32[464,768]{1,0:T(8,128)S(1)}, f32[464,768]{1,0:T(8,128)S(1)}, u32[]{:S(2)}, u32[]{:S(2)}) collective-permute-start(f32[464,768]{1,0:T(8,128)S(1)} %pack.1.o0), channel_id=1, source_target_pairs={{0,8},{2,26},{8,16},{10,2},{16,24},{18,10},{24,0},{26,18},{1,9},{3... | collective-permute-start | bytes 4276232 | tf_op jit(solution)/shard_map/ppermute | solution.py:419
  10.3 36.0 %collective-permute-start.4 = (f32[464,768]{1,0:T(8,128)S(1)}, f32[464,768]{1,0:T(8,128)}, u32[]{:S(2)}, u32[]{:S(2)}) collective-permute-start(f32[464,768]{1,0:T(8,128)S(1)} %pack.1.o0), channel_id=1, source_target_pairs={{0,24},{2,10},{8,0},{10,18},{16,8},{18,26},{24,16},{26,2},{1,25},{... | collective-permute-start | bytes 4276232 | tf_op jit(solution)/shard_map/ppermute | solution.py:420
  40.1 19.3 %collective-permute-start.5 = (f32[464,768]{1,0:T(8,128)S(1)}, f32[464,768]{1,0:T(8,128)}, u32[]{:S(2)}, u32[]{:S(2)}) collective-permute-start(f32[464,768]{1,0:T(8,128)S(1)} %collective-permute-done.3.r1), channel_id=1, source_target_pairs={{0,8},{2,26},{8,16},{10,2},{16,24},{18,10},{24,0},{26,18},{1,9},{3... | collective-permute-start | bytes 4276232 | tf_op jit(solution)/shard_map/ppermute | solution.py:421
  43.7 29.2 %collective-permute-start.2 = (f32[464,768]{1,0:T(8,128)S(1)}, f32[464,768]{1,0:T(8,128)}, u32[]{:S(2)}, u32[]{:S(2)}) collective-permute-start(f32[464,768]{1,0:T(8,128)S(1)} %pack.1.o0), channel_id=1, source_target_pairs={{0,2},{2,0},{1,3},{3,1},{4,6},{6,4},{5,7},{7,5},{8,10},{10,8},{9,1... | collective-permute-start | bytes 4276232 | tf_op jit(solution)/shard_map/ppermute | solution.py:416
  43.7 1.1 copy-start.6
  44.8 28.1 %collective-permute-start.6 = (f32[464,768]{1,0:T(8,128)S(1)}, f32[464,768]{1,0:T(8,128)}, u32[]{:S(2)}, u32[]{:S(2)}) collective-permute-start(f32[464,768]{1,0:T(8,128)S(1)} %collective-permute-done.3.r1), channel_id=1, source_target_pairs={{0,2},{2,0},{1,3},{3,1},{4,6},{6,4},{5,7},{7,5},{8,10},{10,8},{9,1... | collective-permute-start | bytes 4276232 | tf_op jit(solution)/shard_map/ppermute | solution.py:416
  45.3 1.1 copy-start.10
  46.4 26.5 %collective-permute-start.7 = (f32[464,768]{1,0:T(8,128)}, f32[464,768]{1,0:T(8,128)}, u32[]{:S(2)}, u32[]{:S(2)}) collective-permute-start(f32[464,768]{1,0:T(8,128)} %collective-permute-done.4.r2), channel_id=1, source_target_pairs={{0,2},{2,0},{1,3},{3,1},{4,6},{6,4},{5,7},{7,5},{8,10},{10,8},{9,1... | collective-permute-start | bytes 4276232 | tf_op jit(solution)/shard_map/ppermute | solution.py:416
  59.4 13.5 %collective-permute-start.8 = (f32[464,768]{1,0:T(8,128)}, f32[464,768]{1,0:T(8,128)}, u32[]{:S(2)}, u32[]{:S(2)}) collective-permute-start(f32[464,768]{1,0:T(8,128)} %collective-permute-done.5.r3), channel_id=1, source_target_pairs={{0,2},{2,0},{1,3},{3,1},{4,6},{6,4},{5,7},{7,5},{8,10},{10,8},{9,1... | collective-permute-start | bytes 4276232 | tf_op jit(solution)/shard_map/ppermute | solution.py:416
  63.8 7.4 %collective-permute-start = (f32[64,384]{1,0:T(8,128)S(1)}, f32[64,384]{1,0:T(8,128)S(1)}, u32[]{:S(2)}, u32[]{:S(2)}) collective-permute-start(f32[64,384]{1,0:T(8,128)S(1)} %bitcast.30), channel_id=1, source_target_pairs={{0,0},{1,2},{2,1},{3,3},{4,4},{5,6},{6,5},{7,7},{8,8},{9,10},{10,9... | collective-permute-start | bytes 294920 | tf_op jit(solution)/shard_map/ppermute | solution.py:429
  71.2 1.6 collective-permute-start.1
  72.9 1.4 copy-start.7
  74.3 1.4 copy-start.11
  79.7 22.2 %copy-start = (bf16[4,360,720]{2,1,0:T(8,128)(2,1)}, bf16[4,360,720]{2,1,0:T(8,128)(2,1)S(1)}, u32[]{:S(2)}) copy-start(bf16[4,360,720]{2,1,0:T(8,128)(2,1)S(1)} %get-tuple-element.24.refs_5_.refs_7_) | copy-start | bytes 6220804
  79.7 22.2 %copy-start.3 = (f32[4,8,768]{2,1,0:T(8,128)}, f32[4,8,768]{2,1,0:T(8,128)S(1)}, u32[]{:S(2)}) copy-start(f32[4,8,768]{2,1,0:T(8,128)S(1)} %get-tuple-element.25.refs_6_.refs_8_) | copy-start | bytes 294916
  83.4 7.5 %collective-permute-start.9 = (f32[192,384]{1,0:T(8,128)S(1)}, f32[192,384]{1,0:T(8,128)S(1)}, u32[]{:S(2)}, u32[]{:S(2)}) collective-permute-start(f32[192,384]{1,0:T(8,128)S(1)} %forward_light.3), channel_id=1, source_target_pairs={{0,32},{32,64},{64,96},{1,33},{33,65},{65,97},{2,34},{34,66},{66,9... | collective-permute-start | bytes 884744 | tf_op jit(solution)/shard_map/ppermute | solution.py:487
  94.5 7.5 %collective-permute-start.10 = (f32[192,384]{1,0:T(8,128)S(1)}, f32[192,384]{1,0:T(8,128)S(1)}, u32[]{:S(2)}, u32[]{:S(2)}) collective-permute-start(f32[192,384]{1,0:T(8,128)S(1)} %forward_light.4), channel_id=1, source_target_pairs={{0,32},{32,64},{64,96},{1,33},{33,65},{65,97},{2,34},{34,66},{66,9... | collective-permute-start | bytes 884744 | tf_op jit(solution)/shard_map/ppermute | solution.py:487
  106.3 7.8 %collective-permute-start.11 = (f32[192,384]{1,0:T(8,128)}, f32[192,384]{1,0:T(8,128)}, u32[]{:S(2)}, u32[]{:S(2)}) collective-permute-start(f32[192,384]{1,0:T(8,128)} %forward_light.5), channel_id=1, source_target_pairs={{0,32},{32,64},{64,96},{1,33},{33,65},{65,97},{2,34},{34,66},{66,9... | collective-permute-start | bytes 884744 | tf_op jit(solution)/shard_map/ppermute | solution.py:487
  114.0 1.6 copy-start.1
  115.7 0.9 copy-start.4
  116.6 4.5 %copy-start.14 = (bf16[720,512]{1,0:T(8,128)(2,1)S(1)}, bf16[720,512]{1,0:T(8,128)(2,1)}, u32[]{:S(2)}) copy-start(bf16[720,512]{1,0:T(8,128)(2,1)} %two_ref.1) | copy-start | bytes 2211844
  116.6 4.5 %copy-start.21 = (bf16[360,512]{1,0:T(8,128)(2,1)S(1)}, bf16[360,512]{1,0:T(8,128)(2,1)}, u32[]{:S(2)}) copy-start(bf16[360,512]{1,0:T(8,128)(2,1)} %one_ref.1) | copy-start | bytes 1105924
  116.6 6.4 %copy-start.2 = (bf16[4,360,720]{2,1,0:T(8,128)(2,1)S(1)}, bf16[4,360,720]{2,1,0:T(8,128)(2,1)}, u32[]{:S(2)}) copy-start(bf16[4,360,720]{2,1,0:T(8,128)(2,1)} %copy-done) | copy-start | bytes 6220804
  121.1 5.7 %copy-start.12 = (f32[4,224,384]{2,1,0:T(8,128)}, f32[4,224,384]{2,1,0:T(8,128)S(1)}, u32[]{:S(2)}) copy-start(f32[4,224,384]{2,1,0:T(8,128)S(1)} %get-tuple-element.26.lo) | copy-start | bytes 4128772
  126.8 6.0 %collective-permute-start.18 = (f32[192,384]{1,0:T(8,128)S(1)}, f32[192,384]{1,0:T(8,128)S(1)}, u32[]{:S(2)}, u32[]{:S(2)}) collective-permute-start(f32[192,384]{1,0:T(8,128)S(1)} %backward_light.3), channel_id=1, source_target_pairs={{32,0},{64,32},{96,64},{33,1},{65,33},{97,65},{34,2},{66,34},{98,6... | collective-permute-start | bytes 884744 | tf_op jit(solution)/shard_map/ppermute | solution.py:529
  136.7 19.8 %copy-start.5 = (f32[4,8,768]{2,1,0:T(8,128)S(1)}, f32[4,8,768]{2,1,0:T(8,128)}, u32[]{:S(2)}) copy-start(f32[4,8,768]{2,1,0:T(8,128)} %copy-done.3) | copy-start | bytes 294916
  136.7 7.6 %collective-permute-start.19 = (f32[192,384]{1,0:T(8,128)S(1)}, f32[192,384]{1,0:T(8,128)S(1)}, u32[]{:S(2)}, u32[]{:S(2)}) collective-permute-start(f32[192,384]{1,0:T(8,128)S(1)} %backward_light.4), channel_id=1, source_target_pairs={{32,0},{64,32},{96,64},{33,1},{65,33},{97,65},{34,2},{66,34},{98,6... | collective-permute-start | bytes 884744 | tf_op jit(solution)/shard_map/ppermute | solution.py:529
  148.2 8.3 %collective-permute-start.20 = (f32[192,384]{1,0:T(8,128)S(1)}, f32[192,384]{1,0:T(8,128)S(1)}, u32[]{:S(2)}, u32[]{:S(2)}) collective-permute-start(f32[192,384]{1,0:T(8,128)S(1)} %backward_light.5), channel_id=1, source_target_pairs={{32,0},{64,32},{96,64},{33,1},{65,33},{97,65},{34,2},{66,34},{98,6... | collective-permute-start | bytes 884744 | tf_op jit(solution)/shard_map/ppermute | solution.py:529
  161.8 1.1 copy-start.8
  162.9 21.9 %collective-permute-start.21 = (f32[4,120,384]{2,1,0:T(8,128)S(1)}, f32[4,120,384]{2,1,0:T(8,128)S(1)}, u32[]{:S(2)}, u32[]{:S(2)}) collective-permute-start(f32[4,120,384]{2,1,0:T(8,128)S(1)} %get-tuple-element.33), channel_id=1, source_target_pairs={{0,4},{2,7},{4,1},{6,2},{1,5},{3,6},{5,0},{7,3},{8,12},{10,15},{12... | collective-permute-start | bytes 2211848 | tf_op jit(solution)/shard_map/ppermute | solution.py:419
  174.1 23.7 %collective-permute-start.12 = (f32[4,112,384]{2,1,0:T(8,128)S(1)}, f32[4,112,384]{2,1,0:T(8,128)S(1)}, u32[]{:S(2)}, u32[]{:S(2)}) collective-permute-start(f32[4,112,384]{2,1,0:T(8,128)S(1)} %get-tuple-element.27), channel_id=1, source_target_pairs={{0,4},{2,7},{4,1},{6,2},{1,5},{3,6},{5,0},{7,3},{8,12},{10,15},{12... | collective-permute-start | bytes 2064392 | tf_op jit(solution)/shard_map/ppermute | solution.py:419
  174.1 40.8 %collective-permute-start.22 = (f32[4,120,384]{2,1,0:T(8,128)S(1)}, f32[4,120,384]{2,1,0:T(8,128)S(1)}, u32[]{:S(2)}, u32[]{:S(2)}) collective-permute-start(f32[4,120,384]{2,1,0:T(8,128)S(1)} %get-tuple-element.33), channel_id=1, source_target_pairs={{0,5},{2,6},{4,0},{6,3},{1,4},{3,7},{5,1},{7,2},{8,13},{10,14},{12... | collective-permute-start | bytes 2211848 | tf_op jit(solution)/shard_map/ppermute | solution.py:420
  184.9 30.1 %collective-permute-start.23 = (f32[4,120,384]{2,1,0:T(8,128)S(1)}, f32[4,120,384]{2,1,0:T(8,128)S(1)}, u32[]{:S(2)}, u32[]{:S(2)}) collective-permute-start(f32[4,120,384]{2,1,0:T(8,128)S(1)} %collective-permute-done.21.r1), channel_id=1, source_target_pairs={{0,4},{2,7},{4,1},{6,2},{1,5},{3,6},{5,0},{7,3},{8,12},{10,15},{12... | collective-permute-start | bytes 2211848 | tf_op jit(solution)/shard_map/ppermute | solution.py:421
  188.3 21.6 %collective-permute-start.13 = (f32[4,112,384]{2,1,0:T(8,128)S(1)}, f32[4,112,384]{2,1,0:T(8,128)}, u32[]{:S(2)}, u32[]{:S(2)}) collective-permute-start(f32[4,112,384]{2,1,0:T(8,128)S(1)} %get-tuple-element.27), channel_id=1, source_target_pairs={{0,5},{2,6},{4,0},{6,3},{1,4},{3,7},{5,1},{7,2},{8,13},{10,14},{12... | collective-permute-start | bytes 2064392 | tf_op jit(solution)/shard_map/ppermute | solution.py:420
  197.8 22.6 %collective-permute-start.14 = (f32[4,112,384]{2,1,0:T(8,128)S(1)}, f32[4,112,384]{2,1,0:T(8,128)}, u32[]{:S(2)}, u32[]{:S(2)}) collective-permute-start(f32[4,112,384]{2,1,0:T(8,128)S(1)} %collective-permute-done.12.l1), channel_id=1, source_target_pairs={{0,4},{2,7},{4,1},{6,2},{1,5},{3,6},{5,0},{7,3},{8,12},{10,15},{12... | collective-permute-start | bytes 2064392 | tf_op jit(solution)/shard_map/ppermute | solution.py:421
  200.9 23.5 %collective-permute-start.15 = (f32[4,112,384]{2,1,0:T(8,128)S(1)}, f32[4,112,384]{2,1,0:T(8,128)S(1)}, u32[]{:S(2)}, u32[]{:S(2)}) collective-permute-start(f32[4,112,384]{2,1,0:T(8,128)S(1)} %collective-permute-done.12.l1), channel_id=1, source_target_pairs={{0,2},{2,0},{1,3},{3,1},{4,6},{6,4},{5,7},{7,5},{8,10},{10,8},{9,1... | collective-permute-start | bytes 2064392 | tf_op jit(solution)/shard_map/ppermute | solution.py:416
  209.0 0.9 copy-start.15
  209.9 17.9 %collective-permute-start.24 = (f32[4,120,384]{2,1,0:T(8,128)S(1)}, f32[4,120,384]{2,1,0:T(8,128)S(1)}, u32[]{:S(2)}, u32[]{:S(2)}) collective-permute-start(f32[4,120,384]{2,1,0:T(8,128)S(1)} %collective-permute-done.21.r1), channel_id=1, source_target_pairs={{0,2},{2,0},{1,3},{3,1},{4,6},{6,4},{5,7},{7,5},{8,10},{10,8},{9,1... | collective-permute-start | bytes 2211848 | tf_op jit(solution)/shard_map/ppermute | solution.py:416
  214.9 12.9 %collective-permute-start.25 = (f32[4,120,384]{2,1,0:T(8,128)S(1)}, f32[4,120,384]{2,1,0:T(8,128)}, u32[]{:S(2)}, u32[]{:S(2)}) collective-permute-start(f32[4,120,384]{2,1,0:T(8,128)S(1)} %collective-permute-done.22.r2), channel_id=1, source_target_pairs={{0,2},{2,0},{1,3},{3,1},{4,6},{6,4},{5,7},{7,5},{8,10},{10,8},{9,1... | collective-permute-start | bytes 2211848 | tf_op jit(solution)/shard_map/ppermute | solution.py:416
  214.9 12.9 %collective-permute-start.26 = (f32[4,120,384]{2,1,0:T(8,128)S(1)}, f32[4,120,384]{2,1,0:T(8,128)}, u32[]{:S(2)}, u32[]{:S(2)}) collective-permute-start(f32[4,120,384]{2,1,0:T(8,128)S(1)} %collective-permute-done.23.r3), channel_id=1, source_target_pairs={{0,2},{2,0},{1,3},{3,1},{4,6},{6,4},{5,7},{7,5},{8,10},{10,8},{9,1... | collective-permute-start | bytes 2211848 | tf_op jit(solution)/shard_map/ppermute | solution.py:416
  220.4 6.1 %collective-permute-start.16 = (f32[4,112,384]{2,1,0:T(8,128)}, f32[4,112,384]{2,1,0:T(8,128)}, u32[]{:S(2)}, u32[]{:S(2)}) collective-permute-start(f32[4,112,384]{2,1,0:T(8,128)} %collective-permute-done.13.l2), channel_id=1, source_target_pairs={{0,2},{2,0},{1,3},{3,1},{4,6},{6,4},{5,7},{7,5},{8,10},{10,8},{9,1... | collective-permute-start | bytes 2064392 | tf_op jit(solution)/shard_map/ppermute | solution.py:416
  224.4 0.9 copy-start.17
  225.3 2.5 collective-permute-start.17
  227.8 1.4 copy-start.9
  229.2 1.3 copy-start.13
  230.5 1.1 copy-start.16
  231.6 1.1 copy-start.18
  238.6 10.6 %collective-permute-start.27 = (f32[256,384]{1,0:T(8,128)S(1)}, f32[256,384]{1,0:T(8,128)S(1)}, u32[]{:S(2)}, u32[]{:S(2)}) collective-permute-start(f32[256,384]{1,0:T(8,128)S(1)} %get-tuple-element.55), channel_id=1, source_target_pairs={{0,8},{2,26},{8,16},{10,2},{16,24},{18,10},{24,0},{26,18},{1,9},{3... | collective-permute-start | bytes 1179656 | tf_op jit(solution)/shard_map/ppermute | solution.py:555
  240.1 30.2 %collective-permute-start.29 = (f32[256,384]{1,0:T(8,128)S(1)}, f32[256,384]{1,0:T(8,128)S(1)}, u32[]{:S(2)}, u32[]{:S(2)}) collective-permute-start(f32[256,384]{1,0:T(8,128)S(1)} %get-tuple-element.54), channel_id=1, source_target_pairs={{0,24},{2,10},{8,0},{10,18},{16,8},{18,26},{24,16},{26,2},{1,25},{... | collective-permute-start | bytes 1179656 | tf_op jit(solution)/shard_map/ppermute | solution.py:556
  249.2 21.0 %collective-permute-start.28 = (f32[256,384]{1,0:T(8,128)S(1)}, f32[256,384]{1,0:T(8,128)S(1)}, u32[]{:S(2)}, u32[]{:S(2)}) collective-permute-start(f32[256,384]{1,0:T(8,128)S(1)} %fusion), channel_id=1, source_target_pairs={{0,8},{2,26},{8,16},{10,2},{16,24},{18,10},{24,0},{26,18},{1,9},{3... | collective-permute-start | bytes 1179656 | tf_op jit(solution)/shard_map/ppermute | solution.py:557
  260.8 8.8 %collective-permute-start.30 = (f32[4,4,384]{2,0,1:T(4,128)S(1)}, f32[4,4,384]{2,0,1:T(4,128)S(1)}, u32[]{:S(2)}, u32[]{:S(2)}) collective-permute-start(f32[4,4,384]{2,0,1:T(4,128)S(1)} %copy.40), channel_id=1, source_target_pairs={{0,0},{1,2},{2,1},{3,3},{4,4},{5,6},{6,5},{7,7},{8,8},{9,10},{10,9... | collective-permute-start | bytes 73736 | tf_op jit(solution)/shard_map/ppermute | solution.py:570

commit v2 on v1

v2 whole, which is shorter than its diff:
```python
import jax
import jax.numpy as jnp
from jax import lax
from jax.experimental import pallas as pl
from jax.experimental.pallas import tpu as pltpu
from jax.sharding import Mesh, PartitionSpec as P

loss_scale = 64.0
root_coef = 0.7978845608028654
cube_coef = 0.044715

C1 = 360
C2 = 720
PAD1 = 384
HEAD = 512
CLASSES = 150
F32 = jnp.float32
BF16 = jnp.bfloat16
VMEM_LIMIT = 16 * 2**20

WROWS = 464
QROWS = 64
AROWS = WROWS - 4 * QROWS
LROWS = 224
RROWS = 240
GROWS = 256


def params():
    return pltpu.CompilerParams(vmem_limit_bytes=VMEM_LIMIT)


def gelu_pair(values):
    inner = root_coef * (values + cube_coef * values * values * values)
    tangent = jnp.tanh(inner)
    result = 0.5 * values * (1.0 + tangent)
    slope = 0.5 * (1.0 + tangent) + 0.5 * values * (1.0 - tangent * tangent) * root_coef * (
        1.0 + 3.0 * cube_coef * values * values
    )
    return result, slope


def gelu_only(values):
    inner = root_coef * (values + cube_coef * values * values * values)
    return 0.5 * values * (1.0 + jnp.tanh(inner))


def dot(left, right):
    return jnp.dot(left, right, preferred_element_type=F32)


def dot_nt(left, right):
    return lax.dot_general(left, right, (((1,), (1,)), ((), ())), preferred_element_type=F32)


def dot_tn(left, right):
    return lax.dot_general(left, right, (((0,), (0,)), ((), ())), preferred_element_type=F32)


def shifted(even, odd):
    spot = lax.broadcasted_iota(jnp.int32, even.shape, 0)
    after = jnp.where(spot == 15, 0.0, pltpu.roll(even, 15, 0))
    before = jnp.where(spot == 0, 0.0, pltpu.roll(odd, 1, 0))
    return after, before


def neighbours(blocks):
    rows = []
    for r in range(4):
        even, odd = blocks[2 * r], blocks[2 * r + 1]
        after, before = shifted(even, odd)
        rows.append(((before, even, odd), (even, odd, after)))
    return rows


def stencil(rows, taps):
    out = []
    for r in range(4):
        for b in range(2):
            total = None
            for i in (-1, 0, 1):
                if 0 <= r + i < 4:
                    for j in range(3):
                        term = taps[3 * (i + 1) + j] * rows[r + i][b][j]
                        total = term if total is None else total + term
            out.append(total)
    return out


def tap_sums(rows, grads):
    sums = []
    for i in (-1, 0, 1):
        for j in range(3):
            total = None
            for r in range(4):
                if 0 <= r + i < 4:
                    for b in range(2):
                        term = rows[r + i][b][j] * grads[2 * r + b]
                        total = term if total is None else total + term
            sums.append(jnp.sum(total, axis=0, keepdims=True))
    return sums


def pool(blocks):
    parts = [blocks[4 * q] + blocks[4 * q + 1] + blocks[4 * q + 2] + blocks[4 * q + 3] for q in range(2)]
    return jnp.concatenate(parts, axis=0)


def split(values):
    return [values[16 * q : 16 * q + 16] for q in range(8)]


def join(blocks):
    return jnp.concatenate(blocks, axis=0)


def up2(values):
    return [values[16 * (q // 4) : 16 * (q // 4) + 16] for q in range(8)]


def decode_aux(aux):
    taps = [aux[t : t + 1, 0:C1] for t in range(8)] + [aux[0:1, PAD1 : PAD1 + C1]]
    gain1 = aux[1:2, PAD1 : PAD1 + C1]
    gain2 = jnp.concatenate([aux[2:3, PAD1 : 2 * PAD1], aux[3:4, PAD1:C2]], axis=1)
    return taps, gain1, gain2


def put(ref, row, values):
    width = values.shape[1]
    if width < PAD1:
        values = jnp.concatenate([values, jnp.zeros((values.shape[0], PAD1 - width), F32)], axis=1)
    ref[row : row + values.shape[0], :] = values


def put_two(ref, row, values):
    put(ref, row, values[:, 0:PAD1])
    put(ref, row + values.shape[0], values[:, PAD1:C2])


def get_two(ref, row):
    return jnp.concatenate([ref[row : row + 32, :], ref[row + 32 : row + 64, 0 : C2 - PAD1]], axis=1)


def pack_kernel(where, up_hbm, mix_hbm, down_hbm, tap_hbm, g1_hbm, g2_hbm, out_ref, straight_ref, quarter_ref, up_ref, mix_ref, down_ref, tap_ref, g1_ref, g2_ref, sems):
    core = where[2]
    pairs = (
        (up_hbm, up_ref), (mix_hbm, mix_ref), (down_hbm, down_ref), (tap_hbm, tap_ref), (g1_hbm, g1_ref), (g2_hbm, g2_ref)
    )
    copies = [pltpu.make_async_copy(src, dst, sems.at[at]) for at, (src, dst) in enumerate(pairs)]
    for copy in copies:
        copy.start()
    for copy in copies:
        copy.wait()
    mix = mix_ref[0].astype(F32)

    @pl.when(core == 0)
    def _():
        up = up_ref[0].astype(F32)
        out_ref[0:368, 0:C1] = up[0:368]
        out_ref[0:352, PAD1 : PAD1 + C1] = up[368:720]
        out_ref[368:464, 0:C1] = mix[0:96]
        out_ref[368:464, PAD1 : PAD1 + C1] = mix[96:192]

    @pl.when(core == 1)
    def _():
        down = down_ref[0].astype(F32)
        taps = tap_ref[0].astype(F32)
        out_ref[0:360, 0:C2] = down
        out_ref[360:368, 0:C1] = taps[0:8]
        out_ref[360:361, PAD1 : PAD1 + C1] = taps[8:9]
        out_ref[361:362, PAD1 : PAD1 + C1] = g1_ref[...]
        out_ref[362:363, PAD1 : 2 * PAD1] = g2_ref[:, 0:PAD1]
        out_ref[363:364, PAD1:C2] = g2_ref[:, PAD1:C2]
        out_ref[368:464, 0:C1] = mix[192:288]
        out_ref[368:440, PAD1 : PAD1 + C1] = mix[288:360]

    straight_ref[...] = out_ref[0:AROWS, :]
    quarter_ref[...] = out_ref[pl.ds(pl.multiple_of(AROWS + where[3] * QROWS, 8), QROWS), :]


def write_column(first, second, at, up_ref, mix_ref, down_ref, aux_ref):
    up = jnp.concatenate([first[0:368, 0:C1], first[0:352, PAD1 : PAD1 + C1]], axis=0)
    up_ref[at] = up.astype(BF16)
    mix = jnp.concatenate(
        [
            first[368:464, 0:C1],
            first[368:464, PAD1 : PAD1 + C1],
            second[368:464, 0:C1],
            second[368:440, PAD1 : PAD1 + C1],
        ],
        axis=0,
    )
    mix_ref[at] = mix.astype(BF16)
    down_ref[at] = second[0:360, 0:C2].astype(BF16)
    aux_ref[at] = second[360:368, :]


def join_kernel(first, second, third, out_ref):
    for at, ref in enumerate((first, second, third)):
        out_ref[QROWS * at : QROWS * at + QROWS, :] = ref[...]


def add_kernel(first, second, out_ref):
    out_ref[...] = first[...] + second[...]


def own_kernel(where, half, mate, *refs):
    outs, parts, sems = refs[0:4], refs[4:8], refs[8]

    @pl.when(where[2] == 0)
    def _():
        write_column(half, mate, 0, *parts)

    @pl.when(where[2] == 1)
    def _():
        write_column(mate, half, 0, *parts)

    copies = [pltpu.make_async_copy(parts[k].at[0], outs[k].at[where[1]], sems.at[k]) for k in range(4)]
    for copy in copies:
        copy.start()
    for copy in copies:
        copy.wait()


def others_kernel(where, *refs):
    mine, theirs, refs = refs[0:7], refs[7:14], refs[18:]
    outs, parts, halves, sems = refs[0:4], refs[4:8], refs[8], refs[9]
    core, spot = where[2], where[3]
    sign = 1 - 2 * core

    for at in range(3):
        for pieces, hand, place, which in ((mine, sign, core, at), (theirs, -sign, 1 - core, (1, 0, 2)[at])):
            halves[place, 0:AROWS, :] = pieces[which][...]
            for quarters, shift in zip(pieces[3:7], (0, 1, -1, 2)):
                source = lax.rem(spot + 4 - hand * shift, 4)
                rows = pl.ds(pl.multiple_of(AROWS + source * QROWS, 8), QROWS)
                halves[place, rows, :] = quarters[QROWS * which : QROWS * which + QROWS, :]
        write_column(halves.at[0], halves.at[1], at, *parts)
        column = lax.rem(where[1] + 4 - sign * (1, -1, 2)[at], 4)
        for k in range(4):
            pltpu.make_async_copy(parts[k].at[at], outs[k].at[column], sems.at[at, k]).start()
    for at in range(3):
        column = lax.rem(where[1] + 4 - sign * (1, -1, 2)[at], 4)
        for k in range(4):
            pltpu.make_async_copy(parts[k].at[at], outs[k].at[column], sems.at[at, k]).wait()


def hand_over(where, column, factors, slots):
    half = factors.shape[0] // 2
    for at in range(3):

        @pl.when(column == where[4 + at])
        def _(at=at):
            slots[at][0:half, :] = factors[pl.ds(pl.multiple_of(where[2] * half, 8), half), :]

    @pl.when(column == where[1])
    def _():
        slots[3][...] = factors[...]


def take(where, halves, whole):
    core = where[2]
    whole[pl.ds(pl.multiple_of(core * 96, 8), 96), :] = halves[0][...]
    whole[pl.ds(pl.multiple_of((1 - core) * 96, 8), 96), :] = halves[1][...]
    return whole[0:128, 0:C1], get_two(whole, 128)


def give(where, first, second, whole, half):
    put(whole, 0, first)
    put_two(whole, 128, second)
    half[...] = whole[pl.ds(pl.multiple_of(where[2] * 96, 8), 96), :]


def read_crop(where, same, cross, crop):
    crop[pl.ds(pl.multiple_of(where[2] * 64, 8), 64), :] = same[...]
    crop[pl.ds(pl.multiple_of((1 - where[2]) * 64, 8), 64), :] = cross[...]


def forward_kernel(opening, full, where, *refs):
    if opening:
        state1, state2 = jnp.zeros((128, C1), F32), jnp.zeros((32, C2), F32)
    else:
        state1, state2 = take(where, refs[0:2], refs[-1])
        refs = refs[2:]
    same_ref, cross_ref, up_ref, mix_ref, down_ref, aux_ref, out_ref, *rest = refs
    crop_ref, whole = refs[-2:]
    read_crop(where, same_ref, cross_ref, crop_ref)
    if full:
        mixture_ref, slope1_ref, slope2_ref, *slots = rest[:-3]
        factors = rest[-3]
    for column in range(4):
        taps, gain1, gain2 = decode_aux(aux_ref[column])
        narrow = state2.astype(BF16)
        ups = up2(dot(narrow, up_ref[column]))
        mixture = [crop_ref[16 * q : 16 * q + 16, 0:C1] + ups[q] for q in range(8)]
        depth = join(stencil(neighbours(mixture), taps))
        if full:
            active, slope1 = gelu_pair(depth)
        else:
            active = gelu_only(depth)
        hidden = active.astype(BF16)
        state1 = gain1 * state1 + dot(hidden, mix_ref[column])
        pooled = (pool(split(state1)) * 0.25).astype(BF16)
        lifted = dot(pooled, down_ref[column])
        if full:
            active2, slope2 = gelu_pair(lifted)
        else:
            active2 = gelu_only(lifted)
        state2 = gain2 * state2 + active2
        if full:
            mixture_ref[column] = join(mixture)
            slope1_ref[column] = slope1
            slope2_ref[column] = slope2
            put(factors, 0, hidden.astype(F32))
            put(factors, 128, pooled.astype(F32))
            put_two(factors, 160, narrow.astype(F32))
            hand_over(where, column, factors, slots)
    if full:
        put(out_ref, 0, state1)
        put_two(out_ref, 128, state2)
    else:
        give(where, state1, state2, whole, out_ref)


def head_kernel(where, msg_ref, same_ref, cross_ref, one_ref, two_ref, cls_ref, out_ref, first, second, crop_ref):
    read_crop(where, same_ref, cross_ref, crop_ref)
    state1 = msg_ref[0:128, 0:C1].astype(BF16)
    state2 = get_two(msg_ref, 128).astype(BF16)
    labels = crop_ref[:, C1 : C1 + 1].astype(jnp.int32)
    second[...] = dot(state2, two_ref[...])
    first[...] = dot(state1, one_ref[...])
    lateral = first[...] + join(up2(second[...]))
    active, slope = gelu_pair(lateral)
    logits = dot_nt(active.astype(BF16), cls_ref[...])
    classes = lax.broadcasted_iota(jnp.int32, logits.shape, 1)
    logits = logits - jnp.max(logits, axis=-1, keepdims=True)
    powers = jnp.exp(logits)
    probs = powers / jnp.sum(powers, axis=-1, keepdims=True)
    onehot = (classes == labels).astype(F32)
    grad_logits = (probs - onehot) * (loss_scale / 2048.0)
    grad_lat = dot(grad_logits.astype(BF16), cls_ref[...]) * slope
    put(out_ref, 0, dot_nt(grad_lat.astype(BF16), one_ref[...]))
    put_two(out_ref, 128, dot_nt(pool(split(grad_lat)).astype(BF16), two_ref[...]))


def backward_kernel(opening, full, where, *refs):
    if opening:
        head_ref, *refs = refs
        cot1, cot2 = head_ref[0:128, 0:C1], get_two(head_ref, 128)
    else:
        near, far, head_ref, *refs = refs
        cot1, cot2 = take(where, (near, far), refs[-1])
        last = where[0] == 3
        cot1 = jnp.where(last, head_ref[0:128, 0:C1], cot1)
        cot2 = jnp.where(last, get_two(head_ref, 128), cot2)
    slope1_ref, slope2_ref, up_ref, mix_ref, down_ref, aux_ref, *rest = refs
    if full:
        mixture_ref, *slots, stem_own, factors, stem_sum, whole = rest
    else:
        out_ref, whole = rest
    for column in (3, 2, 1, 0):
        taps, gain1, gain2 = decode_aux(aux_ref[column])
        grad_s = (cot2 * slope2_ref[column]).astype(BF16)
        back = dot_nt(grad_s, down_ref[column]) * 0.25
        total1 = cot1 + join(up2(back))
        narrow_total = total1.astype(BF16)
        grad_depth = dot_nt(narrow_total, mix_ref[column]) * slope1_ref[column]
        grads = split(grad_depth)
        grad_mixture = stencil(neighbours(grads), taps[::-1])
        grad_narrow = pool(grad_mixture).astype(BF16)
        if not full or column > 0:
            cot2 = gain2 * cot2 + dot_nt(grad_narrow, up_ref[column])
            cot1 = gain1 * total1
        if full:
            put(factors, 0, narrow_total.astype(F32))
            put(factors, 128, grad_narrow.astype(F32))
            put_two(factors, 160, grad_s.astype(F32))
            sums = tap_sums(neighbours(split(mixture_ref[column])), grads)
            put(factors, 224, jnp.concatenate(sums + [jnp.zeros((7, C1), F32)], axis=0))
            hand_over(where, column, factors, slots)
            mixed = join(grad_mixture)
            stem_sum[...] = mixed if column == 3 else stem_sum[...] + mixed
    if full:
        mine = stem_sum[pl.ds(pl.multiple_of(where[2] * 64, 8), 64), :]
        mine = jnp.concatenate([mine, jnp.zeros((64, PAD1 - C1), F32)], axis=1)
        targets = [(where[4 + at], slots[at].at[RROWS // 2 :]) for at in range(3)] + [(where[1], stem_own)]
        for cell in range(4):
            rows = [16 * q + 4 * y + cell for y in range(4) for q in range(4)]
            part = join([mine[row : row + 1] for row in rows])
            for target, ref in targets:

                @pl.when(target == cell)
                def _(part=part, ref=ref):
                    ref[...] = part
    else:
        give(where, cot1, cot2, whole, out_ref)


def weight_kernel(where, lo, l1, l2, l3, m1, m2, m3, ro, r1, r2, r3, s1, s2, s3, stem_own, *rest):
    *outs, c0, c1, c2, c3, left, right = rest
    core = where[2]
    for full_ref, own, pairs, rows in (
        (left, lo, ((l1, m2), (l2, m1), (l3, m3)), LROWS),
        (right, ro, ((r1, s2), (r2, s1), (r3, s3)), RROWS),
    ):
        half = rows // 2
        mine = pl.ds(pl.multiple_of(core * half, 8), half)
        other = pl.ds(pl.multiple_of((1 - core) * half, 8), half)
        full_ref[0] = own[...]
        for at, (near, far) in enumerate(pairs):
            full_ref[at + 1, mine, :] = near[0:half, :]
            full_ref[at + 1, other, :] = far[0:half, :]

    def stack(ref, row, count):
        return jnp.concatenate([ref[q, row : row + count, :] for q in range(4)], axis=0)

    hidden = stack(left, 0, 128)
    pooled = stack(left, 128, 32)
    narrow = jnp.concatenate([stack(left, 160, 32), stack(left, 192, 32)], axis=1)
    total = stack(right, 0, 128).astype(BF16)
    grad_narrow = stack(right, 128, 32).astype(BF16)
    grad_lo = stack(right, 160, 32).astype(BF16)
    grad_hi = stack(right, 192, 32).astype(BF16)
    taps = right[0, 224:240, :] + right[1, 224:240, :] + right[2, 224:240, :] + right[3, 224:240, :]
    for at, out_ref in enumerate(outs):
        block = where[7 + at]
        back1 = lax.rem(PAD1 - 45 * block, PAD1)
        back2 = lax.rem(2 * PAD1 - 90 * block, 2 * PAD1)
        some_hidden = pltpu.roll(hidden, back1, 1)[:, 0:128].astype(BF16)
        some_pooled = pltpu.roll(pooled, back1, 1)[:, 0:128].astype(BF16)
        some_narrow = pltpu.roll(narrow, back2, 1)[:, 0:128].astype(BF16)
        out_ref[0:96, :] = dot_tn(some_narrow, grad_narrow)[0:96]
        out_ref[96:144, :] = dot_tn(some_hidden, total)[0:48]
        out_ref[144:192, :] = dot_tn(some_pooled, grad_lo)[0:48]
        out_ref[192:240, :] = dot_tn(some_pooled, grad_hi)[0:48]
        out_ref[240:256, :] = pltpu.roll(taps, back1, 1)
    z, sign, skip = where[1], 1 - 2 * core, RROWS // 2
    sources = ((stem_own, 0, z), (r1, skip, z - sign), (r2, skip, z + sign), (r3, skip, z + 2))
    for ref, row, source in sources:
        for cell in range(4):
            part = ref[row + 4 * cell : row + 4 * cell + 4, :]
            for shift, out_ref in enumerate((c0, c1, c2, c3)):

                @pl.when(lax.rem(where[0] + shift, 4) == cell)
                def _(part=part, out_ref=out_ref, source=source):
                    out_ref[lax.rem(source + 4, 4)] = part


def final_kernel(where, own, near, far, c0, c1, c2, c3, up_ref, mix_ref, down_ref, tap_ref, stem_ref):
    total = own[...] + near[...] + far[...]
    up_ref[:, 0, :] = total[0:90, 0:C1]
    mix_ref[:, 0, :] = total[96:141, 0:C1]
    down_ref[:, 0, 0:PAD1] = total[144:189]
    down_ref[:, 0, PAD1:C2] = total[192:237, 0 : C2 - PAD1]
    tap_ref[:, 0, :] = total[240:249, 0:45]
    cells = c0[...] + c1[...] + c2[...] + c3[...]
    stem_ref[:, 0] = cells[:, 0:2, 0:C1]
    stem_ref[:, 1] = cells[:, 2:4, 0:C1]


def shape(*dims, kind=F32):
    return jax.ShapeDtypeStruct(dims, kind)


SMEM = pl.BlockSpec(memory_space=pltpu.SMEM)
WHOLE = pl.BlockSpec(memory_space=pltpu.VMEM)
ANY = pl.BlockSpec(memory_space=pl.ANY)
HBM = pl.BlockSpec(memory_space=pltpu.HBM)


def shards(stem, labels, up_proj, mix_proj, down_proj, dw_kernel, gain1, gain2, lat_one, lat_two, classifier):
    y, z = lax.axis_index("y"), lax.axis_index("z")
    core = lax.axis_index("core")
    sign = 1 - 2 * core
    spot = lax.axis_index("xh") * 2 + lax.axis_index("xl")

    def around(at):
        return [(at + sign + 4) % 4, (at - sign + 4) % 4, (at + 2) % 4]

    blocks = [(x % 2) * 4 + core * 2 + x // 2 for x in around(spot) + [spot]]
    where = jnp.stack([y, z, core, spot, *around(z), *blocks]).astype(jnp.int32)

    def z_ring(step):
        return [
            (2 * at + c, 2 * ((at + (step if c == 0 else -step)) % 4) + c) for at in range(4) for c in range(2)
        ]

    def x_spot(x, c):
        return ((x % 2) * 2 + c) * 2 + x // 2

    def x_ring(step):
        return [
            (x_spot(x, c), x_spot((x + (step if c == 0 else -step)) % 4, c)) for x in range(4) for c in range(2)
        ]

    z_axes, x_axes = ("z", "core"), ("xl", "core", "xh")

    def swap(values):
        return lax.ppermute(values, "core", [(0, 1), (1, 0)])

    def deliver(slots):
        near = lax.ppermute(slots[0], z_axes, z_ring(1))
        away = lax.ppermute(slots[1], z_axes, z_ring(-1))
        opposite = lax.ppermute(slots[2], z_axes, z_ring(2))
        return near, away, opposite

    piece = lax.dynamic_index_in_dim(stem, z, 0, keepdims=False).astype(F32)
    marks = lax.dynamic_index_in_dim(labels, z, 0, keepdims=False).astype(F32)
    piece = jnp.concatenate([piece, marks[..., None], jnp.zeros((2, 32, PAD1 - C1 - 1), F32)], axis=-1)
    piece = piece.reshape(2, 16, 2, PAD1).transpose(0, 2, 1, 3).reshape(64, PAD1)
    where, piece = lax.optimization_barrier((where, piece))
    pairs = [(c, s) for c in range(2) for s in range(2)]
    same = lax.ppermute(piece, ("core", "xh"), [(2 * c + s, 2 * s + c) for c, s in pairs])
    cross = lax.ppermute(piece, ("core", "xh"), [(2 * c + s, 2 * (1 - s) + c) for c, s in pairs])
    weight_dims = ((C2, C1), (C1, C1), (C1, C2))
    half, straight, quarter = pl.pallas_call(
        pack_kernel,
        out_shape=(shape(WROWS, 2 * PAD1), shape(AROWS, 2 * PAD1), shape(QROWS, 2 * PAD1)),
        in_specs=[SMEM] + [HBM] * 6,
        out_specs=(WHOLE,) * 3,
        scratch_shapes=[pltpu.VMEM((1,) + dims, BF16) for dims in weight_dims]
        + [pltpu.VMEM((1, 9, C1), BF16), pltpu.VMEM((1, C1), F32), pltpu.VMEM((1, C2), F32)]
        + [pltpu.SemaphoreType.DMA((6,))],
        compiler_params=params(),
        name="pack",
    )(where, up_proj, mix_proj, down_proj, dw_kernel, gain1, gain2)

    def both_ways(values, axes, ring):
        return lax.ppermute(values, axes, ring(1)), lax.ppermute(values, axes, ring(-1))

    near, away = both_ways(quarter, z_axes, z_ring)
    opposite = lax.ppermute(near, z_axes, z_ring(1))
    near, away, opposite, straight, same, cross = lax.optimization_barrier((near, away, opposite, straight, same, cross))
    quarters = pl.pallas_call(
        join_kernel,
        out_shape=shape(3 * QROWS, 2 * PAD1),
        in_specs=[WHOLE] * 3,
        out_specs=WHOLE,
        compiler_params=params(),
        name="join_quarters",
    )(near, away, opposite)
    straights = both_ways(straight, z_axes, z_ring)
    spread = both_ways(quarters, x_axes, x_ring)
    mine = [
        *straights,
        lax.ppermute(straights[0], z_axes, z_ring(1)),
        quarters,
        *spread,
        lax.ppermute(spread[0], x_axes, x_ring(1)),
    ]
    columns = tuple(shape(4, *dims, kind=BF16) for dims in weight_dims) + (shape(4, 8, 2 * PAD1),)

    def column_scratch(count):
        return [pltpu.VMEM((count,) + dims, BF16) for dims in weight_dims] + [pltpu.VMEM((count, 8, 2 * PAD1), F32)]

    weights = pl.pallas_call(
        own_kernel,
        out_shape=columns,
        in_specs=[SMEM] + [WHOLE] * 2,
        out_specs=(ANY,) * 4,
        scratch_shapes=column_scratch(1) + [pltpu.SemaphoreType.DMA((4,))],
        compiler_params=params(),
        name="own_column",
    )(where, half, swap(half))
    weights = pl.pallas_call(
        others_kernel,
        out_shape=columns,
        in_specs=[SMEM] + [WHOLE] * 14 + [ANY] * 4,
        out_specs=(ANY,) * 4,
        input_output_aliases={15 + k: k for k in range(4)},
        scratch_shapes=column_scratch(3) + [pltpu.VMEM((2, WROWS, 2 * PAD1), F32), pltpu.SemaphoreType.DMA((3, 4))],
        compiler_params=params(),
        name="other_columns",
    )(where, *mine, *[swap(part) for part in mine], *weights)

    whole = pltpu.VMEM((192, PAD1), F32)

    def forward(halves, full):
        dims = [(192, PAD1) if full else (96, PAD1)]
        if full:
            dims += [(4, 128, C1), (4, 128, C1), (4, 32, C2)] + [(LROWS // 2, PAD1)] * 3 + [(LROWS, PAD1)]
        return pl.pallas_call(
            lambda *refs: forward_kernel(not halves, full, *refs),
            out_shape=tuple(shape(*each) for each in dims),
            in_specs=[SMEM] + [WHOLE] * (len(halves) + 6),
            out_specs=(WHOLE,) * len(dims),
            scratch_shapes=[pltpu.VMEM((LROWS, PAD1), F32)] * full + [pltpu.VMEM((128, PAD1), F32), whole],
            compiler_params=params(),
            name="forward_full" if full else "forward_light",
        )(where, *halves, same, cross, *weights)

    def hop(half, pairs):
        half = lax.ppermute(half, "y", pairs)
        return half, swap(half)

    halves = ()
    for tick in range(3):
        halves = hop(forward(halves, False)[0], [(0, 1), (1, 2), (2, 3)])
    msg, mixture, slope1, slope2, *lefts, left = forward(halves, True)
    lefts = deliver(lefts)

    head = pl.pallas_call(
        head_kernel,
        out_shape=shape(192, PAD1),
        in_specs=[SMEM] + [WHOLE] * 6,
        out_specs=WHOLE,
        scratch_shapes=[pltpu.VMEM((128, HEAD), F32), pltpu.VMEM((32, HEAD), F32), pltpu.VMEM((128, PAD1), F32)],
        compiler_params=params(),
        name="head",
    )(where, msg, same, cross, lat_one, lat_two, classifier.T)

    def backward(halves, full):
        operands = [*halves, head, slope1, slope2, *weights]
        dims = [(96, PAD1)]
        if full:
            operands.append(mixture)
            dims = [(RROWS // 2 + 16, PAD1)] * 3 + [(RROWS, PAD1), (16, PAD1)]
        return pl.pallas_call(
            lambda *refs: backward_kernel(not halves, full, *refs),
            out_shape=tuple(shape(*each) for each in dims),
            in_specs=[SMEM] + [WHOLE] * len(operands),
            out_specs=(WHOLE,) * len(dims),
            scratch_shapes=[pltpu.VMEM((RROWS, PAD1), F32), pltpu.VMEM((128, C1), F32)] * full + [whole],
            compiler_params=params(),
            name="backward_full" if full else "backward_light",
        )(where, *operands)

    halves = ()
    for tick in range(3):
        halves = hop(backward(halves, False)[0], [(1, 0), (2, 1), (3, 2)])
        if tick == 0:
            halves, lefts = lax.optimization_barrier((halves, lefts))
            mates = [swap(part) for part in lefts]
        if tick == 1:
            halves, mates = lax.optimization_barrier((halves, mates))
    slots = backward(halves, True)
    rights = deliver(slots[0:3])

    *partial, c0, c1, c2, c3 = pl.pallas_call(
        weight_kernel,
        out_shape=(shape(GROWS, PAD1),) * 4 + (shape(4, 4, PAD1),) * 4,
        in_specs=[SMEM] + [WHOLE] * 15,
        out_specs=(WHOLE,) * 8,
        scratch_shapes=[pltpu.VMEM((4, LROWS, PAD1), F32), pltpu.VMEM((4, RROWS, PAD1), F32)],
        compiler_params=params(),
        name="weight_grads",
    )(where, left, *lefts, *mates, slots[3], *rights, *[swap(part) for part in rights], slots[4])
    relay = lax.ppermute(partial[2], x_axes, x_ring(1))
    away = lax.ppermute(partial[1], x_axes, x_ring(-1))
    relay, away, cells = lax.optimization_barrier((relay, away, (c0, c1, c2, c3)))
    passed = pl.pallas_call(
        add_kernel,
        out_shape=shape(GROWS, PAD1),
        in_specs=[WHOLE] * 2,
        out_specs=WHOLE,
        compiler_params=params(),
        name="add_relay",
    )(partial[0], relay)
    near = lax.ppermute(passed, x_axes, x_ring(1))

    def stem_pairs(step):
        return [(4 * at + 2 * k + h, 4 * ((at + step) % 4) + 2 * h + k) for at in range(4) for k, h in pairs]

    cells = [lax.ppermute(cells[step], ("y", "core", "xh"), stem_pairs(step)) for step in range(4)]
    *grads, grad_stem = pl.pallas_call(
        final_kernel,
        out_shape=(shape(90, 1, C1), shape(45, 1, C1), shape(45, 1, C2), shape(9, 1, 45), shape(4, 2, 2, C1)),
        in_specs=[SMEM] + [WHOLE] * 7,
        out_specs=(WHOLE,) * 5,
        compiler_params=params(),
        name="final",
    )(where, partial[3], near, away, *cells)
    return (*[grad.transpose(1, 0, 2) for grad in grads], grad_stem)


def solution(mesh):
    fine = Mesh(mesh.devices.reshape(4, 4, 2, 2, 2), ("y", "z", "xl", "core", "xh"))
    col, dp, strip, both = ("y", "z"), ("xl", "core"), "xh", ("xl", "core", "xh")
    return jax.shard_map(
        shards,
        mesh=fine,
        in_specs=(
            P(dp, strip, None, None),
            P(dp, strip, None),
            P(col, None, None),
            P(col, None, None),
            P(col, None, None),
            P(col, None, None),
            P(col, None),
            P(col, None),
            P(),
            P(),
            P(),
        ),
        out_specs=(
            P(col, both, None),
            P(col, both, None),
            P(col, both, None),
            P(col, None, both),
            P(dp, strip, col, None),
        ),
        check_vma=False,
    )
```

time: 277 us -> 205 us (0.74); the launches traced: 273 us -> 204 us
  waiting for transfers between devices: 110 us -> 82.7 us
  local copies, waits for them, and re-layouts: 27.5 us -> 5.76 us
  blocking collectives: 10.4 us -> 0 us
  Pallas kernels: 45.3 us -> 39 us
    ppermute x19 -> x28, waiting for transfers between devices: 104 us -> 71.2 us  [the longest x6 21.5 us: hop(): half = lax.ppermute(half, 'y', pairs)]
    unnamed x59 -> x18, local copies, waits for them, and re-layouts: 25.8 us -> 5.15 us
    all_to_all x1 -> x0, blocking collectives: 10.4 us -> none  [shards(): cells = lax.all_to_all(cells, ('y', 'z'), 0, 0, tiled=True)]
    pallas_call x12 -> x15, Pallas kernels: 43.5 us -> 37.2 us  [the longest x4 15 us: backward(): pl.pallas_call(lambda *refs: backward_kernel(not halves, full, *refs), ou...]
    ppermute x10 -> x20, waiting for transfers between devices: 2.33 us -> 6.93 us  [swap(): return lax.ppermute(values, 'core', [(0, 1), (1, 0)])]
    ppermute x19 -> x28, starting transfers between devices: 50.4 us -> 46.4 us  [the longest x6 12.6 us: hop(): half = lax.ppermute(half, 'y', pairs)]
    ppermute x10 -> x20, starting transfers between devices: 21.7 us -> 22 us  [swap(): return lax.ppermute(values, 'core', [(0, 1), (1, 0)])]
  transfers between devices with their start and end apart: 31 -> 50, of which waited for: 17 -> 28; matrix products, arithmetic and copies ran while one was open for 2% -> 0% of each run, Pallas kernels for 0% -> 0%
where the time goes in v2:
time: 205 us; the launch traced here: 204 us
  waiting for transfers between devices  82.7 us (40%)
  starting transfers between devices  74 us (36%)
  Pallas kernels  39 us (19%)
  local copies, waits for them, and re-layouts  5.76 us (3%)
    ppermute x20, starting transfers between devices, swap(): return lax.ppermute(values, 'core', [(0, 1), (1, 0)])  22 us
    ppermute x6, waiting for transfers between devices, hop(): half = lax.ppermute(half, 'y', pairs)  21.5 us
    pallas_call x4, Pallas kernels, backward(): pl.pallas_call(lambda *refs: backward_kernel(not halves, full, *refs), ou...  15 us
    pallas_call x4, Pallas kernels, forward(): pl.pallas_call(lambda *refs: forward_kernel(not halves, full, *refs), out...  13.5 us
    ppermute x6, starting transfers between devices, hop(): half = lax.ppermute(half, 'y', pairs)  12.6 us
    ppermute x4, starting transfers between devices, shards(): lax.ppermute(cells[step], ('y', 'core', 'xh'), stem_pairs(step))  12 us
    ppermute x3, waiting for transfers between devices, both_ways(): lax.ppermute(values, axes, ring(1))  11.4 us
    ppermute x1, waiting for transfers between devices, shards(): relay = lax.ppermute(partial[2], x_axes, x_ring(1))  8.16 us
  transfers between devices with their start and end apart: 50, of which 28 were waited for; matrix products, arithmetic and copies ran while one was open for 0% of the time, Pallas kernels for 0%

profile of v2, /device:TPU:25, one launch (start us, length us, event | category | flops | bytes accessed | tf_op | source)
XLA Modules:
  0.0 204.2 jit_solution(4998332669629362096)
XLA Ops:
  3.1 1.1 copy-done.1
  4.1 1.0 copy-done.2
  9.2 3.8 %collective-permute-start = (f32[64,768]{1,0:T(8,128)S(1)}, f32[64,768]{1,0:T(8,128)S(1)}, u32[]{:S(2)}, u32[]{:S(2)}) collective-permute-start(f32[64,768]{1,0:T(8,128)S(1)} %get-tuple-element.67), channel_id=1, source_target_pairs={{0,8},{2,26},{8,16},{10,2},{16,24},{18,10},{24,0},{26,18},{1,9},{3... | collective-permute-start | bytes 589832 | tf_op jit(solution)/shard_map/ppermute | solution.py:529
  13.0 3.5 %collective-permute-done.first = f32[64,768]{1,0:T(8,128)S(1)} collective-permute-done((f32[64,768]{1,0:T(8,128)S(1)}, f32[64,768]{1,0:T(8,128)S(1)}, u32[]{:S(2)}, u32[]{:S(2)}) %collective-permute-start) | collective-permute-done | bytes 196640 | tf_op jit(solution)/shard_map/ppermute | solution.py:529
  16.5 3.4 %collective-permute-start.2 = (f32[64,768]{1,0:T(8,128)S(1)}, f32[64,768]{1,0:T(8,128)S(1)}, u32[]{:S(2)}, u32[]{:S(2)}) collective-permute-start(f32[64,768]{1,0:T(8,128)S(1)} %collective-permute-done.first), channel_id=1, source_target_pairs={{0,8},{2,26},{8,16},{10,2},{16,24},{18,10},{24,0},{26,18},{1,9},{3... | collective-permute-start | bytes 589832 | tf_op jit(solution)/shard_map/ppermute | solution.py:532
  19.9 2.7 %collective-permute-start.4 = (f32[64,384]{1,0:T(8,128)S(1)}, f32[64,384]{1,0:T(8,128)S(1)}, u32[]{:S(2)}, u32[]{:S(2)}) collective-permute-start(f32[64,384]{1,0:T(8,128)S(1)} %bitcast.22), channel_id=1, source_target_pairs={{0,2},{1,0},{2,3},{3,1},{4,6},{5,4},{6,7},{7,5},{8,10},{9,8},{10,1... | collective-permute-start | bytes 294920 | tf_op jit(solution)/shard_map/ppermute | solution.py:514
  22.7 2.8 %collective-permute-start.3 = (f32[64,384]{1,0:T(8,128)S(1)}, f32[64,384]{1,0:T(8,128)S(1)}, u32[]{:S(2)}, u32[]{:S(2)}) collective-permute-start(f32[64,384]{1,0:T(8,128)S(1)} %bitcast.23), channel_id=1, source_target_pairs={{0,0},{1,2},{2,1},{3,3},{4,4},{5,6},{6,5},{7,7},{8,8},{9,10},{10,9... | collective-permute-start | bytes 294920 | tf_op jit(solution)/shard_map/ppermute | solution.py:513
  25.5 4.6 %collective-permute-done.3.refs_1_.refs_3_.same_ref = f32[64,384]{1,0:T(8,128)S(1)} collective-permute-done((f32[64,384]{1,0:T(8,128)S(1)}, f32[64,384]{1,0:T(8,128)S(1)}, u32[]{:S(2)}, u32[]{:S(2)}) %collective-permute-start.3) | collective-permute-done | bytes 98336 | tf_op jit(solution)/shard_map/ppermute | solution.py:513
  31.5 2.4 %collective-permute-start.8 = (f32[192,768]{1,0:T(8,128)S(1)}, f32[192,768]{1,0:T(8,128)S(1)}, u32[]{:S(2)}, u32[]{:S(2)}) collective-permute-start(f32[192,768]{1,0:T(8,128)S(1)} %join_quarters.1.refs_3_), channel_id=1, source_target_pairs={{0,4},{2,7},{4,1},{6,2},{1,5},{3,6},{5,0},{7,3},{8,12},{10,15},{12... | collective-permute-start | bytes 1769480 | tf_op jit(solution)/shard_map/ppermute | solution.py:529
  34.4 7.9 %collective-permute-done.5.refs_0_ = f32[208,768]{1,0:T(8,128)S(1)} collective-permute-done((f32[208,768]{1,0:T(8,128)S(1)}, f32[208,768]{1,0:T(8,128)S(1)}, u32[]{:S(2)}, u32[]{:S(2)}) %collective-permute-start.5) | collective-permute-done | bytes 639008 | tf_op jit(solution)/shard_map/ppermute | solution.py:529
  42.4 1.5 collective-permute-start.7
  43.9 2.2 %collective-permute-done.9.refs_5_ = f32[192,768]{1,0:T(8,128)S(1)} collective-permute-done((f32[192,768]{1,0:T(8,128)S(1)}, f32[192,768]{1,0:T(8,128)S(1)}, u32[]{:S(2)}, u32[]{:S(2)}) %collective-permute-start.9) | collective-permute-done | bytes 589856 | tf_op jit(solution)/shard_map/ppermute | solution.py:529
  46.1 1.1 collective-permute-start.16
  47.3 1.5 collective-permute-start.10
  49.3 4.1 %collective-permute-done.7.refs_2_ = f32[208,768]{1,0:T(8,128)S(1)} collective-permute-done((f32[208,768]{1,0:T(8,128)S(1)}, f32[208,768]{1,0:T(8,128)S(1)}, u32[]{:S(2)}, u32[]{:S(2)}) %collective-permute-start.7) | collective-permute-done | bytes 639008 | tf_op jit(solution)/shard_map/ppermute | solution.py:546
  53.9 2.4 %collective-permute-done.10.refs_6_ = f32[192,768]{1,0:T(8,128)S(1)} collective-permute-done((f32[192,768]{1,0:T(8,128)S(1)}, f32[192,768]{1,0:T(8,128)S(1)}, u32[]{:S(2)}, u32[]{:S(2)}) %collective-permute-start.10) | collective-permute-done | bytes 589856 | tf_op jit(solution)/shard_map/ppermute | solution.py:549
  56.3 3.0 %collective-permute-start.17 = (f32[192,768]{1,0:T(8,128)S(1)}, f32[192,768]{1,0:T(8,128)S(1)}, u32[]{:S(2)}, u32[]{:S(2)}) collective-permute-start(f32[192,768]{1,0:T(8,128)S(1)} %collective-permute-done.10.refs_6_), channel_id=1, source_target_pairs={{0,2},{2,0},{1,3},{3,1},{4,6},{6,4},{5,7},{7,5},{8,10},{10,8},{9,1... | collective-permute-start | bytes 1769480 | tf_op jit(solution)/shard_map/ppermute | solution.py:499
  60.9 2.3 %other_columns.1 = (bf16[4,720,360]{2,1,0:T(8,128)(2,1)S(1)}, bf16[4,360,360]{2,1,0:T(8,128)(2,1)S(1)}, bf16[4,360,720]{2,1,0:T(8,128)(2,1)S(1)}, f32[4,8,768]{2,1,0:T(8,128)S(1)}) custom-call(s32[11]{0:T(128)S(1)} %stack.47.where.refs_0_, ...), custom_call_target="tpu_custom_call", output_to_operand_aliasing={{0}: (15, {}), {1}: (16, {}), {2}: (17, {}), {3}: (18, {})} | custom-call | tf_op jit(solution)/shard_map/other_columns/pallas_call | solution.py:565
  63.2 3.2 %forward_light.3 = f32[96,384]{1,0:T(8,128)S(1)} custom-call(s32[11]{0:T(128)S(1)} %stack.47.where.refs_0_, f32[64,384]{1,0:T(8,128)S(1)} %collective-permute-done.3.refs_1_.refs_3_.same_ref, f32[64,384]{1,0:T(8,128)S(1)} %collective-permute-done.4.refs_2_.refs_4_.cross_ref, bf16[4,720,360]{2,1,0:T(8,128)(2,1)S(1)} %get-tuple-element.81.refs_3_.refs_5_.refs_4_.refs_6_, ...), custom_call_target="tpu_custom_call" | custom-call | tf_op jit(solution)/shard_map/forward_light/pallas_call | solution.py:582
  66.4 1.3 collective-permute-start.19
  67.7 5.7 %collective-permute-done.19.refs_1_ = f32[96,384]{1,0:T(8,128)S(1)} collective-permute-done((f32[96,384]{1,0:T(8,128)S(1)}, f32[96,384]{1,0:T(8,128)S(1)}, u32[]{:S(2)}, u32[]{:S(2)}) %collective-permute-start.19) | collective-permute-done | bytes 147488 | tf_op jit(solution)/shard_map/ppermute | solution.py:593
  73.4 1.2 collective-permute-start.20
  74.6 1.0 collective-permute-done.20.refs_2_
  75.6 3.2 %forward_light.4 = f32[96,384]{1,0:T(8,128)S(1)} custom-call(s32[11]{0:T(128)S(1)} %stack.47.where.refs_0_, f32[96,384]{1,0:T(8,128)S(1)} %collective-permute-done.19.refs_1_, f32[96,384]{1,0:T(8,128)S(1)} %collective-permute-done.20.refs_2_, f32[64,384]{1,0:T(8,128)S(1)} %collective-permute-done.3.refs_1_.refs_3_.same_ref, ...), custom_call_target="tpu_custom_call" | custom-call | tf_op jit(solution)/shard_map/forward_light/pallas_call | solution.py:582
  78.8 1.3 collective-permute-start.21
  80.1 5.7 %collective-permute-done.21.refs_1_ = f32[96,384]{1,0:T(8,128)S(1)} collective-permute-done((f32[96,384]{1,0:T(8,128)S(1)}, f32[96,384]{1,0:T(8,128)S(1)}, u32[]{:S(2)}, u32[]{:S(2)}) %collective-permute-start.21) | collective-permute-done | bytes 147488 | tf_op jit(solution)/shard_map/ppermute | solution.py:593
  85.8 1.2 collective-permute-start.22
  87.0 1.0 collective-permute-done.22.refs_2_
  88.0 3.2 %forward_light.5 = f32[96,384]{1,0:T(8,128)S(1)} custom-call(s32[11]{0:T(128)S(1)} %stack.47.where.refs_0_, f32[96,384]{1,0:T(8,128)S(1)} %collective-permute-done.21.refs_1_, f32[96,384]{1,0:T(8,128)S(1)} %collective-permute-done.22.refs_2_, f32[64,384]{1,0:T(8,128)S(1)} %collective-permute-done.3.refs_1_.refs_3_.same_ref, ...), custom_call_target="tpu_custom_call" | custom-call | tf_op jit(solution)/shard_map/forward_light/pallas_call | solution.py:582
  91.2 1.4 collective-permute-start.23
  92.6 5.7 %collective-permute-done.23.refs_1_ = f32[96,384]{1,0:T(8,128)S(1)} collective-permute-done((f32[96,384]{1,0:T(8,128)S(1)}, f32[96,384]{1,0:T(8,128)S(1)}, u32[]{:S(2)}, u32[]{:S(2)}) %collective-permute-start.23) | collective-permute-done | bytes 147488 | tf_op jit(solution)/shard_map/ppermute | solution.py:593
  98.3 1.2 collective-permute-start.24
  99.5 1.0 collective-permute-done.24.refs_2_
  100.5 3.9 %forward_full.1 = (f32[192,384]{1,0:T(8,128)S(1)}, f32[4,128,360]{2,1,0:T(8,128)S(1)}, f32[4,128,360]{2,1,0:T(8,128)S(1)}, f32[4,32,720]{2,1,0:T(8,128)S(1)}, f3...) custom-call(s32[11]{0:T(128)S(1)} %stack.47.where.refs_0_, ...), custom_call_target="tpu_custom_call" | custom-call | tf_op jit(solution)/shard_map/forward_full/pallas_call | solution.py:582
  104.4 1.8 head.1.refs_1_.refs_3_
  106.2 3.5 %backward_light.3 = f32[96,384]{1,0:T(8,128)S(1)} custom-call(s32[11]{0:T(128)S(1)} %stack.47.where.refs_0_, f32[192,384]{1,0:T(8,128)S(1)} %head.1.refs_1_.refs_3_, f32[4,128,360]{2,1,0:T(8,128)S(1)} %get-tuple-element.87.refs_2_.refs_4_, f32[4,32,720]{2,1,0:T(8,128)S(1)} %get-tuple-element.88.refs_3_.refs_5_, ...), custom_call_target="tpu_custom_call" | custom-call | tf_op jit(solution)/shard_map/backward_light/pallas_call | solution.py:618
  109.7 2.4 %collective-permute-start.25 = (f32[96,384]{1,0:T(8,128)S(1)}, f32[96,384]{1,0:T(8,128)S(1)}, u32[]{:S(2)}, u32[]{:S(2)}) collective-permute-start(f32[96,384]{1,0:T(8,128)S(1)} %backward_light.3), channel_id=1, source_target_pairs={{32,0},{64,32},{96,64},{33,1},{65,33},{97,65},{34,2},{66,34},{98,6... | collective-permute-start | bytes 442376 | tf_op jit(solution)/shard_map/ppermute | solution.py:593
  112.1 1.5 collective-permute-start.27
  113.6 1.2 collective-permute-start.29
  114.9 1.4 collective-permute-start.26
  116.4 7.8 %collective-permute-done.28.l2 = f32[112,384]{1,0:T(8,128)S(1)} collective-permute-done((f32[112,384]{1,0:T(8,128)S(1)}, f32[112,384]{1,0:T(8,128)S(1)}, u32[]{:S(2)}, u32[]{:S(2)}) %collective-permute-start.28) | collective-permute-done | bytes 172064 | tf_op jit(solution)/shard_map/ppermute | solution.py:503
  124.2 3.5 %backward_light.4 = f32[96,384]{1,0:T(8,128)S(1)} custom-call(s32[11]{0:T(128)S(1)} %stack.47.where.refs_0_, f32[96,384]{1,0:T(8,128)S(1)} %collective-permute-done.25.refs_1_, f32[96,384]{1,0:T(8,128)S(1)} %collective-permute-done.26.refs_2_, f32[192,384]{1,0:T(8,128)S(1)} %head.1.refs_1_.refs_3_, f32[4,128,360]{2,1,0:T(8,128)S(1)} %get-tuple-element.87.refs_2_.refs_4_, ...), custom_call_target="tpu_custom_call" | custom-call | tf_op jit(solution)/shard_map/backward_light/pallas_call | solution.py:618
  127.7 2.1 %collective-permute-start.30 = (f32[96,384]{1,0:T(8,128)S(1)}, f32[96,384]{1,0:T(8,128)S(1)}, u32[]{:S(2)}, u32[]{:S(2)}) collective-permute-start(f32[96,384]{1,0:T(8,128)S(1)} %backward_light.4), channel_id=1, source_target_pairs={{32,0},{64,32},{96,64},{33,1},{65,33},{97,65},{34,2},{66,34},{98,6... | collective-permute-start | bytes 442376 | tf_op jit(solution)/shard_map/ppermute | solution.py:593
  131.1 1.5 collective-permute-done.30.refs_1_
  132.6 1.2 collective-permute-start.31
  133.8 1.0 collective-permute-done.31.refs_2_
  134.8 3.5 %backward_light.5 = f32[96,384]{1,0:T(8,128)S(1)} custom-call(s32[11]{0:T(128)S(1)} %stack.47.where.refs_0_, f32[96,384]{1,0:T(8,128)S(1)} %collective-permute-done.30.refs_1_, f32[96,384]{1,0:T(8,128)S(1)} %collective-permute-done.31.refs_2_, f32[192,384]{1,0:T(8,128)S(1)} %head.1.refs_1_.refs_3_, f32[4,128,360]{2,1,0:T(8,128)S(1)} %get-tuple-element.87.refs_2_.refs_4_, ...), custom_call_target="tpu_custom_call" | custom-call | tf_op jit(solution)/shard_map/backward_light/pallas_call | solution.py:618
  138.3 4.1 %collective-permute-start.35 = (f32[96,384]{1,0:T(8,128)S(1)}, f32[96,384]{1,0:T(8,128)S(1)}, u32[]{:S(2)}, u32[]{:S(2)}) collective-permute-start(f32[96,384]{1,0:T(8,128)S(1)} %backward_light.5), channel_id=1, source_target_pairs={{32,0},{64,32},{96,64},{33,1},{65,33},{97,65},{34,2},{66,34},{98,6... | collective-permute-start | bytes 442376 | tf_op jit(solution)/shard_map/ppermute | solution.py:593
  142.4 2.8 %collective-permute-done.35.refs_1_ = f32[96,384]{1,0:T(8,128)S(1)} collective-permute-done((f32[96,384]{1,0:T(8,128)S(1)}, f32[96,384]{1,0:T(8,128)S(1)}, u32[]{:S(2)}, u32[]{:S(2)}) %collective-permute-start.35) | collective-permute-done | bytes 147488 | tf_op jit(solution)/shard_map/ppermute | solution.py:593
  145.3 1.2 collective-permute-start.36
  146.5 1.0 collective-permute-done.36.refs_2_
  147.5 4.5 %backward_full.1 = (f32[136,384]{1,0:T(8,128)S(1)}, f32[136,384]{1,0:T(8,128)S(1)}, f32[136,384]{1,0:T(8,128)S(1)}, f32[240,384]{1,0:T(8,128)S(1)}, f32[16,384]{1,0:T(8,128)S(1)}) custom-call(s32[11]{0:T(128)S(1)} %stack.47.where.refs_0_, f32[96,384]{1,0:T(8,128)S(1)} %collective-permute-done.35.refs_1_, f32[96,384]{1,0:T(8,128)S(1)} %collective-permute-done.36.refs_2_, ...), custom_call_target="tpu_custom_call" | custom-call | tf_op jit(solution)/shard_map/backward_full/pallas_call | solution.py:618
  154.3 4.1 %collective-permute-done.37.r1 = f32[136,384]{1,0:T(8,128)S(1)} collective-permute-done((f32[136,384]{1,0:T(8,128)S(1)}, f32[136,384]{1,0:T(8,128)S(1)}, u32[]{:S(2)}, u32[]{:S(2)}) %collective-permute-start.37) | collective-permute-done | bytes 208928 | tf_op jit(solution)/shard_map/ppermute | solution.py:502
  158.4 7.6 %collective-permute-start.40 = (f32[136,384]{1,0:T(8,128)S(1)}, f32[136,384]{1,0:T(8,128)S(1)}, u32[]{:S(2)}, u32[]{:S(2)}) collective-permute-start(f32[136,384]{1,0:T(8,128)S(1)} %collective-permute-done.37.r1), channel_id=1, source_target_pairs={{0,2},{2,0},{1,3},{3,1},{4,6},{6,4},{5,7},{7,5},{8,10},{10,8},{9,1... | collective-permute-start | bytes 626696 | tf_op jit(solution)/shard_map/ppermute | solution.py:499
  167.8 3.1 %weight_grads.1 = (f32[256,384]{1,0:T(8,128)S(1)}, f32[256,384]{1,0:T(8,128)S(1)}, f32[256,384]{1,0:T(8,128)S(1)}, f32[256,384]{1,0:T(8,128)S(1)}, f32[4,4,384]{...) custom-call(s32[11]{0:T(128)S(1)} %stack.47.where.refs_0_, ...), custom_call_target="tpu_custom_call" | custom-call | tf_op jit(solution)/shard_map/weight_grads/pallas_call | solution.py:639
  170.9 2.2 %collective-permute-start.43 = (f32[256,384]{1,0:T(8,128)S(1)}, f32[256,384]{1,0:T(8,128)S(1)}, u32[]{:S(2)}, u32[]{:S(2)}) collective-permute-start(f32[256,384]{1,0:T(8,128)S(1)} %get-tuple-element.110), channel_id=1, source_target_pairs={{0,4},{2,7},{4,1},{6,2},{1,5},{3,6},{5,0},{7,3},{8,12},{10,15},{12... | collective-permute-start | bytes 1179656 | tf_op jit(solution)/shard_map/ppermute | solution.py:648
  173.2 8.2 %collective-permute-done.43.second = f32[256,384]{1,0:T(8,128)S(1)} collective-permute-done((f32[256,384]{1,0:T(8,128)S(1)}, f32[256,384]{1,0:T(8,128)S(1)}, u32[]{:S(2)}, u32[]{:S(2)}) %collective-permute-start.43) | collective-permute-done | bytes 393248 | tf_op jit(solution)/shard_map/ppermute | solution.py:648
  181.3 2.5 %collective-permute-done.44.far = f32[256,384]{1,0:T(8,128)S(1)} collective-permute-done((f32[256,384]{1,0:T(8,128)S(1)}, f32[256,384]{1,0:T(8,128)S(1)}, u32[]{:S(2)}, u32[]{:S(2)}) %collective-permute-start.44) | collective-permute-done | bytes 393248 | tf_op jit(solution)/shard_map/ppermute | solution.py:649
  184.0 5.2 %collective-permute-start.46 = (f32[4,4,384]{2,1,0:T(4,128)S(1)}, f32[4,4,384]{2,1,0:T(4,128)S(1)}, u32[]{:S(2)}, u32[]{:S(2)}) collective-permute-start(f32[4,4,384]{2,1,0:T(4,128)S(1)} %get-tuple-element.118), channel_id=1, source_target_pairs={{0,0},{1,2},{2,1},{3,3},{32,32},{33,34},{34,33},{35,35},{64,64},{6... | collective-permute-start | bytes 73736 | tf_op jit(solution)/shard_map/ppermute | solution.py:664
  189.3 1.7 collective-permute-start.47
  191.0 5.1 %collective-permute-start.48 = (f32[4,4,384]{2,1,0:T(4,128)S(1)}, f32[4,4,384]{2,1,0:T(4,128)S(1)}, u32[]{:S(2)}, u32[]{:S(2)}) collective-permute-start(f32[4,4,384]{2,1,0:T(4,128)S(1)} %get-tuple-element.120), channel_id=1, source_target_pairs={{0,64},{1,66},{2,65},{3,67},{32,96},{33,98},{34,97},{35,99},{64,0}... | collective-permute-start | bytes 73736 | tf_op jit(solution)/shard_map/ppermute | solution.py:664
  196.0 2.1 %collective-permute-done.48.c2 = f32[4,4,384]{2,1,0:T(4,128)S(1)} collective-permute-done((f32[4,4,384]{2,1,0:T(4,128)S(1)}, f32[4,4,384]{2,1,0:T(4,128)S(1)}, u32[]{:S(2)}, u32[]{:S(2)}) %collective-permute-start.48) | collective-permute-done | bytes 24608 | tf_op jit(solution)/shard_map/ppermute | solution.py:664
  198.1 4.8 %collective-permute-done.49.c3 = f32[4,4,384]{2,1,0:T(4,128)S(1)} collective-permute-done((f32[4,4,384]{2,1,0:T(4,128)S(1)}, f32[4,4,384]{2,1,0:T(4,128)S(1)}, u32[]{:S(2)}, u32[]{:S(2)}) %collective-permute-start.49) | collective-permute-done | bytes 24608 | tf_op jit(solution)/shard_map/ppermute | solution.py:664
  202.9 1.3 final.1
  (80 shorter events, 16.7 us)
Async XLA Ops:
  3.1 1.1 copy-start.1
  4.1 1.1 copy-start.2
  5.2 1.0 copy-start.4
  6.1 0.7 copy-start.6
  6.9 0.7 copy-start.7
  7.5 0.7 copy-start.8
  9.2 7.3 %collective-permute-start = (f32[64,768]{1,0:T(8,128)S(1)}, f32[64,768]{1,0:T(8,128)S(1)}, u32[]{:S(2)}, u32[]{:S(2)}) collective-permute-start(f32[64,768]{1,0:T(8,128)S(1)} %get-tuple-element.67), channel_id=1, source_target_pairs={{0,8},{2,26},{8,16},{10,2},{16,24},{18,10},{24,0},{26,18},{1,9},{3... | collective-permute-start | bytes 589832 | tf_op jit(solution)/shard_map/ppermute | solution.py:529
  13.0 17.1 %collective-permute-start.1 = (f32[64,768]{1,0:T(8,128)S(1)}, f32[64,768]{1,0:T(8,128)S(1)}, u32[]{:S(2)}, u32[]{:S(2)}) collective-permute-start(f32[64,768]{1,0:T(8,128)S(1)} %get-tuple-element.67), channel_id=1, source_target_pairs={{0,24},{2,10},{8,0},{10,18},{16,8},{18,26},{24,16},{26,2},{1,25},{... | collective-permute-start | bytes 589832 | tf_op jit(solution)/shard_map/ppermute | solution.py:529
  16.5 13.6 %collective-permute-start.2 = (f32[64,768]{1,0:T(8,128)S(1)}, f32[64,768]{1,0:T(8,128)S(1)}, u32[]{:S(2)}, u32[]{:S(2)}) collective-permute-start(f32[64,768]{1,0:T(8,128)S(1)} %collective-permute-done.first), channel_id=1, source_target_pairs={{0,8},{2,26},{8,16},{10,2},{16,24},{18,10},{24,0},{26,18},{1,9},{3... | collective-permute-start | bytes 589832 | tf_op jit(solution)/shard_map/ppermute | solution.py:532
  19.9 28.9 %collective-permute-start.18 = (f32[464,768]{1,0:T(8,128)S(1)}, f32[464,768]{1,0:T(8,128)S(1)}, u32[]{:S(2)}, u32[]{:S(2)}) collective-permute-start(f32[464,768]{1,0:T(8,128)S(1)} %get-tuple-element.76.half), channel_id=1, source_target_pairs={{0,2},{2,0},{1,3},{3,1},{4,6},{6,4},{5,7},{7,5},{8,10},{10,8},{9,1... | collective-permute-start | bytes 4276232 | tf_op jit(solution)/shard_map/ppermute | solution.py:499
  19.9 5.5 %collective-permute-start.4 = (f32[64,384]{1,0:T(8,128)S(1)}, f32[64,384]{1,0:T(8,128)S(1)}, u32[]{:S(2)}, u32[]{:S(2)}) collective-permute-start(f32[64,384]{1,0:T(8,128)S(1)} %bitcast.22), channel_id=1, source_target_pairs={{0,2},{1,0},{2,3},{3,1},{4,6},{5,4},{6,7},{7,5},{8,10},{9,8},{10,1... | collective-permute-start | bytes 294920 | tf_op jit(solution)/shard_map/ppermute | solution.py:514
  22.7 7.4 %collective-permute-start.3 = (f32[64,384]{1,0:T(8,128)S(1)}, f32[64,384]{1,0:T(8,128)S(1)}, u32[]{:S(2)}, u32[]{:S(2)}) collective-permute-start(f32[64,384]{1,0:T(8,128)S(1)} %bitcast.23), channel_id=1, source_target_pairs={{0,0},{1,2},{2,1},{3,3},{4,4},{5,6},{6,5},{7,7},{8,8},{9,10},{10,9... | collective-permute-start | bytes 294920 | tf_op jit(solution)/shard_map/ppermute | solution.py:513
  30.1 12.3 %collective-permute-start.5 = (f32[208,768]{1,0:T(8,128)S(1)}, f32[208,768]{1,0:T(8,128)S(1)}, u32[]{:S(2)}, u32[]{:S(2)}) collective-permute-start(f32[208,768]{1,0:T(8,128)S(1)} %get-tuple-element.72), channel_id=1, source_target_pairs={{0,8},{2,26},{8,16},{10,2},{16,24},{18,10},{24,0},{26,18},{1,9},{3... | collective-permute-start | bytes 1916936 | tf_op jit(solution)/shard_map/ppermute | solution.py:529
  31.0 2.8 %collective-permute-start.14 = (f32[192,768]{1,0:T(8,128)S(1)}, f32[192,768]{1,0:T(8,128)S(1)}, u32[]{:S(2)}, u32[]{:S(2)}) collective-permute-start(f32[192,768]{1,0:T(8,128)S(1)} %join_quarters.1.refs_3_), channel_id=1, source_target_pairs={{0,2},{2,0},{1,3},{3,1},{4,6},{6,4},{5,7},{7,5},{8,10},{10,8},{9,1... | collective-permute-start | bytes 1769480 | tf_op jit(solution)/shard_map/ppermute | solution.py:499
  31.1 15.0 %collective-permute-start.9 = (f32[192,768]{1,0:T(8,128)S(1)}, f32[192,768]{1,0:T(8,128)S(1)}, u32[]{:S(2)}, u32[]{:S(2)}) collective-permute-start(f32[192,768]{1,0:T(8,128)S(1)} %join_quarters.1.refs_3_), channel_id=1, source_target_pairs={{0,5},{2,6},{4,0},{6,3},{1,4},{3,7},{5,1},{7,2},{8,13},{10,14},{12... | collective-permute-start | bytes 1769480 | tf_op jit(solution)/shard_map/ppermute | solution.py:529
  31.5 15.7 %collective-permute-start.8 = (f32[192,768]{1,0:T(8,128)S(1)}, f32[192,768]{1,0:T(8,128)S(1)}, u32[]{:S(2)}, u32[]{:S(2)}) collective-permute-start(f32[192,768]{1,0:T(8,128)S(1)} %join_quarters.1.refs_3_), channel_id=1, source_target_pairs={{0,4},{2,7},{4,1},{6,2},{1,5},{3,6},{5,0},{7,3},{8,12},{10,15},{12... | collective-permute-start | bytes 1769480 | tf_op jit(solution)/shard_map/ppermute | solution.py:529
  33.9 14.9 %collective-permute-start.6 = (f32[208,768]{1,0:T(8,128)S(1)}, f32[208,768]{1,0:T(8,128)S(1)}, u32[]{:S(2)}, u32[]{:S(2)}) collective-permute-start(f32[208,768]{1,0:T(8,128)S(1)} %get-tuple-element.72), channel_id=1, source_target_pairs={{0,24},{2,10},{8,0},{10,18},{16,8},{18,26},{24,16},{26,2},{1,25},{... | collective-permute-start | bytes 1916936 | tf_op jit(solution)/shard_map/ppermute | solution.py:529
  42.4 11.0 %collective-permute-start.7 = (f32[208,768]{1,0:T(8,128)S(1)}, f32[208,768]{1,0:T(8,128)S(1)}, u32[]{:S(2)}, u32[]{:S(2)}) collective-permute-start(f32[208,768]{1,0:T(8,128)S(1)} %collective-permute-done.5.refs_0_), channel_id=1, source_target_pairs={{0,8},{2,26},{8,16},{10,2},{16,24},{18,10},{24,0},{26,18},{1,9},{3... | collective-permute-start | bytes 1916936 | tf_op jit(solution)/shard_map/ppermute | solution.py:546
  46.1 7.2 %collective-permute-start.16 = (f32[192,768]{1,0:T(8,128)S(1)}, f32[192,768]{1,0:T(8,128)S(1)}, u32[]{:S(2)}, u32[]{:S(2)}) collective-permute-start(f32[192,768]{1,0:T(8,128)S(1)} %collective-permute-done.9.refs_5_), channel_id=1, source_target_pairs={{0,2},{2,0},{1,3},{3,1},{4,6},{6,4},{5,7},{7,5},{8,10},{10,8},{9,1... | collective-permute-start | bytes 1769480 | tf_op jit(solution)/shard_map/ppermute | solution.py:499
  47.3 9.0 %collective-permute-start.10 = (f32[192,768]{1,0:T(8,128)S(1)}, f32[192,768]{1,0:T(8,128)S(1)}, u32[]{:S(2)}, u32[]{:S(2)}) collective-permute-start(f32[192,768]{1,0:T(8,128)S(1)} %collective-permute-done.8.refs_4_), channel_id=1, source_target_pairs={{0,4},{2,7},{4,1},{6,2},{1,5},{3,6},{5,0},{7,3},{8,12},{10,15},{12... | collective-permute-start | bytes 1769480 | tf_op jit(solution)/shard_map/ppermute | solution.py:549
  48.8 11.5 %collective-permute-start.12 = (f32[208,768]{1,0:T(8,128)S(1)}, f32[208,768]{1,0:T(8,128)S(1)}, u32[]{:S(2)}, u32[]{:S(2)}) collective-permute-start(f32[208,768]{1,0:T(8,128)S(1)} %collective-permute-done.6.refs_1_), channel_id=1, source_target_pairs={{0,2},{2,0},{1,3},{3,1},{4,6},{6,4},{5,7},{7,5},{8,10},{10,8},{9,1... | collective-permute-start | bytes 1916936 | tf_op jit(solution)/shard_map/ppermute | solution.py:499
  48.8 11.5 %collective-permute-start.11 = (f32[208,768]{1,0:T(8,128)S(1)}, f32[208,768]{1,0:T(8,128)S(1)}, u32[]{:S(2)}, u32[]{:S(2)}) collective-permute-start(f32[208,768]{1,0:T(8,128)S(1)} %collective-permute-done.5.refs_0_), channel_id=1, source_target_pairs={{0,2},{2,0},{1,3},{3,1},{4,6},{6,4},{5,7},{7,5},{8,10},{10,8},{9,1... | collective-permute-start | bytes 1916936 | tf_op jit(solution)/shard_map/ppermute | solution.py:499
  53.3 7.5 %collective-permute-start.13 = (f32[208,768]{1,0:T(8,128)S(1)}, f32[208,768]{1,0:T(8,128)S(1)}, u32[]{:S(2)}, u32[]{:S(2)}) collective-permute-start(f32[208,768]{1,0:T(8,128)S(1)} %collective-permute-done.7.refs_2_), channel_id=1, source_target_pairs={{0,2},{2,0},{1,3},{3,1},{4,6},{6,4},{5,7},{7,5},{8,10},{10,8},{9,1... | collective-permute-start | bytes 1916936 | tf_op jit(solution)/shard_map/ppermute | solution.py:499
  53.3 6.9 %collective-permute-start.15 = (f32[192,768]{1,0:T(8,128)S(1)}, f32[192,768]{1,0:T(8,128)S(1)}, u32[]{:S(2)}, u32[]{:S(2)}) collective-permute-start(f32[192,768]{1,0:T(8,128)S(1)} %collective-permute-done.8.refs_4_), channel_id=1, source_target_pairs={{0,2},{2,0},{1,3},{3,1},{4,6},{6,4},{5,7},{7,5},{8,10},{10,8},{9,1... | collective-permute-start | bytes 1769480 | tf_op jit(solution)/shard_map/ppermute | solution.py:499
  56.3 4.6 %collective-permute-start.17 = (f32[192,768]{1,0:T(8,128)S(1)}, f32[192,768]{1,0:T(8,128)S(1)}, u32[]{:S(2)}, u32[]{:S(2)}) collective-permute-start(f32[192,768]{1,0:T(8,128)S(1)} %collective-permute-done.10.refs_6_), channel_id=1, source_target_pairs={{0,2},{2,0},{1,3},{3,1},{4,6},{6,4},{5,7},{7,5},{8,10},{10,8},{9,1... | collective-permute-start | bytes 1769480 | tf_op jit(solution)/shard_map/ppermute | solution.py:499
  66.4 7.0 %collective-permute-start.19 = (f32[96,384]{1,0:T(8,128)S(1)}, f32[96,384]{1,0:T(8,128)S(1)}, u32[]{:S(2)}, u32[]{:S(2)}) collective-permute-start(f32[96,384]{1,0:T(8,128)S(1)} %forward_light.3), channel_id=1, source_target_pairs={{0,32},{32,64},{64,96},{1,33},{33,65},{65,97},{2,34},{34,66},{66,9... | collective-permute-start | bytes 442376 | tf_op jit(solution)/shard_map/ppermute | solution.py:593
  73.4 2.2 %collective-permute-start.20 = (f32[96,384]{1,0:T(8,128)S(1)}, f32[96,384]{1,0:T(8,128)S(1)}, u32[]{:S(2)}, u32[]{:S(2)}) collective-permute-start(f32[96,384]{1,0:T(8,128)S(1)} %collective-permute-done.19.refs_1_), channel_id=1, source_target_pairs={{0,2},{2,0},{1,3},{3,1},{4,6},{6,4},{5,7},{7,5},{8,10},{10,8},{9,1... | collective-permute-start | bytes 442376 | tf_op jit(solution)/shard_map/ppermute | solution.py:499
  78.8 7.0 %collective-permute-start.21 = (f32[96,384]{1,0:T(8,128)S(1)}, f32[96,384]{1,0:T(8,128)S(1)}, u32[]{:S(2)}, u32[]{:S(2)}) collective-permute-start(f32[96,384]{1,0:T(8,128)S(1)} %forward_light.4), channel_id=1, source_target_pairs={{0,32},{32,64},{64,96},{1,33},{33,65},{65,97},{2,34},{34,66},{66,9... | collective-permute-start | bytes 442376 | tf_op jit(solution)/shard_map/ppermute | solution.py:593
  85.8 2.2 %collective-permute-start.22 = (f32[96,384]{1,0:T(8,128)S(1)}, f32[96,384]{1,0:T(8,128)S(1)}, u32[]{:S(2)}, u32[]{:S(2)}) collective-permute-start(f32[96,384]{1,0:T(8,128)S(1)} %collective-permute-done.21.refs_1_), channel_id=1, source_target_pairs={{0,2},{2,0},{1,3},{3,1},{4,6},{6,4},{5,7},{7,5},{8,10},{10,8},{9,1... | collective-permute-start | bytes 442376 | tf_op jit(solution)/shard_map/ppermute | solution.py:499
  91.2 13.2 %copy-start = (bf16[720,512]{1,0:T(8,128)(2,1)S(1)}, bf16[720,512]{1,0:T(8,128)(2,1)}, u32[]{:S(2)}) copy-start(bf16[720,512]{1,0:T(8,128)(2,1)} %two_ref.1) | copy-start | bytes 2211844
  91.2 13.2 %copy-start.3 = (bf16[360,512]{1,0:T(8,128)(2,1)S(1)}, bf16[360,512]{1,0:T(8,128)(2,1)}, u32[]{:S(2)}) copy-start(bf16[360,512]{1,0:T(8,128)(2,1)} %one_ref.1) | copy-start | bytes 1105924
  91.2 13.2 %copy-start.5 = (bf16[512,150]{0,1:T(8,128)(2,1)S(1)}, bf16[512,150]{0,1:T(8,128)(2,1)}, u32[]{:S(2)}) copy-start(bf16[512,150]{0,1:T(8,128)(2,1)} %param.21) | copy-start | bytes 460804
  91.2 7.1 %collective-permute-start.23 = (f32[96,384]{1,0:T(8,128)S(1)}, f32[96,384]{1,0:T(8,128)S(1)}, u32[]{:S(2)}, u32[]{:S(2)}) collective-permute-start(f32[96,384]{1,0:T(8,128)S(1)} %forward_light.5), channel_id=1, source_target_pairs={{0,32},{32,64},{64,96},{1,33},{33,65},{65,97},{2,34},{34,66},{66,9... | collective-permute-start | bytes 442376 | tf_op jit(solution)/shard_map/ppermute | solution.py:593
  98.3 2.2 %collective-permute-start.24 = (f32[96,384]{1,0:T(8,128)S(1)}, f32[96,384]{1,0:T(8,128)S(1)}, u32[]{:S(2)}, u32[]{:S(2)}) collective-permute-start(f32[96,384]{1,0:T(8,128)S(1)} %collective-permute-done.23.refs_1_), channel_id=1, source_target_pairs={{0,2},{2,0},{1,3},{3,1},{4,6},{6,4},{5,7},{7,5},{8,10},{10,8},{9,1... | collective-permute-start | bytes 442376 | tf_op jit(solution)/shard_map/ppermute | solution.py:499
  109.7 5.2 %collective-permute-start.25 = (f32[96,384]{1,0:T(8,128)S(1)}, f32[96,384]{1,0:T(8,128)S(1)}, u32[]{:S(2)}, u32[]{:S(2)}) collective-permute-start(f32[96,384]{1,0:T(8,128)S(1)} %backward_light.3), channel_id=1, source_target_pairs={{32,0},{64,32},{96,64},{33,1},{65,33},{97,65},{34,2},{66,34},{98,6... | collective-permute-start | bytes 442376 | tf_op jit(solution)/shard_map/ppermute | solution.py:593
  112.1 4.3 %collective-permute-start.27 = (f32[112,384]{1,0:T(8,128)S(1)}, f32[112,384]{1,0:T(8,128)S(1)}, u32[]{:S(2)}, u32[]{:S(2)}) collective-permute-start(f32[112,384]{1,0:T(8,128)S(1)} %get-tuple-element.89), channel_id=1, source_target_pairs={{0,8},{2,26},{8,16},{10,2},{16,24},{18,10},{24,0},{26,18},{1,9},{3... | collective-permute-start | bytes 516104 | tf_op jit(solution)/shard_map/ppermute | solution.py:502
  113.5 10.7 %collective-permute-start.28 = (f32[112,384]{1,0:T(8,128)S(1)}, f32[112,384]{1,0:T(8,128)S(1)}, u32[]{:S(2)}, u32[]{:S(2)}) collective-permute-start(f32[112,384]{1,0:T(8,128)S(1)} %get-tuple-element.90), channel_id=1, source_target_pairs={{0,24},{2,10},{8,0},{10,18},{16,8},{18,26},{24,16},{26,2},{1,25},{... | collective-permute-start | bytes 516104 | tf_op jit(solution)/shard_map/ppermute | solution.py:503
  113.6 10.6 %collective-permute-start.29 = (f32[112,384]{1,0:T(8,128)S(1)}, f32[112,384]{1,0:T(8,128)S(1)}, u32[]{:S(2)}, u32[]{:S(2)}) collective-permute-start(f32[112,384]{1,0:T(8,128)S(1)} %get-tuple-element.91), channel_id=1, source_target_pairs={{0,16},{2,18},{8,24},{10,26},{16,0},{18,2},{24,8},{26,10},{1,17},{... | collective-permute-start | bytes 516104 | tf_op jit(solution)/shard_map/ppermute | solution.py:504
  114.9 9.3 %collective-permute-start.26 = (f32[96,384]{1,0:T(8,128)S(1)}, f32[96,384]{1,0:T(8,128)S(1)}, u32[]{:S(2)}, u32[]{:S(2)}) collective-permute-start(f32[96,384]{1,0:T(8,128)S(1)} %collective-permute-done.25.refs_1_), channel_id=1, source_target_pairs={{0,2},{2,0},{1,3},{3,1},{4,6},{6,4},{5,7},{7,5},{8,10},{10,8},{9,1... | collective-permute-start | bytes 442376 | tf_op jit(solution)/shard_map/ppermute | solution.py:499
  127.7 4.9 %collective-permute-start.30 = (f32[96,384]{1,0:T(8,128)S(1)}, f32[96,384]{1,0:T(8,128)S(1)}, u32[]{:S(2)}, u32[]{:S(2)}) collective-permute-start(f32[96,384]{1,0:T(8,128)S(1)} %backward_light.4), channel_id=1, source_target_pairs={{32,0},{64,32},{96,64},{33,1},{65,33},{97,65},{34,2},{66,34},{98,6... | collective-permute-start | bytes 442376 | tf_op jit(solution)/shard_map/ppermute | solution.py:593
  129.8 4.0 %collective-permute-start.32 = (f32[112,384]{1,0:T(8,128)S(1)}, f32[112,384]{1,0:T(8,128)S(1)}, u32[]{:S(2)}, u32[]{:S(2)}) collective-permute-start(f32[112,384]{1,0:T(8,128)S(1)} %collective-permute-done.27.l1), channel_id=1, source_target_pairs={{0,2},{2,0},{1,3},{3,1},{4,6},{6,4},{5,7},{7,5},{8,10},{10,8},{9,1... | collective-permute-start | bytes 516104 | tf_op jit(solution)/shard_map/ppermute | solution.py:499
  130.6 3.3 %collective-permute-start.33 = (f32[112,384]{1,0:T(8,128)S(1)}, f32[112,384]{1,0:T(8,128)S(1)}, u32[]{:S(2)}, u32[]{:S(2)}) collective-permute-start(f32[112,384]{1,0:T(8,128)S(1)} %collective-permute-done.28.l2), channel_id=1, source_target_pairs={{0,2},{2,0},{1,3},{3,1},{4,6},{6,4},{5,7},{7,5},{8,10},{10,8},{9,1... | collective-permute-start | bytes 516104 | tf_op jit(solution)/shard_map/ppermute | solution.py:499
  130.6 3.2 %collective-permute-start.34 = (f32[112,384]{1,0:T(8,128)S(1)}, f32[112,384]{1,0:T(8,128)S(1)}, u32[]{:S(2)}, u32[]{:S(2)}) collective-permute-start(f32[112,384]{1,0:T(8,128)S(1)} %collective-permute-done.29.l3), channel_id=1, source_target_pairs={{0,2},{2,0},{1,3},{3,1},{4,6},{6,4},{5,7},{7,5},{8,10},{10,8},{9,1... | collective-permute-start | bytes 516104 | tf_op jit(solution)/shard_map/ppermute | solution.py:499
  132.6 2.2 %collective-permute-start.31 = (f32[96,384]{1,0:T(8,128)S(1)}, f32[96,384]{1,0:T(8,128)S(1)}, u32[]{:S(2)}, u32[]{:S(2)}) collective-permute-start(f32[96,384]{1,0:T(8,128)S(1)} %collective-permute-done.30.refs_1_), channel_id=1, source_target_pairs={{0,2},{2,0},{1,3},{3,1},{4,6},{6,4},{5,7},{7,5},{8,10},{10,8},{9,1... | collective-permute-start | bytes 442376 | tf_op jit(solution)/shard_map/ppermute | solution.py:499
  138.3 7.0 %collective-permute-start.35 = (f32[96,384]{1,0:T(8,128)S(1)}, f32[96,384]{1,0:T(8,128)S(1)}, u32[]{:S(2)}, u32[]{:S(2)}) collective-permute-start(f32[96,384]{1,0:T(8,128)S(1)} %backward_light.5), channel_id=1, source_target_pairs={{32,0},{64,32},{96,64},{33,1},{65,33},{97,65},{34,2},{66,34},{98,6... | collective-permute-start | bytes 442376 | tf_op jit(solution)/shard_map/ppermute | solution.py:593
  145.3 2.2 %collective-permute-start.36 = (f32[96,384]{1,0:T(8,128)S(1)}, f32[96,384]{1,0:T(8,128)S(1)}, u32[]{:S(2)}, u32[]{:S(2)}) collective-permute-start(f32[96,384]{1,0:T(8,128)S(1)} %collective-permute-done.35.refs_1_), channel_id=1, source_target_pairs={{0,2},{2,0},{1,3},{3,1},{4,6},{6,4},{5,7},{7,5},{8,10},{10,8},{9,1... | collective-permute-start | bytes 442376 | tf_op jit(solution)/shard_map/ppermute | solution.py:499
  152.0 6.4 %collective-permute-start.37 = (f32[136,384]{1,0:T(8,128)S(1)}, f32[136,384]{1,0:T(8,128)S(1)}, u32[]{:S(2)}, u32[]{:S(2)}) collective-permute-start(f32[136,384]{1,0:T(8,128)S(1)} %get-tuple-element.104), channel_id=1, source_target_pairs={{0,8},{2,26},{8,16},{10,2},{16,24},{18,10},{24,0},{26,18},{1,9},{3... | collective-permute-start | bytes 626696 | tf_op jit(solution)/shard_map/ppermute | solution.py:502
  152.8 13.3 %collective-permute-start.38 = (f32[136,384]{1,0:T(8,128)S(1)}, f32[136,384]{1,0:T(8,128)S(1)}, u32[]{:S(2)}, u32[]{:S(2)}) collective-permute-start(f32[136,384]{1,0:T(8,128)S(1)} %get-tuple-element.105), channel_id=1, source_target_pairs={{0,24},{2,10},{8,0},{10,18},{16,8},{18,26},{24,16},{26,2},{1,25},{... | collective-permute-start | bytes 626696 | tf_op jit(solution)/shard_map/ppermute | solution.py:503
  153.6 12.5 %collective-permute-start.39 = (f32[136,384]{1,0:T(8,128)S(1)}, f32[136,384]{1,0:T(8,128)S(1)}, u32[]{:S(2)}, u32[]{:S(2)}) collective-permute-start(f32[136,384]{1,0:T(8,128)S(1)} %get-tuple-element.106), channel_id=1, source_target_pairs={{0,16},{2,18},{8,24},{10,26},{16,0},{18,2},{24,8},{26,10},{1,17},{... | collective-permute-start | bytes 626696 | tf_op jit(solution)/shard_map/ppermute | solution.py:504
  158.4 8.7 %collective-permute-start.40 = (f32[136,384]{1,0:T(8,128)S(1)}, f32[136,384]{1,0:T(8,128)S(1)}, u32[]{:S(2)}, u32[]{:S(2)}) collective-permute-start(f32[136,384]{1,0:T(8,128)S(1)} %collective-permute-done.37.r1), channel_id=1, source_target_pairs={{0,2},{2,0},{1,3},{3,1},{4,6},{6,4},{5,7},{7,5},{8,10},{10,8},{9,1... | collective-permute-start | bytes 626696 | tf_op jit(solution)/shard_map/ppermute | solution.py:499
  166.1 1.5 collective-permute-start.41
  166.1 1.8 collective-permute-start.42
  170.9 10.4 %collective-permute-start.43 = (f32[256,384]{1,0:T(8,128)S(1)}, f32[256,384]{1,0:T(8,128)S(1)}, u32[]{:S(2)}, u32[]{:S(2)}) collective-permute-start(f32[256,384]{1,0:T(8,128)S(1)} %get-tuple-element.110), channel_id=1, source_target_pairs={{0,4},{2,7},{4,1},{6,2},{1,5},{3,6},{5,0},{7,3},{8,12},{10,15},{12... | collective-permute-start | bytes 1179656 | tf_op jit(solution)/shard_map/ppermute | solution.py:648
  173.2 10.6 %collective-permute-start.44 = (f32[256,384]{1,0:T(8,128)S(1)}, f32[256,384]{1,0:T(8,128)S(1)}, u32[]{:S(2)}, u32[]{:S(2)}) collective-permute-start(f32[256,384]{1,0:T(8,128)S(1)} %get-tuple-element.111), channel_id=1, source_target_pairs={{0,5},{2,6},{4,0},{6,3},{1,4},{3,7},{5,1},{7,2},{8,13},{10,14},{12... | collective-permute-start | bytes 1179656 | tf_op jit(solution)/shard_map/ppermute | solution.py:649
  183.8 19.1 %collective-permute-start.45 = (f32[256,384]{1,0:T(8,128)S(1)}, f32[256,384]{1,0:T(8,128)S(1)}, u32[]{:S(2)}, u32[]{:S(2)}) collective-permute-start(f32[256,384]{1,0:T(8,128)S(1)} %add_relay.1), channel_id=1, source_target_pairs={{0,4},{2,7},{4,1},{6,2},{1,5},{3,6},{5,0},{7,3},{8,12},{10,15},{12... | collective-permute-start | bytes 1179656 | tf_op jit(solution)/shard_map/ppermute | solution.py:659
  184.0 12.0 %collective-permute-start.46 = (f32[4,4,384]{2,1,0:T(4,128)S(1)}, f32[4,4,384]{2,1,0:T(4,128)S(1)}, u32[]{:S(2)}, u32[]{:S(2)}) collective-permute-start(f32[4,4,384]{2,1,0:T(4,128)S(1)} %get-tuple-element.118), channel_id=1, source_target_pairs={{0,0},{1,2},{2,1},{3,3},{32,32},{33,34},{34,33},{35,35},{64,64},{6... | collective-permute-start | bytes 73736 | tf_op jit(solution)/shard_map/ppermute | solution.py:664
  189.3 6.8 %collective-permute-start.47 = (f32[4,4,384]{2,1,0:T(4,128)S(1)}, f32[4,4,384]{2,1,0:T(4,128)S(1)}, u32[]{:S(2)}, u32[]{:S(2)}) collective-permute-start(f32[4,4,384]{2,1,0:T(4,128)S(1)} %get-tuple-element.119), channel_id=1, source_target_pairs={{0,32},{1,34},{2,33},{3,35},{32,64},{33,66},{34,65},{35,67},{64,96... | collective-permute-start | bytes 73736 | tf_op jit(solution)/shard_map/ppermute | solution.py:664
  191.0 7.2 %collective-permute-start.48 = (f32[4,4,384]{2,1,0:T(4,128)S(1)}, f32[4,4,384]{2,1,0:T(4,128)S(1)}, u32[]{:S(2)}, u32[]{:S(2)}) collective-permute-start(f32[4,4,384]{2,1,0:T(4,128)S(1)} %get-tuple-element.120), channel_id=1, source_target_pairs={{0,64},{1,66},{2,65},{3,67},{32,96},{33,98},{34,97},{35,99},{64,0}... | collective-permute-start | bytes 73736 | tf_op jit(solution)/shard_map/ppermute | solution.py:664
  196.0 6.9 %collective-permute-start.49 = (f32[4,4,384]{2,1,0:T(4,128)S(1)}, f32[4,4,384]{2,1,0:T(4,128)S(1)}, u32[]{:S(2)}, u32[]{:S(2)}) collective-permute-start(f32[4,4,384]{2,1,0:T(4,128)S(1)} %get-tuple-element.121), channel_id=1, source_target_pairs={{0,96},{1,98},{2,97},{3,99},{32,0},{33,2},{34,1},{35,3},{64,32},{6... | collective-permute-start | bytes 73736 | tf_op jit(solution)/shard_map/ppermute | solution.py:664

commit v3 on v2

--- a/solution.py
+++ b/solution.py
@@ -17,6 +17,7 @@
 F32 = jnp.float32
 BF16 = jnp.bfloat16
 VMEM_LIMIT = 16 * 2**20
+PACK_LIMIT = 60 * 2**20
 
 WROWS = 464
 QROWS = 64
@@ -26,8 +27,8 @@
 GROWS = 256
 
 
-def params():
-    return pltpu.CompilerParams(vmem_limit_bytes=VMEM_LIMIT)
+def params(limit=VMEM_LIMIT):
+    return pltpu.CompilerParams(vmem_limit_bytes=limit)
 
 
 def gelu_pair(values):
@@ -141,41 +142,58 @@
     return jnp.concatenate([ref[row : row + 32, :], ref[row + 32 : row + 64, 0 : C2 - PAD1]], axis=1)
 
 
-def pack_kernel(where, up_hbm, mix_hbm, down_hbm, tap_hbm, g1_hbm, g2_hbm, out_ref, straight_ref, quarter_ref, up_ref, mix_ref, down_ref, tap_ref, g1_ref, g2_ref, sems):
+def pack_kernel(where, *refs):
+    sources, outs, held, sems = refs[0:8], refs[8:12], refs[12:20], refs[22]
+    (half_ref, wide_ref), (straight_ref, quarter_ref, piece_ref, aux_ref) = refs[20:22], outs
+    up_ref, mix_ref, down_ref, tap_ref, g1_ref, g2_ref, stem_ref, label_ref = held
     core = where[2]
-    pairs = (
-        (up_hbm, up_ref), (mix_hbm, mix_ref), (down_hbm, down_ref), (tap_hbm, tap_ref), (g1_hbm, g1_ref), (g2_hbm, g2_ref)
-    )
-    copies = [pltpu.make_async_copy(src, dst, sems.at[at]) for at, (src, dst) in enumerate(pairs)]
+    copies = [
+        pltpu.make_async_copy(src.at[where[1]] if at >= 6 else src, dst, sems.at[at])
+        for at, (src, dst) in enumerate(zip(sources, held))
+    ]
     for copy in copies:
         copy.start()
     for copy in copies:
         copy.wait()
     mix = mix_ref[0].astype(F32)
+    taps = tap_ref[0].astype(F32)
+    aux_ref[0:8, 0:C1] = taps[0:8]
+    aux_ref[0:1, PAD1 : PAD1 + C1] = taps[8:9]
+    aux_ref[1:2, PAD1 : PAD1 + C1] = g1_ref[...]
+    aux_ref[2:3, PAD1 : 2 * PAD1] = g2_ref[:, 0:PAD1]
+    aux_ref[3:4, PAD1:C2] = g2_ref[:, PAD1:C2]
 
     @pl.when(core == 0)
     def _():
         up = up_ref[0].astype(F32)
-        out_ref[0:368, 0:C1] = up[0:368]
-        out_ref[0:352, PAD1 : PAD1 + C1] = up[368:720]
-        out_ref[368:464, 0:C1] = mix[0:96]
-        out_ref[368:464, PAD1 : PAD1 + C1] = mix[96:192]
+        half_ref[0:368, 0:C1] = up[0:368]
+        half_ref[0:352, PAD1 : PAD1 + C1] = up[368:720]
+        half_ref[368:464, 0:C1] = mix[0:96]
+        half_ref[368:464, PAD1 : PAD1 + C1] = mix[96:192]
 
     @pl.when(core == 1)
     def _():
-        down = down_ref[0].astype(F32)
-        taps = tap_ref[0].astype(F32)
-        out_ref[0:360, 0:C2] = down
-        out_ref[360:368, 0:C1] = taps[0:8]
-        out_ref[360:361, PAD1 : PAD1 + C1] = taps[8:9]
-        out_ref[361:362, PAD1 : PAD1 + C1] = g1_ref[...]
-        out_ref[362:363, PAD1 : 2 * PAD1] = g2_ref[:, 0:PAD1]
-        out_ref[363:364, PAD1:C2] = g2_ref[:, PAD1:C2]
-        out_ref[368:464, 0:C1] = mix[192:288]
-        out_ref[368:440, PAD1 : PAD1 + C1] = mix[288:360]
-
-    straight_ref[...] = out_ref[0:AROWS, :]
-    quarter_ref[...] = out_ref[pl.ds(pl.multiple_of(AROWS + where[3] * QROWS, 8), QROWS), :]
+        half_ref[0:360, 0:C2] = down_ref[0].astype(F32)
+        half_ref[360:368, :] = aux_ref[...]
+        half_ref[368:464, 0:C1] = mix[192:288]
+        half_ref[368:440, PAD1 : PAD1 + C1] = mix[288:360]
+
+    straight_ref[...] = half_ref[0:AROWS, :]
+    quarter_ref[...] = half_ref[pl.ds(pl.multiple_of(AROWS + where[3] * QROWS, 8), QROWS), :]
+
+    wide = jnp.concatenate([stem_ref[...].astype(F32), jnp.zeros((2, 32, PAD1 - C1), F32)], axis=2)
+    for part in range(3):
+        wide_ref[part] = wide[:, :, 128 * part : 128 * part + 128]
+    marks = label_ref[...].astype(F32)
+    cell = lax.broadcasted_iota(jnp.int32, (16, 32), 0)
+    pixel = lax.broadcasted_iota(jnp.int32, (16, 32), 1)
+    lane = lax.broadcasted_iota(jnp.int32, (16, PAD1), 1)
+    for a in range(2):
+        for b in range(2):
+            chosen = jnp.where(pixel == 2 * cell + b, marks[a : a + 1], 0.0)
+            mark = jnp.sum(chosen, axis=1, keepdims=True)
+            pixels = jnp.concatenate([wide_ref[part, a, pl.ds(b, 16, stride=2), :] for part in range(3)], axis=1)
+            piece_ref[32 * a + 16 * b : 32 * a + 16 * b + 16, :] = jnp.where(lane == C1, mark, pixels)
 
 
 def write_column(first, second, at, up_ref, mix_ref, down_ref, aux_ref):
@@ -204,30 +222,23 @@
     out_ref[...] = first[...] + second[...]
 
 
-def own_kernel(where, half, mate, *refs):
-    outs, parts, sems = refs[0:4], refs[4:8], refs[8]
-
-    @pl.when(where[2] == 0)
-    def _():
-        write_column(half, mate, 0, *parts)
-
-    @pl.when(where[2] == 1)
-    def _():
-        write_column(mate, half, 0, *parts)
-
-    copies = [pltpu.make_async_copy(parts[k].at[0], outs[k].at[where[1]], sems.at[k]) for k in range(4)]
-    for copy in copies:
-        copy.start()
-    for copy in copies:
-        copy.wait()
-
-
-def others_kernel(where, *refs):
-    mine, theirs, refs = refs[0:7], refs[7:14], refs[18:]
+def columns_kernel(where, *refs):
+    mine, theirs, own, refs = refs[0:7], refs[7:14], refs[14:18], refs[18:]
     outs, parts, halves, sems = refs[0:4], refs[4:8], refs[8], refs[9]
     core, spot = where[2], where[3]
     sign = 1 - 2 * core
 
+    def moves(at):
+        if at == 3:
+            sources = [ref.at[0] for ref in own[0:3]] + [own[3]]
+            column = where[1]
+        else:
+            sources = [ref.at[at] for ref in parts]
+            column = lax.rem(where[1] + 4 - sign * (1, -1, 2)[at], 4)
+        return [pltpu.make_async_copy(src, outs[k].at[column], sems.at[at, k]) for k, src in enumerate(sources)]
+
+    for move in moves(3):
+        move.start()
     for at in range(3):
         for pieces, hand, place, which in ((mine, sign, core, at), (theirs, -sign, 1 - core, (1, 0, 2)[at])):
             halves[place, 0:AROWS, :] = pieces[which][...]
@@ -236,13 +247,11 @@
                 rows = pl.ds(pl.multiple_of(AROWS + source * QROWS, 8), QROWS)
                 halves[place, rows, :] = quarters[QROWS * which : QROWS * which + QROWS, :]
         write_column(halves.at[0], halves.at[1], at, *parts)
-        column = lax.rem(where[1] + 4 - sign * (1, -1, 2)[at], 4)
-        for k in range(4):
-            pltpu.make_async_copy(parts[k].at[at], outs[k].at[column], sems.at[at, k]).start()
-    for at in range(3):
-        column = lax.rem(where[1] + 4 - sign * (1, -1, 2)[at], 4)
-        for k in range(4):
-            pltpu.make_async_copy(parts[k].at[at], outs[k].at[column], sems.at[at, k]).wait()
+        for move in moves(at):
+            move.start()
+    for at in range(4):
+        for move in moves(at):
+            move.wait()
 
 
 def hand_over(where, column, factors, slots):
@@ -262,6 +271,21 @@
     core = where[2]
     whole[pl.ds(pl.multiple_of(core * 96, 8), 96), :] = halves[0][...]
     whole[pl.ds(pl.multiple_of((1 - core) * 96, 8), 96), :] = halves[1][...]
+
+
+def take_own(where, pairs, planes, start, whole):
+    for at, plane in enumerate(planes):
+
+        @pl.when(where[0] == plane)
+        def _(at=at):
+            take(where, pairs[2 * at : 2 * at + 2], whole)
+
+    @pl.when(where[0] == 6 - sum(planes))
+    def _():
+        whole[...] = jnp.zeros((192, PAD1), F32) if start is None else start[...]
+
+
+def unfold(whole):
     return whole[0:128, 0:C1], get_two(whole, 128)
 
 
@@ -279,8 +303,13 @@
 def forward_kernel(opening, full, where, *refs):
     if opening:
         state1, state2 = jnp.zeros((128, C1), F32), jnp.zeros((32, C2), F32)
+    elif full:
+        take_own(where, refs[0:6], (1, 2, 3), None, refs[-1])
+        state1, state2 = unfold(refs[-1])
+        refs = refs[6:]
     else:
-        state1, state2 = take(where, refs[0:2], refs[-1])
+        take(where, refs[0:2], refs[-1])
+        state1, state2 = unfold(refs[-1])
         refs = refs[2:]
     same_ref, cross_ref, up_ref, mix_ref, down_ref, aux_ref, out_ref, *rest = refs
     crop_ref, whole = refs[-2:]
@@ -346,13 +375,15 @@
 def backward_kernel(opening, full, where, *refs):
     if opening:
         head_ref, *refs = refs
-        cot1, cot2 = head_ref[0:128, 0:C1], get_two(head_ref, 128)
+        cot1, cot2 = unfold(head_ref)
+    elif full:
+        take_own(where, refs[0:6], (2, 1, 0), refs[6], refs[-1])
+        cot1, cot2 = unfold(refs[-1])
+        refs = refs[7:]
     else:
-        near, far, head_ref, *refs = refs
-        cot1, cot2 = take(where, (near, far), refs[-1])
-        last = where[0] == 3
-        cot1 = jnp.where(last, head_ref[0:128, 0:C1], cot1)
-        cot2 = jnp.where(last, get_two(head_ref, 128), cot2)
+        take(where, refs[0:2], refs[-1])
+        cot1, cot2 = unfold(refs[-1])
+        refs = refs[2:]
     slope1_ref, slope2_ref, up_ref, mix_ref, down_ref, aux_ref, *rest = refs
     if full:
         mixture_ref, *slots, stem_own, factors, stem_sum, whole = rest
@@ -504,33 +535,30 @@
         opposite = lax.ppermute(slots[2], z_axes, z_ring(2))
         return near, away, opposite
 
-    piece = lax.dynamic_index_in_dim(stem, z, 0, keepdims=False).astype(F32)
-    marks = lax.dynamic_index_in_dim(labels, z, 0, keepdims=False).astype(F32)
-    piece = jnp.concatenate([piece, marks[..., None], jnp.zeros((2, 32, PAD1 - C1 - 1), F32)], axis=-1)
-    piece = piece.reshape(2, 16, 2, PAD1).transpose(0, 2, 1, 3).reshape(64, PAD1)
-    where, piece = lax.optimization_barrier((where, piece))
+    weight_dims = ((C2, C1), (C1, C1), (C1, C2))
+    straight, quarter, piece, aux = pl.pallas_call(
+        pack_kernel,
+        out_shape=(shape(AROWS, 2 * PAD1), shape(QROWS, 2 * PAD1), shape(64, PAD1), shape(8, 2 * PAD1)),
+        in_specs=[SMEM] + [HBM] * 8,
+        out_specs=(WHOLE,) * 4,
+        scratch_shapes=[pltpu.VMEM((1,) + dims, BF16) for dims in weight_dims]
+        + [pltpu.VMEM((1, 9, C1), BF16), pltpu.VMEM((1, C1), F32), pltpu.VMEM((1, C2), F32)]
+        + [pltpu.VMEM((2, 32, C1), BF16), pltpu.VMEM((2, 32), jnp.int32)]
+        + [pltpu.VMEM((WROWS, 2 * PAD1), F32), pltpu.VMEM((3, 2, 32, 128), F32), pltpu.SemaphoreType.DMA((8,))],
+        compiler_params=params(PACK_LIMIT),
+        name="pack",
+    )(where, up_proj, mix_proj, down_proj, dw_kernel, gain1, gain2, stem, labels)
+
     pairs = [(c, s) for c in range(2) for s in range(2)]
     same = lax.ppermute(piece, ("core", "xh"), [(2 * c + s, 2 * s + c) for c, s in pairs])
     cross = lax.ppermute(piece, ("core", "xh"), [(2 * c + s, 2 * (1 - s) + c) for c, s in pairs])
-    weight_dims = ((C2, C1), (C1, C1), (C1, C2))
-    half, straight, quarter = pl.pallas_call(
-        pack_kernel,
-        out_shape=(shape(WROWS, 2 * PAD1), shape(AROWS, 2 * PAD1), shape(QROWS, 2 * PAD1)),
-        in_specs=[SMEM] + [HBM] * 6,
-        out_specs=(WHOLE,) * 3,
-        scratch_shapes=[pltpu.VMEM((1,) + dims, BF16) for dims in weight_dims]
-        + [pltpu.VMEM((1, 9, C1), BF16), pltpu.VMEM((1, C1), F32), pltpu.VMEM((1, C2), F32)]
-        + [pltpu.SemaphoreType.DMA((6,))],
-        compiler_params=params(),
-        name="pack",
-    )(where, up_proj, mix_proj, down_proj, dw_kernel, gain1, gain2)
 
     def both_ways(values, axes, ring):
         return lax.ppermute(values, axes, ring(1)), lax.ppermute(values, axes, ring(-1))
 
     near, away = both_ways(quarter, z_axes, z_ring)
     opposite = lax.ppermute(near, z_axes, z_ring(1))
-    near, away, opposite, straight, same, cross = lax.optimization_barrier((near, away, opposite, straight, same, cross))
+    near, away, opposite, straight = lax.optimization_barrier((near, away, opposite, straight))
     quarters = pl.pallas_call(
         join_kernel,
         out_shape=shape(3 * QROWS, 2 * PAD1),
@@ -541,6 +569,7 @@
     )(near, away, opposite)
     straights = both_ways(straight, z_axes, z_ring)
     spread = both_ways(quarters, x_axes, x_ring)
+    straights, spread, quarters, same, cross = lax.optimization_barrier((straights, spread, quarters, same, cross))
     mine = [
         *straights,
         lax.ppermute(straights[0], z_axes, z_ring(1)),
@@ -548,30 +577,16 @@
         *spread,
         lax.ppermute(spread[0], x_axes, x_ring(1)),
     ]
-    columns = tuple(shape(4, *dims, kind=BF16) for dims in weight_dims) + (shape(4, 8, 2 * PAD1),)
-
-    def column_scratch(count):
-        return [pltpu.VMEM((count,) + dims, BF16) for dims in weight_dims] + [pltpu.VMEM((count, 8, 2 * PAD1), F32)]
-
     weights = pl.pallas_call(
-        own_kernel,
-        out_shape=columns,
-        in_specs=[SMEM] + [WHOLE] * 2,
-        out_specs=(ANY,) * 4,
-        scratch_shapes=column_scratch(1) + [pltpu.SemaphoreType.DMA((4,))],
-        compiler_params=params(),
-        name="own_column",
-    )(where, half, swap(half))
-    weights = pl.pallas_call(
-        others_kernel,
-        out_shape=columns,
+        columns_kernel,
+        out_shape=tuple(shape(4, *dims, kind=BF16) for dims in weight_dims) + (shape(4, 8, 2 * PAD1),),
         in_specs=[SMEM] + [WHOLE] * 14 + [ANY] * 4,
         out_specs=(ANY,) * 4,
-        input_output_aliases={15 + k: k for k in range(4)},
-        scratch_shapes=column_scratch(3) + [pltpu.VMEM((2, WROWS, 2 * PAD1), F32), pltpu.SemaphoreType.DMA((3, 4))],
+        scratch_shapes=[pltpu.VMEM((3,) + dims, BF16) for dims in weight_dims]
+        + [pltpu.VMEM((3, 8, 2 * PAD1), F32), pltpu.VMEM((2, WROWS, 2 * PAD1), F32), pltpu.SemaphoreType.DMA((4, 4))],
         compiler_params=params(),
-        name="other_columns",
-    )(where, *mine, *[swap(part) for part in mine], *weights)
+        name="columns",
+    )(where, *mine, *[swap(part) for part in mine], up_proj, mix_proj, down_proj, aux)
 
     whole = pltpu.VMEM((192, PAD1), F32)
 
@@ -593,10 +608,10 @@
         half = lax.ppermute(half, "y", pairs)
         return half, swap(half)
 
-    halves = ()
+    arrived = [()]
     for tick in range(3):
-        halves = hop(forward(halves, False)[0], [(0, 1), (1, 2), (2, 3)])
-    msg, mixture, slope1, slope2, *lefts, left = forward(halves, True)
+        arrived.append(hop(forward(arrived[-1], False)[0], [(tick, tick + 1)]))
+    msg, mixture, slope1, slope2, *lefts, left = forward(sum(arrived, ()), True)
     lefts = deliver(lefts)
 
     head = pl.pallas_call(
@@ -610,7 +625,7 @@
     )(where, msg, same, cross, lat_one, lat_two, classifier.T)
 
     def backward(halves, full):
-        operands = [*halves, head, slope1, slope2, *weights]
+        operands = [*halves, *([] if halves and not full else [head]), slope1, slope2, *weights]
         dims = [(96, PAD1)]
         if full:
             operands.append(mixture)
@@ -625,15 +640,15 @@
             name="backward_full" if full else "backward_light",
         )(where, *operands)
 
-    halves = ()
+    arrived = [()]
     for tick in range(3):
-        halves = hop(backward(halves, False)[0], [(1, 0), (2, 1), (3, 2)])
-        if tick == 0:
-            halves, lefts = lax.optimization_barrier((halves, lefts))
+        arrived.append(hop(backward(arrived[-1], False)[0], [(3 - tick, 2 - tick)]))
+        if tick == 1:
+            arrived[-1], lefts = lax.optimization_barrier((arrived[-1], lefts))
             mates = [swap(part) for part in lefts]
-        if tick == 1:
-            halves, mates = lax.optimization_barrier((halves, mates))
-    slots = backward(halves, True)
+        if tick == 2:
+            arrived[-1], mates = lax.optimization_barrier((arrived[-1], mates))
+    slots = backward(sum(arrived, ()), True)
     rights = deliver(slots[0:3])
 
     *partial, c0, c1, c2, c3 = pl.pallas_call(

time: 205 us -> 193 us (0.941)
  local copies, waits for them, and re-layouts: 5.76 us -> 1.46 us
  starting transfers between devices: 74 us -> 69.7 us
  waiting for transfers between devices: 82.7 us -> 79.6 us
    ppermute x1, waiting for transfers between devices: 0.01 us -> 9.45 us  [shards(): lax.ppermute(piece, ('core', 'xh'), [(2 * c + s, 2 * (1 - s) + c) for c,...]
    ppermute x3, waiting for transfers between devices: 11.4 us -> 3.79 us  [both_ways(): lax.ppermute(values, axes, ring(1))]
    ppermute x6, starting transfers between devices: 12.6 us -> 5.4 us  [hop(): half = lax.ppermute(half, 'y', pairs)]
    ppermute x20 -> x19, starting transfers between devices: 22 us -> 16.9 us  [swap(): return lax.ppermute(values, 'core', [(0, 1), (1, 0)])]
    unnamed x18 -> x16, local copies, waits for them, and re-layouts: 5.15 us -> 0.77 us
    ppermute x2, waiting for transfers between devices: 7.84 us -> 3.56 us  [deliver(): away = lax.ppermute(slots[1], z_axes, z_ring(-1))]
    ppermute x1, starting transfers between devices: 2.8 us -> 6.48 us  [shards(): lax.ppermute(piece, ('core', 'xh'), [(2 * c + s, 2 * s + c) for c, s in p...]
    ppermute x2, waiting for transfers between devices: 0.01 us -> 3.43 us  [deliver(): opposite = lax.ppermute(slots[2], z_axes, z_ring(2))]
  transfers between devices with their start and end apart: 50 -> 49, of which waited for: 28 -> 27; matrix products, arithmetic and copies ran while one was open for 0% -> 0% of each run, Pallas kernels for 0% -> 0%
where the time goes in v3:
time: 193 us
  waiting for transfers between devices  79.6 us (41%)
  starting transfers between devices  69.7 us (36%)
  Pallas kernels  40.6 us (21%)
    ppermute x6, waiting for transfers between devices, hop(): half = lax.ppermute(half, 'y', pairs)  19.3 us
    ppermute x19, starting transfers between devices, swap(): return lax.ppermute(values, 'core', [(0, 1), (1, 0)])  16.9 us
    pallas_call x4, Pallas kernels, backward(): pl.pallas_call(lambda *refs: backward_kernel(not halves, full, *refs), ou...  15 us
    pallas_call x4, Pallas kernels, forward(): pl.pallas_call(lambda *refs: forward_kernel(not halves, full, *refs), out...  13.5 us
    ppermute x4, starting transfers between devices, shards(): lax.ppermute(cells[step], ('y', 'core', 'xh'), stem_pairs(step))  11.8 us
    ppermute x1, waiting for transfers between devices, shards(): lax.ppermute(piece, ('core', 'xh'), [(2 * c + s, 2 * (1 - s) + c) for c,...  9.45 us
    ppermute x3, starting transfers between devices, both_ways(): lax.ppermute(values, axes, ring(1))  8.41 us
    ppermute x1, waiting for transfers between devices, shards(): relay = lax.ppermute(partial[2], x_axes, x_ring(1))  8.2 us
  transfers between devices with their start and end apart: 49, of which 27 were waited for; matrix products, arithmetic and copies ran while one was open for 0% of the time, Pallas kernels for 0%

profile of v3, /device:TPU:25, one launch (start us, length us, event | category | flops | bytes accessed | tf_op | source)
XLA Modules:
  0.0 192.5 jit_solution(9838005479174791897)
XLA Ops:
  0.9 0.7 stack.47.where.refs_0_
  1.5 3.2 %pack.1 = (f32[208,768]{1,0:T(8,128)}, f32[64,768]{1,0:T(8,128)}, f32[64,384]{1,0:T(8,128)}, f32[8,768]{1,0:T(8,128)}) custom-call(s32[11]{0:T(128)} %stack.47.where.refs_0_, bf16[1,720,360]{2,1,0:T(8,128)(2,1)} %refs_14_.1, bf16[1,360,360]{2,1,0:T(8,128)(2,1)} %refs_15_.1, bf16[1,360,720]{2,1,0:T(8,128)(2,1)} %refs_16_.1, bf16[1,9,360]{2,1,0:T(8,128)(2,1)} %refs_3_.1, ...), custom_call_target="tpu_custom_call" | custom-call | tf_op jit(solution)/shard_map/pack/pallas_call | solution.py:539
  4.7 3.8 %collective-permute-start = (f32[64,768]{1,0:T(8,128)}, f32[64,768]{1,0:T(8,128)S(1)}, u32[]{:S(2)}, u32[]{:S(2)}) collective-permute-start(f32[64,768]{1,0:T(8,128)} %get-tuple-element.66), channel_id=1, source_target_pairs={{0,8},{2,26},{8,16},{10,2},{16,24},{18,10},{24,0},{26,18},{1,9},{3... | collective-permute-start | bytes 589832 | tf_op jit(solution)/shard_map/ppermute | solution.py:557
  8.6 3.8 %collective-permute-done.first = f32[64,768]{1,0:T(8,128)S(1)} collective-permute-done((f32[64,768]{1,0:T(8,128)}, f32[64,768]{1,0:T(8,128)S(1)}, u32[]{:S(2)}, u32[]{:S(2)}) %collective-permute-start) | collective-permute-done | bytes 196640 | tf_op jit(solution)/shard_map/ppermute | solution.py:557
  12.3 3.3 %collective-permute-start.2 = (f32[64,768]{1,0:T(8,128)S(1)}, f32[64,768]{1,0:T(8,128)S(1)}, u32[]{:S(2)}, u32[]{:S(2)}) collective-permute-start(f32[64,768]{1,0:T(8,128)S(1)} %collective-permute-done.first), channel_id=1, source_target_pairs={{0,8},{2,26},{8,16},{10,2},{16,24},{18,10},{24,0},{26,18},{1,9},{3... | collective-permute-start | bytes 589832 | tf_op jit(solution)/shard_map/ppermute | solution.py:560
  15.7 2.6 %collective-permute-done.2.third = f32[64,768]{1,0:T(8,128)S(1)} collective-permute-done((f32[64,768]{1,0:T(8,128)S(1)}, f32[64,768]{1,0:T(8,128)S(1)}, u32[]{:S(2)}, u32[]{:S(2)}) %collective-permute-start.2) | collective-permute-done | bytes 196640 | tf_op jit(solution)/shard_map/ppermute | solution.py:560
  18.3 3.1 %collective-permute-start.3 = (f32[208,768]{1,0:T(8,128)}, f32[208,768]{1,0:T(8,128)S(1)}, u32[]{:S(2)}, u32[]{:S(2)}) collective-permute-start(f32[208,768]{1,0:T(8,128)} %get-tuple-element.68), channel_id=1, source_target_pairs={{0,8},{2,26},{8,16},{10,2},{16,24},{18,10},{24,0},{26,18},{1,9},{3... | collective-permute-start | bytes 1916936 | tf_op jit(solution)/shard_map/ppermute | solution.py:557
  21.4 1.3 collective-permute-start.6
  22.7 1.5 collective-permute-start.5
  24.2 1.5 collective-permute-start.8
  25.7 9.5 %collective-permute-done.8.refs_2_.refs_4_.refs_8_.cross_ref = f32[64,384]{1,0:T(8,128)S(1)} collective-permute-done((f32[64,384]{1,0:T(8,128)}, f32[64,384]{1,0:T(8,128)S(1)}, u32[]{:S(2)}, u32[]{:S(2)}) %collective-permute-start.8) | collective-permute-done | bytes 98336 | tf_op jit(solution)/shard_map/ppermute | solution.py:554
  35.2 6.5 %collective-permute-start.7 = (f32[64,384]{1,0:T(8,128)}, f32[64,384]{1,0:T(8,128)S(1)}, u32[]{:S(2)}, u32[]{:S(2)}) collective-permute-start(f32[64,384]{1,0:T(8,128)} %get-tuple-element.72), channel_id=1, source_target_pairs={{0,0},{1,2},{2,1},{3,3},{4,4},{5,6},{6,5},{7,7},{8,8},{9,10},{10,9... | collective-permute-start | bytes 294920 | tf_op jit(solution)/shard_map/ppermute | solution.py:553
  41.6 2.5 %collective-permute-done.7.refs_1_.refs_3_.refs_7_.same_ref = f32[64,384]{1,0:T(8,128)S(1)} collective-permute-done((f32[64,384]{1,0:T(8,128)}, f32[64,384]{1,0:T(8,128)S(1)}, u32[]{:S(2)}, u32[]{:S(2)}) %collective-permute-start.7) | collective-permute-done | bytes 98336 | tf_op jit(solution)/shard_map/ppermute | solution.py:553
  44.2 1.5 collective-permute-start.9
  46.2 1.9 collective-permute-start.10
  48.6 5.2 %collective-permute-done.9.refs_2_ = f32[208,768]{1,0:T(8,128)S(1)} collective-permute-done((f32[208,768]{1,0:T(8,128)S(1)}, f32[208,768]{1,0:T(8,128)S(1)}, u32[]{:S(2)}, u32[]{:S(2)}) %collective-permute-start.9) | collective-permute-done | bytes 639008 | tf_op jit(solution)/shard_map/ppermute | solution.py:575
  54.3 0.9 collective-permute-done.10.refs_6_
  55.2 2.1 %collective-permute-start.17 = (f32[192,768]{1,0:T(8,128)S(1)}, f32[192,768]{1,0:T(8,128)S(1)}, u32[]{:S(2)}, u32[]{:S(2)}) collective-permute-start(f32[192,768]{1,0:T(8,128)S(1)} %collective-permute-done.10.refs_6_), channel_id=1, source_target_pairs={{0,2},{2,0},{1,3},{3,1},{4,6},{6,4},{5,7},{7,5},{8,10},{10,8},{9,1... | collective-permute-start | bytes 1769480 | tf_op jit(solution)/shard_map/ppermute | solution.py:530
  57.3 1.6 collective-permute-done.17.refs_13_
  59.0 0.7 copy-done.7
  59.7 2.6 %columns.1 = (bf16[4,720,360]{2,1,0:T(8,128)(2,1)S(1)}, bf16[4,360,360]{2,1,0:T(8,128)(2,1)S(1)}, bf16[4,360,720]{2,1,0:T(8,128)(2,1)S(1)}, f32[4,8,768]{2,1,0:T(8,128)S(1)}) custom-call(s32[11]{0:T(128)S(1)} %copy-done.6, f32[208,768]{1,0:T(8,128)S(1)} %collective-permute-done.3.refs_0_, f32[208,768]{1,0:T(8,128)S(1)} %collective-permute-done.4.refs_1_, ...), custom_call_target="tpu_custom_call" | custom-call | tf_op jit(solution)/shard_map/columns/pallas_call | solution.py:580
  62.3 3.2 %forward_light.3 = f32[96,384]{1,0:T(8,128)S(1)} custom-call(s32[11]{0:T(128)S(1)} %copy-done.6, f32[64,384]{1,0:T(8,128)S(1)} %collective-permute-done.7.refs_1_.refs_3_.refs_7_.same_ref, f32[64,384]{1,0:T(8,128)S(1)} %collective-permute-done.8.refs_2_.refs_4_.refs_8_.cross_ref, ...), custom_call_target="tpu_custom_call" | custom-call | tf_op jit(solution)/shard_map/forward_light/pallas_call | solution.py:597
  65.5 0.7 collective-permute-start.18
  66.8 1.0 collective-permute-done.19.refs_2_
  67.8 3.2 %forward_light.4 = f32[96,384]{1,0:T(8,128)S(1)} custom-call(s32[11]{0:T(128)S(1)} %copy-done.6, f32[96,384]{1,0:T(8,128)S(1)} %collective-permute-done.18.refs_1_, f32[96,384]{1,0:T(8,128)S(1)} %collective-permute-done.19.refs_2_, f32[64,384]{1,0:T(8,128)S(1)} %collective-permute-done.7.refs_1_.refs_3_.refs_7_.same_ref, ...), custom_call_target="tpu_custom_call" | custom-call | tf_op jit(solution)/shard_map/forward_light/pallas_call | solution.py:597
  71.1 0.7 collective-permute-start.20
  72.2 1.0 collective-permute-done.21.refs_2_.refs_4_
  73.2 3.2 %forward_light.5 = f32[96,384]{1,0:T(8,128)S(1)} custom-call(s32[11]{0:T(128)S(1)} %copy-done.6, f32[96,384]{1,0:T(8,128)S(1)} %collective-permute-done.20.refs_1_.refs_3_, f32[96,384]{1,0:T(8,128)S(1)} %collective-permute-done.21.refs_2_.refs_4_, f32[64,384]{1,0:T(8,128)S(1)} %collective-permute-done.7.refs_1_.refs_3_.refs_7_.same_ref, ...), custom_call_target="tpu_custom_call" | custom-call | tf_op jit(solution)/shard_map/forward_light/pallas_call | solution.py:597
  76.5 1.4 collective-permute-start.22
  77.9 16.3 %collective-permute-done.22.refs_5_ = f32[96,384]{1,0:T(8,128)S(1)} collective-permute-done((f32[96,384]{1,0:T(8,128)S(1)}, f32[96,384]{1,0:T(8,128)S(1)}, u32[]{:S(2)}, u32[]{:S(2)}) %collective-permute-start.22) | collective-permute-done | bytes 147488 | tf_op jit(solution)/shard_map/ppermute | solution.py:608
  94.2 0.9 collective-permute-start.23
  95.1 1.0 collective-permute-done.23.refs_6_
  96.1 3.9 %forward_full.1 = (f32[192,384]{1,0:T(8,128)S(1)}, f32[4,128,360]{2,1,0:T(8,128)S(1)}, f32[4,128,360]{2,1,0:T(8,128)S(1)}, f32[4,32,720]{2,1,0:T(8,128)S(1)}, f3...) custom-call(s32[11]{0:T(128)S(1)} %copy-done.6, ...), custom_call_target="tpu_custom_call" | custom-call | tf_op jit(solution)/shard_map/forward_full/pallas_call | solution.py:597
  100.0 1.8 head.1.refs_1_.refs_7_
  101.8 3.5 %backward_light.3 = f32[96,384]{1,0:T(8,128)S(1)} custom-call(s32[11]{0:T(128)S(1)} %copy-done.6, f32[192,384]{1,0:T(8,128)S(1)} %head.1.refs_1_.refs_7_, f32[4,128,360]{2,1,0:T(8,128)S(1)} %get-tuple-element.87.refs_2_.refs_3_.refs_8_, f32[4,32,720]{2,1,0:T(8,128)S(1)} %get-tuple-element.88.refs_3_.refs_4_.refs_9_, ...), custom_call_target="tpu_custom_call" | custom-call | tf_op jit(solution)/shard_map/backward_light/pallas_call | solution.py:633
  105.3 1.3 collective-permute-start.24
  106.6 3.0 %collective-permute-done.24.refs_1_ = f32[96,384]{1,0:T(8,128)S(1)} collective-permute-done((f32[96,384]{1,0:T(8,128)S(1)}, f32[96,384]{1,0:T(8,128)S(1)}, u32[]{:S(2)}, u32[]{:S(2)}) %collective-permute-start.24) | collective-permute-done | bytes 147488 | tf_op jit(solution)/shard_map/ppermute | solution.py:608
  109.6 1.1 collective-permute-start.25
  110.7 1.0 collective-permute-done.25.refs_2_
  111.7 3.5 %backward_light.4 = f32[96,384]{1,0:T(8,128)S(1)} custom-call(s32[11]{0:T(128)S(1)} %copy-done.6, f32[96,384]{1,0:T(8,128)S(1)} %collective-permute-done.24.refs_1_, f32[96,384]{1,0:T(8,128)S(1)} %collective-permute-done.25.refs_2_, f32[4,128,360]{2,1,0:T(8,128)S(1)} %get-tuple-element.87.refs_2_.refs_3_.refs_8_, ...), custom_call_target="tpu_custom_call" | custom-call | tf_op jit(solution)/shard_map/backward_light/pallas_call | solution.py:633
  115.1 0.7 collective-permute-start.26
  115.8 2.2 %collective-permute-start.28 = (f32[112,384]{1,0:T(8,128)S(1)}, f32[112,384]{1,0:T(8,128)S(1)}, u32[]{:S(2)}, u32[]{:S(2)}) collective-permute-start(f32[112,384]{1,0:T(8,128)S(1)} %get-tuple-element.89), channel_id=1, source_target_pairs={{0,8},{2,26},{8,16},{10,2},{16,24},{18,10},{24,0},{26,18},{1,9},{3... | collective-permute-start | bytes 516104 | tf_op jit(solution)/shard_map/ppermute | solution.py:533
  118.1 1.5 collective-permute-start.30
  119.6 1.2 collective-permute-start.27
  120.7 3.6 %collective-permute-done.29.l2 = f32[112,384]{1,0:T(8,128)S(1)} collective-permute-done((f32[112,384]{1,0:T(8,128)S(1)}, f32[112,384]{1,0:T(8,128)S(1)}, u32[]{:S(2)}, u32[]{:S(2)}) %collective-permute-start.29) | collective-permute-done | bytes 172064 | tf_op jit(solution)/shard_map/ppermute | solution.py:534
  124.3 3.4 %collective-permute-done.30.l3 = f32[112,384]{1,0:T(8,128)S(1)} collective-permute-done((f32[112,384]{1,0:T(8,128)S(1)}, f32[112,384]{1,0:T(8,128)S(1)}, u32[]{:S(2)}, u32[]{:S(2)}) %collective-permute-start.30) | collective-permute-done | bytes 172064 | tf_op jit(solution)/shard_map/ppermute | solution.py:535
  127.7 3.5 %backward_light.5 = f32[96,384]{1,0:T(8,128)S(1)} custom-call(s32[11]{0:T(128)S(1)} %copy-done.6, f32[96,384]{1,0:T(8,128)S(1)} %collective-permute-done.26.refs_1_.refs_3_, f32[96,384]{1,0:T(8,128)S(1)} %collective-permute-done.27.refs_2_.refs_4_, f32[4,128,360]{2,1,0:T(8,128)S(1)} %get-tuple-element.87.refs_2_.refs_3_.refs_8_, ...), custom_call_target="tpu_custom_call" | custom-call | tf_op jit(solution)/shard_map/backward_light/pallas_call | solution.py:633
  131.9 0.9 collective-permute-start.33
  134.7 4.6 %backward_full.1 = (f32[136,384]{1,0:T(8,128)S(1)}, f32[136,384]{1,0:T(8,128)S(1)}, f32[136,384]{1,0:T(8,128)S(1)}, f32[240,384]{1,0:T(8,128)S(1)}, f32[16,384]{1,0:T(8,128)S(1)}) custom-call(s32[11]{0:T(128)S(1)} %copy-done.6, f32[96,384]{1,0:T(8,128)S(1)} %collective-permute-done.24.refs_1_, f32[96,384]{1,0:T(8,128)S(1)} %collective-permute-done.25.refs_2_, ...), custom_call_target="tpu_custom_call" | custom-call | tf_op jit(solution)/shard_map/backward_full/pallas_call | solution.py:633
  139.3 1.3 collective-permute-start.36
  140.8 1.0 collective-permute-start.38
  141.8 3.9 %collective-permute-done.36.r1 = f32[136,384]{1,0:T(8,128)S(1)} collective-permute-done((f32[136,384]{1,0:T(8,128)S(1)}, f32[136,384]{1,0:T(8,128)S(1)}, u32[]{:S(2)}, u32[]{:S(2)}) %collective-permute-start.36) | collective-permute-done | bytes 208928 | tf_op jit(solution)/shard_map/ppermute | solution.py:533
  145.8 7.1 %collective-permute-start.39 = (f32[136,384]{1,0:T(8,128)S(1)}, f32[136,384]{1,0:T(8,128)S(1)}, u32[]{:S(2)}, u32[]{:S(2)}) collective-permute-start(f32[136,384]{1,0:T(8,128)S(1)} %collective-permute-done.36.r1), channel_id=1, source_target_pairs={{0,2},{2,0},{1,3},{3,1},{4,6},{6,4},{5,7},{7,5},{8,10},{10,8},{9,1... | collective-permute-start | bytes 626696 | tf_op jit(solution)/shard_map/ppermute | solution.py:530
  154.6 3.1 %weight_grads.1 = (f32[256,384]{1,0:T(8,128)S(1)}, f32[256,384]{1,0:T(8,128)S(1)}, f32[256,384]{1,0:T(8,128)S(1)}, f32[256,384]{1,0:T(8,128)S(1)}, f32[4,4,384]{...) custom-call(s32[11]{0:T(128)S(1)} %copy-done.6, ...), custom_call_target="tpu_custom_call" | custom-call | tf_op jit(solution)/shard_map/weight_grads/pallas_call | solution.py:654
  157.7 3.1 %collective-permute-start.42 = (f32[256,384]{1,0:T(8,128)S(1)}, f32[256,384]{1,0:T(8,128)S(1)}, u32[]{:S(2)}, u32[]{:S(2)}) collective-permute-start(f32[256,384]{1,0:T(8,128)S(1)} %get-tuple-element.110), channel_id=1, source_target_pairs={{0,4},{2,7},{4,1},{6,2},{1,5},{3,6},{5,0},{7,3},{8,12},{10,15},{12... | collective-permute-start | bytes 1179656 | tf_op jit(solution)/shard_map/ppermute | solution.py:663
  160.8 8.2 %collective-permute-done.42.second = f32[256,384]{1,0:T(8,128)S(1)} collective-permute-done((f32[256,384]{1,0:T(8,128)S(1)}, f32[256,384]{1,0:T(8,128)S(1)}, u32[]{:S(2)}, u32[]{:S(2)}) %collective-permute-start.42) | collective-permute-done | bytes 393248 | tf_op jit(solution)/shard_map/ppermute | solution.py:663
  169.0 1.6 collective-permute-done.43.far
  170.7 1.9 collective-permute-start.44
  172.6 4.4 %collective-permute-start.45 = (f32[4,4,384]{2,1,0:T(4,128)S(1)}, f32[4,4,384]{2,1,0:T(4,128)S(1)}, u32[]{:S(2)}, u32[]{:S(2)}) collective-permute-start(f32[4,4,384]{2,1,0:T(4,128)S(1)} %get-tuple-element.118), channel_id=1, source_target_pairs={{0,0},{1,2},{2,1},{3,3},{32,32},{33,34},{34,33},{35,35},{64,64},{6... | collective-permute-start | bytes 73736 | tf_op jit(solution)/shard_map/ppermute | solution.py:679
  176.9 3.8 %collective-permute-start.46 = (f32[4,4,384]{2,1,0:T(4,128)S(1)}, f32[4,4,384]{2,1,0:T(4,128)S(1)}, u32[]{:S(2)}, u32[]{:S(2)}) collective-permute-start(f32[4,4,384]{2,1,0:T(4,128)S(1)} %get-tuple-element.119), channel_id=1, source_target_pairs={{0,32},{1,34},{2,33},{3,35},{32,64},{33,66},{34,65},{35,67},{64,96... | collective-permute-start | bytes 73736 | tf_op jit(solution)/shard_map/ppermute | solution.py:679
  180.7 3.6 %collective-permute-start.47 = (f32[4,4,384]{2,1,0:T(4,128)S(1)}, f32[4,4,384]{2,1,0:T(4,128)S(1)}, u32[]{:S(2)}, u32[]{:S(2)}) collective-permute-start(f32[4,4,384]{2,1,0:T(4,128)S(1)} %get-tuple-element.120), channel_id=1, source_target_pairs={{0,64},{1,66},{2,65},{3,67},{32,96},{33,98},{34,97},{35,99},{64,0}... | collective-permute-start | bytes 73736 | tf_op jit(solution)/shard_map/ppermute | solution.py:679
  184.3 3.6 %collective-permute-done.47.c2 = f32[4,4,384]{2,1,0:T(4,128)S(1)} collective-permute-done((f32[4,4,384]{2,1,0:T(4,128)S(1)}, f32[4,4,384]{2,1,0:T(4,128)S(1)}, u32[]{:S(2)}, u32[]{:S(2)}) %collective-permute-start.47) | collective-permute-done | bytes 24608 | tf_op jit(solution)/shard_map/ppermute | solution.py:679
  187.9 3.3 %collective-permute-done.48.c3 = f32[4,4,384]{2,1,0:T(4,128)S(1)} collective-permute-done((f32[4,4,384]{2,1,0:T(4,128)S(1)}, f32[4,4,384]{2,1,0:T(4,128)S(1)}, u32[]{:S(2)}, u32[]{:S(2)}) %collective-permute-start.48) | collective-permute-done | bytes 24608 | tf_op jit(solution)/shard_map/ppermute | solution.py:679
  191.2 1.3 final.1
  (66 shorter events, 7.4 us)
Async XLA Ops:
  0.6 58.3 %copy-start.1 = (bf16[1,360,720]{2,1,0:T(8,128)(2,1)S(1)}, bf16[1,360,720]{2,1,0:T(8,128)(2,1)}, u32[]{:S(2)}) copy-start(bf16[1,360,720]{2,1,0:T(8,128)(2,1)} %refs_16_.1) | copy-start | bytes 1555204
  0.6 58.3 %copy-start.2 = (bf16[1,360,360]{2,1,0:T(8,128)(2,1)S(1)}, bf16[1,360,360]{2,1,0:T(8,128)(2,1)}, u32[]{:S(2)}) copy-start(bf16[1,360,360]{2,1,0:T(8,128)(2,1)} %refs_15_.1) | copy-start | bytes 777604
  0.7 58.3 %copy-start = (bf16[1,720,360]{2,1,0:T(8,128)(2,1)S(1)}, bf16[1,720,360]{2,1,0:T(8,128)(2,1)}, u32[]{:S(2)}) copy-start(bf16[1,720,360]{2,1,0:T(8,128)(2,1)} %refs_14_.1) | copy-start | bytes 1555204
  1.5 57.4 %copy-start.6 = (s32[11]{0:T(128)S(1)}, s32[11]{0:T(128)}, u32[]{:S(2)}) copy-start(s32[11]{0:T(128)} %stack.47.where.refs_0_) | copy-start | bytes 136
  4.7 7.6 %collective-permute-start = (f32[64,768]{1,0:T(8,128)}, f32[64,768]{1,0:T(8,128)S(1)}, u32[]{:S(2)}, u32[]{:S(2)}) collective-permute-start(f32[64,768]{1,0:T(8,128)} %get-tuple-element.66), channel_id=1, source_target_pairs={{0,8},{2,26},{8,16},{10,2},{16,24},{18,10},{24,0},{26,18},{1,9},{3... | collective-permute-start | bytes 589832 | tf_op jit(solution)/shard_map/ppermute | solution.py:557
  8.6 7.1 %collective-permute-start.1 = (f32[64,768]{1,0:T(8,128)}, f32[64,768]{1,0:T(8,128)S(1)}, u32[]{:S(2)}, u32[]{:S(2)}) collective-permute-start(f32[64,768]{1,0:T(8,128)} %get-tuple-element.66), channel_id=1, source_target_pairs={{0,24},{2,10},{8,0},{10,18},{16,8},{18,26},{24,16},{26,2},{1,25},{... | collective-permute-start | bytes 589832 | tf_op jit(solution)/shard_map/ppermute | solution.py:557
  12.3 5.9 %collective-permute-start.2 = (f32[64,768]{1,0:T(8,128)S(1)}, f32[64,768]{1,0:T(8,128)S(1)}, u32[]{:S(2)}, u32[]{:S(2)}) collective-permute-start(f32[64,768]{1,0:T(8,128)S(1)} %collective-permute-done.first), channel_id=1, source_target_pairs={{0,8},{2,26},{8,16},{10,2},{16,24},{18,10},{24,0},{26,18},{1,9},{3... | collective-permute-start | bytes 589832 | tf_op jit(solution)/shard_map/ppermute | solution.py:560
  18.3 25.9 %collective-permute-start.4 = (f32[208,768]{1,0:T(8,128)}, f32[208,768]{1,0:T(8,128)S(1)}, u32[]{:S(2)}, u32[]{:S(2)}) collective-permute-start(f32[208,768]{1,0:T(8,128)} %get-tuple-element.68), channel_id=1, source_target_pairs={{0,24},{2,10},{8,0},{10,18},{16,8},{18,26},{24,16},{26,2},{1,25},{... | collective-permute-start | bytes 1916936 | tf_op jit(solution)/shard_map/ppermute | solution.py:557
  18.3 25.9 %collective-permute-start.3 = (f32[208,768]{1,0:T(8,128)}, f32[208,768]{1,0:T(8,128)S(1)}, u32[]{:S(2)}, u32[]{:S(2)}) collective-permute-start(f32[208,768]{1,0:T(8,128)} %get-tuple-element.68), channel_id=1, source_target_pairs={{0,8},{2,26},{8,16},{10,2},{16,24},{18,10},{24,0},{26,18},{1,9},{3... | collective-permute-start | bytes 1916936 | tf_op jit(solution)/shard_map/ppermute | solution.py:557
  21.4 22.7 %collective-permute-start.6 = (f32[192,768]{1,0:T(8,128)S(1)}, f32[192,768]{1,0:T(8,128)S(1)}, u32[]{:S(2)}, u32[]{:S(2)}) collective-permute-start(f32[192,768]{1,0:T(8,128)S(1)} %join_quarters.1.refs_3_), channel_id=1, source_target_pairs={{0,5},{2,6},{4,0},{6,3},{1,4},{3,7},{5,1},{7,2},{8,13},{10,14},{12... | collective-permute-start | bytes 1769480 | tf_op jit(solution)/shard_map/ppermute | solution.py:557
  22.7 21.4 %collective-permute-start.5 = (f32[192,768]{1,0:T(8,128)S(1)}, f32[192,768]{1,0:T(8,128)S(1)}, u32[]{:S(2)}, u32[]{:S(2)}) collective-permute-start(f32[192,768]{1,0:T(8,128)S(1)} %join_quarters.1.refs_3_), channel_id=1, source_target_pairs={{0,4},{2,7},{4,1},{6,2},{1,5},{3,6},{5,0},{7,3},{8,12},{10,15},{12... | collective-permute-start | bytes 1769480 | tf_op jit(solution)/shard_map/ppermute | solution.py:557
  24.2 11.0 %collective-permute-start.8 = (f32[64,384]{1,0:T(8,128)}, f32[64,384]{1,0:T(8,128)S(1)}, u32[]{:S(2)}, u32[]{:S(2)}) collective-permute-start(f32[64,384]{1,0:T(8,128)} %get-tuple-element.72), channel_id=1, source_target_pairs={{0,2},{1,0},{2,3},{3,1},{4,6},{5,4},{6,7},{7,5},{8,10},{9,8},{10,1... | collective-permute-start | bytes 294920 | tf_op jit(solution)/shard_map/ppermute | solution.py:554
  35.2 9.0 %collective-permute-start.7 = (f32[64,384]{1,0:T(8,128)}, f32[64,384]{1,0:T(8,128)S(1)}, u32[]{:S(2)}, u32[]{:S(2)}) collective-permute-start(f32[64,384]{1,0:T(8,128)} %get-tuple-element.72), channel_id=1, source_target_pairs={{0,0},{1,2},{2,1},{3,3},{4,4},{5,6},{6,5},{7,7},{8,8},{9,10},{10,9... | collective-permute-start | bytes 294920 | tf_op jit(solution)/shard_map/ppermute | solution.py:553
  44.2 9.6 %collective-permute-start.9 = (f32[208,768]{1,0:T(8,128)S(1)}, f32[208,768]{1,0:T(8,128)S(1)}, u32[]{:S(2)}, u32[]{:S(2)}) collective-permute-start(f32[208,768]{1,0:T(8,128)S(1)} %collective-permute-done.3.refs_0_), channel_id=1, source_target_pairs={{0,8},{2,26},{8,16},{10,2},{16,24},{18,10},{24,0},{26,18},{1,9},{3... | collective-permute-start | bytes 1916936 | tf_op jit(solution)/shard_map/ppermute | solution.py:575
  45.7 2.4 %collective-permute-start.14 = (f32[192,768]{1,0:T(8,128)S(1)}, f32[192,768]{1,0:T(8,128)S(1)}, u32[]{:S(2)}, u32[]{:S(2)}) collective-permute-start(f32[192,768]{1,0:T(8,128)S(1)} %join_quarters.1.refs_3_), channel_id=1, source_target_pairs={{0,2},{2,0},{1,3},{3,1},{4,6},{6,4},{5,7},{7,5},{8,10},{10,8},{9,1... | collective-permute-start | bytes 1769480 | tf_op jit(solution)/shard_map/ppermute | solution.py:530
  45.7 8.1 %collective-permute-start.16 = (f32[192,768]{1,0:T(8,128)S(1)}, f32[192,768]{1,0:T(8,128)S(1)}, u32[]{:S(2)}, u32[]{:S(2)}) collective-permute-start(f32[192,768]{1,0:T(8,128)S(1)} %collective-permute-done.6.refs_5_), channel_id=1, source_target_pairs={{0,2},{2,0},{1,3},{3,1},{4,6},{6,4},{5,7},{7,5},{8,10},{10,8},{9,1... | collective-permute-start | bytes 1769480 | tf_op jit(solution)/shard_map/ppermute | solution.py:530
  46.2 9.0 %collective-permute-start.10 = (f32[192,768]{1,0:T(8,128)S(1)}, f32[192,768]{1,0:T(8,128)S(1)}, u32[]{:S(2)}, u32[]{:S(2)}) collective-permute-start(f32[192,768]{1,0:T(8,128)S(1)} %collective-permute-done.5.refs_4_), channel_id=1, source_target_pairs={{0,4},{2,7},{4,1},{6,2},{1,5},{3,6},{5,0},{7,3},{8,12},{10,15},{12... | collective-permute-start | bytes 1769480 | tf_op jit(solution)/shard_map/ppermute | solution.py:578
  48.1 9.3 %collective-permute-start.12 = (f32[208,768]{1,0:T(8,128)S(1)}, f32[208,768]{1,0:T(8,128)S(1)}, u32[]{:S(2)}, u32[]{:S(2)}) collective-permute-start(f32[208,768]{1,0:T(8,128)S(1)} %collective-permute-done.4.refs_1_), channel_id=1, source_target_pairs={{0,2},{2,0},{1,3},{3,1},{4,6},{6,4},{5,7},{7,5},{8,10},{10,8},{9,1... | collective-permute-start | bytes 1916936 | tf_op jit(solution)/shard_map/ppermute | solution.py:530
  48.1 9.2 %collective-permute-start.11 = (f32[208,768]{1,0:T(8,128)S(1)}, f32[208,768]{1,0:T(8,128)S(1)}, u32[]{:S(2)}, u32[]{:S(2)}) collective-permute-start(f32[208,768]{1,0:T(8,128)S(1)} %collective-permute-done.3.refs_0_), channel_id=1, source_target_pairs={{0,2},{2,0},{1,3},{3,1},{4,6},{6,4},{5,7},{7,5},{8,10},{10,8},{9,1... | collective-permute-start | bytes 1916936 | tf_op jit(solution)/shard_map/ppermute | solution.py:530
  53.8 5.1 %collective-permute-start.13 = (f32[208,768]{1,0:T(8,128)S(1)}, f32[208,768]{1,0:T(8,128)S(1)}, u32[]{:S(2)}, u32[]{:S(2)}) collective-permute-start(f32[208,768]{1,0:T(8,128)S(1)} %collective-permute-done.9.refs_2_), channel_id=1, source_target_pairs={{0,2},{2,0},{1,3},{3,1},{4,6},{6,4},{5,7},{7,5},{8,10},{10,8},{9,1... | collective-permute-start | bytes 1916936 | tf_op jit(solution)/shard_map/ppermute | solution.py:530
  53.8 3.5 %collective-permute-start.15 = (f32[192,768]{1,0:T(8,128)S(1)}, f32[192,768]{1,0:T(8,128)S(1)}, u32[]{:S(2)}, u32[]{:S(2)}) collective-permute-start(f32[192,768]{1,0:T(8,128)S(1)} %collective-permute-done.5.refs_4_), channel_id=1, source_target_pairs={{0,2},{2,0},{1,3},{3,1},{4,6},{6,4},{5,7},{7,5},{8,10},{10,8},{9,1... | collective-permute-start | bytes 1769480 | tf_op jit(solution)/shard_map/ppermute | solution.py:530
  55.2 3.7 %collective-permute-start.17 = (f32[192,768]{1,0:T(8,128)S(1)}, f32[192,768]{1,0:T(8,128)S(1)}, u32[]{:S(2)}, u32[]{:S(2)}) collective-permute-start(f32[192,768]{1,0:T(8,128)S(1)} %collective-permute-done.10.refs_6_), channel_id=1, source_target_pairs={{0,2},{2,0},{1,3},{3,1},{4,6},{6,4},{5,7},{7,5},{8,10},{10,8},{9,1... | collective-permute-start | bytes 1769480 | tf_op jit(solution)/shard_map/ppermute | solution.py:530
  59.0 0.7 copy-start.7
  65.5 0.7 collective-permute-start.18
  66.2 1.7 collective-permute-start.19
  71.1 0.7 collective-permute-start.20
  71.8 1.5 collective-permute-start.21
  76.4 23.6 %copy-start.3 = (bf16[720,512]{1,0:T(8,128)(2,1)S(1)}, bf16[720,512]{1,0:T(8,128)(2,1)}, u32[]{:S(2)}) copy-start(bf16[720,512]{1,0:T(8,128)(2,1)} %two_ref.1) | copy-start | bytes 2211844
  76.4 23.6 %copy-start.4 = (bf16[360,512]{1,0:T(8,128)(2,1)S(1)}, bf16[360,512]{1,0:T(8,128)(2,1)}, u32[]{:S(2)}) copy-start(bf16[360,512]{1,0:T(8,128)(2,1)} %one_ref.1) | copy-start | bytes 1105924
  76.5 23.6 %copy-start.5 = (bf16[512,150]{0,1:T(8,128)(2,1)S(1)}, bf16[512,150]{0,1:T(8,128)(2,1)}, u32[]{:S(2)}) copy-start(bf16[512,150]{0,1:T(8,128)(2,1)} %param.21) | copy-start | bytes 460804
  76.5 17.7 %collective-permute-start.22 = (f32[96,384]{1,0:T(8,128)S(1)}, f32[96,384]{1,0:T(8,128)S(1)}, u32[]{:S(2)}, u32[]{:S(2)}) collective-permute-start(f32[96,384]{1,0:T(8,128)S(1)} %forward_light.5), channel_id=1, source_target_pairs={{64,96},{65,97},{66,98},{67,99},{68,100},{69,101},{70,102},{71,103... | collective-permute-start | bytes 442376 | tf_op jit(solution)/shard_map/ppermute | solution.py:608
  94.2 1.9 collective-permute-start.23
  105.3 4.3 %collective-permute-start.24 = (f32[96,384]{1,0:T(8,128)S(1)}, f32[96,384]{1,0:T(8,128)S(1)}, u32[]{:S(2)}, u32[]{:S(2)}) collective-permute-start(f32[96,384]{1,0:T(8,128)S(1)} %backward_light.3), channel_id=1, source_target_pairs={{96,64},{97,65},{98,66},{99,67},{100,68},{101,69},{102,70},{103,71... | collective-permute-start | bytes 442376 | tf_op jit(solution)/shard_map/ppermute | solution.py:608
  109.6 2.1 %collective-permute-start.25 = (f32[96,384]{1,0:T(8,128)S(1)}, f32[96,384]{1,0:T(8,128)S(1)}, u32[]{:S(2)}, u32[]{:S(2)}) collective-permute-start(f32[96,384]{1,0:T(8,128)S(1)} %collective-permute-done.24.refs_1_), channel_id=1, source_target_pairs={{0,2},{2,0},{1,3},{3,1},{4,6},{6,4},{5,7},{7,5},{8,10},{10,8},{9,1... | collective-permute-start | bytes 442376 | tf_op jit(solution)/shard_map/ppermute | solution.py:530
  115.1 4.4 %collective-permute-start.26 = (f32[96,384]{1,0:T(8,128)S(1)}, f32[96,384]{1,0:T(8,128)S(1)}, u32[]{:S(2)}, u32[]{:S(2)}) collective-permute-start(f32[96,384]{1,0:T(8,128)S(1)} %backward_light.4), channel_id=1, source_target_pairs={{64,32},{65,33},{66,34},{67,35},{68,36},{69,37},{70,38},{71,39},{7... | collective-permute-start | bytes 442376 | tf_op jit(solution)/shard_map/ppermute | solution.py:608
  115.8 4.9 %collective-permute-start.28 = (f32[112,384]{1,0:T(8,128)S(1)}, f32[112,384]{1,0:T(8,128)S(1)}, u32[]{:S(2)}, u32[]{:S(2)}) collective-permute-start(f32[112,384]{1,0:T(8,128)S(1)} %get-tuple-element.89), channel_id=1, source_target_pairs={{0,8},{2,26},{8,16},{10,2},{16,24},{18,10},{24,0},{26,18},{1,9},{3... | collective-permute-start | bytes 516104 | tf_op jit(solution)/shard_map/ppermute | solution.py:533
  118.1 6.2 %collective-permute-start.29 = (f32[112,384]{1,0:T(8,128)S(1)}, f32[112,384]{1,0:T(8,128)S(1)}, u32[]{:S(2)}, u32[]{:S(2)}) collective-permute-start(f32[112,384]{1,0:T(8,128)S(1)} %get-tuple-element.90), channel_id=1, source_target_pairs={{0,24},{2,10},{8,0},{10,18},{16,8},{18,26},{24,16},{26,2},{1,25},{... | collective-permute-start | bytes 516104 | tf_op jit(solution)/shard_map/ppermute | solution.py:534
  118.1 9.6 %collective-permute-start.30 = (f32[112,384]{1,0:T(8,128)S(1)}, f32[112,384]{1,0:T(8,128)S(1)}, u32[]{:S(2)}, u32[]{:S(2)}) collective-permute-start(f32[112,384]{1,0:T(8,128)S(1)} %get-tuple-element.91), channel_id=1, source_target_pairs={{0,16},{2,18},{8,24},{10,26},{16,0},{18,2},{24,8},{26,10},{1,17},{... | collective-permute-start | bytes 516104 | tf_op jit(solution)/shard_map/ppermute | solution.py:535
  119.6 8.2 %collective-permute-start.27 = (f32[96,384]{1,0:T(8,128)S(1)}, f32[96,384]{1,0:T(8,128)S(1)}, u32[]{:S(2)}, u32[]{:S(2)}) collective-permute-start(f32[96,384]{1,0:T(8,128)S(1)} %collective-permute-done.26.refs_1_.refs_3_), channel_id=1, source_target_pairs={{0,2},{2,0},{1,3},{3,1},{4,6},{6,4},{5,7},{7,5},{8,10},{10,8},{9,1... | collective-permute-start | bytes 442376 | tf_op jit(solution)/shard_map/ppermute | solution.py:530
  131.2 2.1 %collective-permute-start.31 = (f32[96,384]{1,0:T(8,128)S(1)}, f32[96,384]{1,0:T(8,128)S(1)}, u32[]{:S(2)}, u32[]{:S(2)}) collective-permute-start(f32[96,384]{1,0:T(8,128)S(1)} %backward_light.5), channel_id=1, source_target_pairs={{32,0},{33,1},{34,2},{35,3},{36,4},{37,5},{38,6},{39,7},{40,8},{41... | collective-permute-start | bytes 442376 | tf_op jit(solution)/shard_map/ppermute | solution.py:608
  131.9 2.0 %collective-permute-start.33 = (f32[112,384]{1,0:T(8,128)S(1)}, f32[112,384]{1,0:T(8,128)S(1)}, u32[]{:S(2)}, u32[]{:S(2)}) collective-permute-start(f32[112,384]{1,0:T(8,128)S(1)} %collective-permute-done.28.l1), channel_id=1, source_target_pairs={{0,2},{2,0},{1,3},{3,1},{4,6},{6,4},{5,7},{7,5},{8,10},{10,8},{9,1... | collective-permute-start | bytes 516104 | tf_op jit(solution)/shard_map/ppermute | solution.py:530
  132.8 1.4 collective-permute-start.34
  132.9 1.6 collective-permute-start.35
  133.3 1.4 collective-permute-start.32
  139.3 6.5 %collective-permute-start.36 = (f32[136,384]{1,0:T(8,128)S(1)}, f32[136,384]{1,0:T(8,128)S(1)}, u32[]{:S(2)}, u32[]{:S(2)}) collective-permute-start(f32[136,384]{1,0:T(8,128)S(1)} %get-tuple-element.104), channel_id=1, source_target_pairs={{0,8},{2,26},{8,16},{10,2},{16,24},{18,10},{24,0},{26,18},{1,9},{3... | collective-permute-start | bytes 626696 | tf_op jit(solution)/shard_map/ppermute | solution.py:533
  140.6 12.3 %collective-permute-start.37 = (f32[136,384]{1,0:T(8,128)S(1)}, f32[136,384]{1,0:T(8,128)S(1)}, u32[]{:S(2)}, u32[]{:S(2)}) collective-permute-start(f32[136,384]{1,0:T(8,128)S(1)} %get-tuple-element.105), channel_id=1, source_target_pairs={{0,24},{2,10},{8,0},{10,18},{16,8},{18,26},{24,16},{26,2},{1,25},{... | collective-permute-start | bytes 626696 | tf_op jit(solution)/shard_map/ppermute | solution.py:534
  140.8 12.1 %collective-permute-start.38 = (f32[136,384]{1,0:T(8,128)S(1)}, f32[136,384]{1,0:T(8,128)S(1)}, u32[]{:S(2)}, u32[]{:S(2)}) collective-permute-start(f32[136,384]{1,0:T(8,128)S(1)} %get-tuple-element.106), channel_id=1, source_target_pairs={{0,16},{2,18},{8,24},{10,26},{16,0},{18,2},{24,8},{26,10},{1,17},{... | collective-permute-start | bytes 626696 | tf_op jit(solution)/shard_map/ppermute | solution.py:535
  145.8 8.2 %collective-permute-start.39 = (f32[136,384]{1,0:T(8,128)S(1)}, f32[136,384]{1,0:T(8,128)S(1)}, u32[]{:S(2)}, u32[]{:S(2)}) collective-permute-start(f32[136,384]{1,0:T(8,128)S(1)} %collective-permute-done.36.r1), channel_id=1, source_target_pairs={{0,2},{2,0},{1,3},{3,1},{4,6},{6,4},{5,7},{7,5},{8,10},{10,8},{9,1... | collective-permute-start | bytes 626696 | tf_op jit(solution)/shard_map/ppermute | solution.py:530
  152.9 1.5 collective-permute-start.40
  152.9 1.8 collective-permute-start.41
  157.7 11.3 %collective-permute-start.42 = (f32[256,384]{1,0:T(8,128)S(1)}, f32[256,384]{1,0:T(8,128)S(1)}, u32[]{:S(2)}, u32[]{:S(2)}) collective-permute-start(f32[256,384]{1,0:T(8,128)S(1)} %get-tuple-element.110), channel_id=1, source_target_pairs={{0,4},{2,7},{4,1},{6,2},{1,5},{3,6},{5,0},{7,3},{8,12},{10,15},{12... | collective-permute-start | bytes 1179656 | tf_op jit(solution)/shard_map/ppermute | solution.py:663
  160.8 9.8 %collective-permute-start.43 = (f32[256,384]{1,0:T(8,128)S(1)}, f32[256,384]{1,0:T(8,128)S(1)}, u32[]{:S(2)}, u32[]{:S(2)}) collective-permute-start(f32[256,384]{1,0:T(8,128)S(1)} %get-tuple-element.111), channel_id=1, source_target_pairs={{0,5},{2,6},{4,0},{6,3},{1,4},{3,7},{5,1},{7,2},{8,13},{10,14},{12... | collective-permute-start | bytes 1179656 | tf_op jit(solution)/shard_map/ppermute | solution.py:664
  170.7 20.5 %collective-permute-start.44 = (f32[256,384]{1,0:T(8,128)S(1)}, f32[256,384]{1,0:T(8,128)S(1)}, u32[]{:S(2)}, u32[]{:S(2)}) collective-permute-start(f32[256,384]{1,0:T(8,128)S(1)} %add_relay.1), channel_id=1, source_target_pairs={{0,4},{2,7},{4,1},{6,2},{1,5},{3,6},{5,0},{7,3},{8,12},{10,15},{12... | collective-permute-start | bytes 1179656 | tf_op jit(solution)/shard_map/ppermute | solution.py:674
  172.6 11.8 %collective-permute-start.45 = (f32[4,4,384]{2,1,0:T(4,128)S(1)}, f32[4,4,384]{2,1,0:T(4,128)S(1)}, u32[]{:S(2)}, u32[]{:S(2)}) collective-permute-start(f32[4,4,384]{2,1,0:T(4,128)S(1)} %get-tuple-element.118), channel_id=1, source_target_pairs={{0,0},{1,2},{2,1},{3,3},{32,32},{33,34},{34,33},{35,35},{64,64},{6... | collective-permute-start | bytes 73736 | tf_op jit(solution)/shard_map/ppermute | solution.py:679
  176.9 7.4 %collective-permute-start.46 = (f32[4,4,384]{2,1,0:T(4,128)S(1)}, f32[4,4,384]{2,1,0:T(4,128)S(1)}, u32[]{:S(2)}, u32[]{:S(2)}) collective-permute-start(f32[4,4,384]{2,1,0:T(4,128)S(1)} %get-tuple-element.119), channel_id=1, source_target_pairs={{0,32},{1,34},{2,33},{3,35},{32,64},{33,66},{34,65},{35,67},{64,96... | collective-permute-start | bytes 73736 | tf_op jit(solution)/shard_map/ppermute | solution.py:679
  180.7 7.2 %collective-permute-start.47 = (f32[4,4,384]{2,1,0:T(4,128)S(1)}, f32[4,4,384]{2,1,0:T(4,128)S(1)}, u32[]{:S(2)}, u32[]{:S(2)}) collective-permute-start(f32[4,4,384]{2,1,0:T(4,128)S(1)} %get-tuple-element.120), channel_id=1, source_target_pairs={{0,64},{1,66},{2,65},{3,67},{32,96},{33,98},{34,97},{35,99},{64,0}... | collective-permute-start | bytes 73736 | tf_op jit(solution)/shard_map/ppermute | solution.py:679
  184.3 6.9 %collective-permute-start.48 = (f32[4,4,384]{2,1,0:T(4,128)S(1)}, f32[4,4,384]{2,1,0:T(4,128)S(1)}, u32[]{:S(2)}, u32[]{:S(2)}) collective-permute-start(f32[4,4,384]{2,1,0:T(4,128)S(1)} %get-tuple-element.121), channel_id=1, source_target_pairs={{0,96},{1,98},{2,97},{3,99},{32,0},{33,2},{34,1},{35,3},{64,32},{6... | collective-permute-start | bytes 73736 | tf_op jit(solution)/shard_map/ppermute | solution.py:679

commit v4 on v3

--- a/solution.py
+++ b/solution.py
@@ -557,8 +557,9 @@
         return lax.ppermute(values, axes, ring(1)), lax.ppermute(values, axes, ring(-1))
 
     near, away = both_ways(quarter, z_axes, z_ring)
+    near, away, same, cross = lax.optimization_barrier((near, away, same, cross))
     opposite = lax.ppermute(near, z_axes, z_ring(1))
-    near, away, opposite, straight = lax.optimization_barrier((near, away, opposite, straight))
+    opposite, straight = lax.optimization_barrier((opposite, straight))
     quarters = pl.pallas_call(
         join_kernel,
         out_shape=shape(3 * QROWS, 2 * PAD1),
@@ -569,7 +570,7 @@
     )(near, away, opposite)
     straights = both_ways(straight, z_axes, z_ring)
     spread = both_ways(quarters, x_axes, x_ring)
-    straights, spread, quarters, same, cross = lax.optimization_barrier((straights, spread, quarters, same, cross))
+    straights, spread, quarters = lax.optimization_barrier((straights, spread, quarters))
     mine = [
         *straights,
         lax.ppermute(straights[0], z_axes, z_ring(1)),

time: 193 us -> 191 us (0.990)
  starting transfers between devices: 69.7 us -> 65.9 us
  waiting for transfers between devices: 79.6 us -> 81.6 us
    ppermute x1, waiting for transfers between devices: 9.45 us -> 0.01 us  [shards(): lax.ppermute(piece, ('core', 'xh'), [(2 * c + s, 2 * (1 - s) + c) for c,...]
    ppermute x3, waiting for transfers between devices: 0.01 us -> 7.57 us  [both_ways(): lax.ppermute(values, axes, ring(-1))]
    ppermute x1, starting transfers between devices: 6.48 us -> 3.16 us  [shards(): lax.ppermute(piece, ('core', 'xh'), [(2 * c + s, 2 * s + c) for c, s in p...]
    ppermute x1, waiting for transfers between devices: 2.5 us -> 4.46 us  [shards(): lax.ppermute(piece, ('core', 'xh'), [(2 * c + s, 2 * s + c) for c, s in p...]
    ppermute x19, starting transfers between devices: 16.9 us -> 18.9 us  [swap(): return lax.ppermute(values, 'core', [(0, 1), (1, 0)])]
where the time goes in v4:
time: 191 us
  waiting for transfers between devices  81.6 us (43%)
  starting transfers between devices  65.9 us (35%)
  Pallas kernels  40.6 us (21%)
    ppermute x6, waiting for transfers between devices, hop(): half = lax.ppermute(half, 'y', pairs)  19.3 us
    ppermute x19, starting transfers between devices, swap(): return lax.ppermute(values, 'core', [(0, 1), (1, 0)])  18.9 us
    pallas_call x4, Pallas kernels, backward(): pl.pallas_call(lambda *refs: backward_kernel(not halves, full, *refs), ou...  15 us
    pallas_call x4, Pallas kernels, forward(): pl.pallas_call(lambda *refs: forward_kernel(not halves, full, *refs), out...  13.5 us
    ppermute x4, starting transfers between devices, shards(): lax.ppermute(cells[step], ('y', 'core', 'xh'), stem_pairs(step))  12.2 us
    ppermute x19, waiting for transfers between devices, swap(): return lax.ppermute(values, 'core', [(0, 1), (1, 0)])  9.4 us
    ppermute x1, waiting for transfers between devices, shards(): relay = lax.ppermute(partial[2], x_axes, x_ring(1))  8.64 us
    ppermute x3, waiting for transfers between devices, both_ways(): lax.ppermute(values, axes, ring(-1))  7.57 us
  transfers between devices with their start and end apart: 49, of which 27 were waited for; matrix products, arithmetic and copies ran while one was open for 0% of the time, Pallas kernels for 0%

profile of v4, /device:TPU:25, one launch (start us, length us, event | category | flops | bytes accessed | tf_op | source)
XLA Modules:
  0.0 190.7 jit_solution(11025966917056698100)
XLA Ops:
  0.9 0.7 stack.47.where.refs_0_
  1.5 3.2 %pack.1 = (f32[208,768]{1,0:T(8,128)}, f32[64,768]{1,0:T(8,128)}, f32[64,384]{1,0:T(8,128)}, f32[8,768]{1,0:T(8,128)}) custom-call(s32[11]{0:T(128)} %stack.47.where.refs_0_, bf16[1,720,360]{2,1,0:T(8,128)(2,1)} %refs_14_.1, bf16[1,360,360]{2,1,0:T(8,128)(2,1)} %refs_15_.1, bf16[1,360,720]{2,1,0:T(8,128)(2,1)} %refs_16_.1, bf16[1,9,360]{2,1,0:T(8,128)(2,1)} %refs_3_.1, ...), custom_call_target="tpu_custom_call" | custom-call | tf_op jit(solution)/shard_map/pack/pallas_call | solution.py:539
  4.7 1.7 collective-permute-start.1
  6.4 2.2 %collective-permute-start = (f32[64,768]{1,0:T(8,128)}, f32[64,768]{1,0:T(8,128)S(1)}, u32[]{:S(2)}, u32[]{:S(2)}) collective-permute-start(f32[64,768]{1,0:T(8,128)} %get-tuple-element.66), channel_id=1, source_target_pairs={{0,8},{2,26},{8,16},{10,2},{16,24},{18,10},{24,0},{26,18},{1,9},{3... | collective-permute-start | bytes 589832 | tf_op jit(solution)/shard_map/ppermute | solution.py:557
  8.6 2.7 %collective-permute-start.3 = (f32[64,384]{1,0:T(8,128)}, f32[64,384]{1,0:T(8,128)S(1)}, u32[]{:S(2)}, u32[]{:S(2)}) collective-permute-start(f32[64,384]{1,0:T(8,128)} %get-tuple-element.67), channel_id=1, source_target_pairs={{0,2},{1,0},{2,3},{3,1},{4,6},{5,4},{6,7},{7,5},{8,10},{9,8},{10,1... | collective-permute-start | bytes 294920 | tf_op jit(solution)/shard_map/ppermute | solution.py:554
  11.4 3.2 %collective-permute-start.2 = (f32[64,384]{1,0:T(8,128)}, f32[64,384]{1,0:T(8,128)S(1)}, u32[]{:S(2)}, u32[]{:S(2)}) collective-permute-start(f32[64,384]{1,0:T(8,128)} %get-tuple-element.67), channel_id=1, source_target_pairs={{0,0},{1,2},{2,1},{3,3},{4,4},{5,6},{6,5},{7,7},{8,8},{9,10},{10,9... | collective-permute-start | bytes 294920 | tf_op jit(solution)/shard_map/ppermute | solution.py:553
  14.6 4.5 %collective-permute-done.2.refs_1_.refs_3_.refs_7_.same_ref = f32[64,384]{1,0:T(8,128)S(1)} collective-permute-done((f32[64,384]{1,0:T(8,128)}, f32[64,384]{1,0:T(8,128)S(1)}, u32[]{:S(2)}, u32[]{:S(2)}) %collective-permute-start.2) | collective-permute-done | bytes 98336 | tf_op jit(solution)/shard_map/ppermute | solution.py:553
  19.0 1.4 collective-permute-start.4
  20.4 3.1 %collective-permute-done.4.third = f32[64,768]{1,0:T(8,128)S(1)} collective-permute-done((f32[64,768]{1,0:T(8,128)S(1)}, f32[64,768]{1,0:T(8,128)S(1)}, u32[]{:S(2)}, u32[]{:S(2)}) %collective-permute-start.4) | collective-permute-done | bytes 196640 | tf_op jit(solution)/shard_map/ppermute | solution.py:561
  23.6 2.7 %collective-permute-start.5 = (f32[208,768]{1,0:T(8,128)}, f32[208,768]{1,0:T(8,128)S(1)}, u32[]{:S(2)}, u32[]{:S(2)}) collective-permute-start(f32[208,768]{1,0:T(8,128)} %get-tuple-element.72), channel_id=1, source_target_pairs={{0,8},{2,26},{8,16},{10,2},{16,24},{18,10},{24,0},{26,18},{1,9},{3... | collective-permute-start | bytes 1916936 | tf_op jit(solution)/shard_map/ppermute | solution.py:557
  26.3 0.8 collective-permute-start.8
  27.1 1.9 %collective-permute-start.7 = (f32[192,768]{1,0:T(8,128)S(1)}, f32[192,768]{1,0:T(8,128)S(1)}, u32[]{:S(2)}, u32[]{:S(2)}) collective-permute-start(f32[192,768]{1,0:T(8,128)S(1)} %join_quarters.1.refs_3_), channel_id=1, source_target_pairs={{0,4},{2,7},{4,1},{6,2},{1,5},{3,6},{5,0},{7,3},{8,12},{10,15},{12... | collective-permute-start | bytes 1769480 | tf_op jit(solution)/shard_map/ppermute | solution.py:557
  29.0 7.6 %collective-permute-done.8.refs_5_ = f32[192,768]{1,0:T(8,128)S(1)} collective-permute-done((f32[192,768]{1,0:T(8,128)S(1)}, f32[192,768]{1,0:T(8,128)S(1)}, u32[]{:S(2)}, u32[]{:S(2)}) %collective-permute-start.8) | collective-permute-done | bytes 589856 | tf_op jit(solution)/shard_map/ppermute | solution.py:557
  36.6 4.8 %collective-permute-done.7.refs_4_ = f32[192,768]{1,0:T(8,128)S(1)} collective-permute-done((f32[192,768]{1,0:T(8,128)S(1)}, f32[192,768]{1,0:T(8,128)S(1)}, u32[]{:S(2)}, u32[]{:S(2)}) %collective-permute-start.7) | collective-permute-done | bytes 589856 | tf_op jit(solution)/shard_map/ppermute | solution.py:557
  41.4 2.3 %collective-permute-start.9 = (f32[208,768]{1,0:T(8,128)S(1)}, f32[208,768]{1,0:T(8,128)S(1)}, u32[]{:S(2)}, u32[]{:S(2)}) collective-permute-start(f32[208,768]{1,0:T(8,128)S(1)} %collective-permute-done.5.refs_0_), channel_id=1, source_target_pairs={{0,8},{2,26},{8,16},{10,2},{16,24},{18,10},{24,0},{26,18},{1,9},{3... | collective-permute-start | bytes 1916936 | tf_op jit(solution)/shard_map/ppermute | solution.py:576
  44.2 2.0 %collective-permute-start.10 = (f32[192,768]{1,0:T(8,128)S(1)}, f32[192,768]{1,0:T(8,128)S(1)}, u32[]{:S(2)}, u32[]{:S(2)}) collective-permute-start(f32[192,768]{1,0:T(8,128)S(1)} %collective-permute-done.7.refs_4_), channel_id=1, source_target_pairs={{0,4},{2,7},{4,1},{6,2},{1,5},{3,6},{5,0},{7,3},{8,12},{10,15},{12... | collective-permute-start | bytes 1769480 | tf_op jit(solution)/shard_map/ppermute | solution.py:579
  46.8 4.3 %collective-permute-done.9.refs_2_ = f32[208,768]{1,0:T(8,128)S(1)} collective-permute-done((f32[208,768]{1,0:T(8,128)S(1)}, f32[208,768]{1,0:T(8,128)S(1)}, u32[]{:S(2)}, u32[]{:S(2)}) %collective-permute-start.9) | collective-permute-done | bytes 639008 | tf_op jit(solution)/shard_map/ppermute | solution.py:576
  51.1 4.1 %collective-permute-start.13 = (f32[208,768]{1,0:T(8,128)S(1)}, f32[208,768]{1,0:T(8,128)S(1)}, u32[]{:S(2)}, u32[]{:S(2)}) collective-permute-start(f32[208,768]{1,0:T(8,128)S(1)} %collective-permute-done.9.refs_2_), channel_id=1, source_target_pairs={{0,2},{2,0},{1,3},{3,1},{4,6},{6,4},{5,7},{7,5},{8,10},{10,8},{9,1... | collective-permute-start | bytes 1916936 | tf_op jit(solution)/shard_map/ppermute | solution.py:530
  55.7 2.0 %collective-permute-done.15.refs_11_ = f32[192,768]{1,0:T(8,128)S(1)} collective-permute-done((f32[192,768]{1,0:T(8,128)S(1)}, f32[192,768]{1,0:T(8,128)S(1)}, u32[]{:S(2)}, u32[]{:S(2)}) %collective-permute-start.15) | collective-permute-done | bytes 589856 | tf_op jit(solution)/shard_map/ppermute | solution.py:530
  57.7 0.8 collective-permute-done.17.refs_13_
  58.6 0.7 copy-done.7
  59.3 2.6 %columns.1 = (bf16[4,720,360]{2,1,0:T(8,128)(2,1)S(1)}, bf16[4,360,360]{2,1,0:T(8,128)(2,1)S(1)}, bf16[4,360,720]{2,1,0:T(8,128)(2,1)S(1)}, f32[4,8,768]{2,1,0:T(8,128)S(1)}) custom-call(s32[11]{0:T(128)S(1)} %copy-done.6, f32[208,768]{1,0:T(8,128)S(1)} %collective-permute-done.5.refs_0_, f32[208,768]{1,0:T(8,128)S(1)} %collective-permute-done.6.refs_1_, ...), custom_call_target="tpu_custom_call" | custom-call | tf_op jit(solution)/shard_map/columns/pallas_call | solution.py:581
  61.9 3.2 %forward_light.3 = f32[96,384]{1,0:T(8,128)S(1)} custom-call(s32[11]{0:T(128)S(1)} %copy-done.6, f32[64,384]{1,0:T(8,128)S(1)} %collective-permute-done.2.refs_1_.refs_3_.refs_7_.same_ref, f32[64,384]{1,0:T(8,128)S(1)} %collective-permute-done.3.refs_2_.refs_4_.refs_8_.cross_ref, ...), custom_call_target="tpu_custom_call" | custom-call | tf_op jit(solution)/shard_map/forward_light/pallas_call | solution.py:598
  65.1 0.7 collective-permute-start.18
  66.4 1.0 collective-permute-done.19.refs_2_
  67.5 3.2 %forward_light.4 = f32[96,384]{1,0:T(8,128)S(1)} custom-call(s32[11]{0:T(128)S(1)} %copy-done.6, f32[96,384]{1,0:T(8,128)S(1)} %collective-permute-done.18.refs_1_, f32[96,384]{1,0:T(8,128)S(1)} %collective-permute-done.19.refs_2_, f32[64,384]{1,0:T(8,128)S(1)} %collective-permute-done.2.refs_1_.refs_3_.refs_7_.same_ref, ...), custom_call_target="tpu_custom_call" | custom-call | tf_op jit(solution)/shard_map/forward_light/pallas_call | solution.py:598
  70.7 0.7 collective-permute-start.20
  71.8 1.0 collective-permute-done.21.refs_2_.refs_4_
  72.8 3.2 %forward_light.5 = f32[96,384]{1,0:T(8,128)S(1)} custom-call(s32[11]{0:T(128)S(1)} %copy-done.6, f32[96,384]{1,0:T(8,128)S(1)} %collective-permute-done.20.refs_1_.refs_3_, f32[96,384]{1,0:T(8,128)S(1)} %collective-permute-done.21.refs_2_.refs_4_, f32[64,384]{1,0:T(8,128)S(1)} %collective-permute-done.2.refs_1_.refs_3_.refs_7_.same_ref, ...), custom_call_target="tpu_custom_call" | custom-call | tf_op jit(solution)/shard_map/forward_light/pallas_call | solution.py:598
  76.1 1.4 collective-permute-start.22
  77.5 16.3 %collective-permute-done.22.refs_5_ = f32[96,384]{1,0:T(8,128)S(1)} collective-permute-done((f32[96,384]{1,0:T(8,128)S(1)}, f32[96,384]{1,0:T(8,128)S(1)}, u32[]{:S(2)}, u32[]{:S(2)}) %collective-permute-start.22) | collective-permute-done | bytes 147488 | tf_op jit(solution)/shard_map/ppermute | solution.py:609
  93.8 0.9 collective-permute-start.23
  94.7 1.0 collective-permute-done.23.refs_6_
  95.7 3.9 %forward_full.1 = (f32[192,384]{1,0:T(8,128)S(1)}, f32[4,128,360]{2,1,0:T(8,128)S(1)}, f32[4,128,360]{2,1,0:T(8,128)S(1)}, f32[4,32,720]{2,1,0:T(8,128)S(1)}, f3...) custom-call(s32[11]{0:T(128)S(1)} %copy-done.6, ...), custom_call_target="tpu_custom_call" | custom-call | tf_op jit(solution)/shard_map/forward_full/pallas_call | solution.py:598
  99.6 1.8 head.1.refs_1_.refs_7_
  101.4 3.5 %backward_light.3 = f32[96,384]{1,0:T(8,128)S(1)} custom-call(s32[11]{0:T(128)S(1)} %copy-done.6, f32[192,384]{1,0:T(8,128)S(1)} %head.1.refs_1_.refs_7_, f32[4,128,360]{2,1,0:T(8,128)S(1)} %get-tuple-element.87.refs_2_.refs_3_.refs_8_, f32[4,32,720]{2,1,0:T(8,128)S(1)} %get-tuple-element.88.refs_3_.refs_4_.refs_9_, ...), custom_call_target="tpu_custom_call" | custom-call | tf_op jit(solution)/shard_map/backward_light/pallas_call | solution.py:634
  104.9 1.3 collective-permute-start.24
  106.2 3.0 %collective-permute-done.24.refs_1_ = f32[96,384]{1,0:T(8,128)S(1)} collective-permute-done((f32[96,384]{1,0:T(8,128)S(1)}, f32[96,384]{1,0:T(8,128)S(1)}, u32[]{:S(2)}, u32[]{:S(2)}) %collective-permute-start.24) | collective-permute-done | bytes 147488 | tf_op jit(solution)/shard_map/ppermute | solution.py:609
  109.2 1.1 collective-permute-start.25
  110.3 1.0 collective-permute-done.25.refs_2_
  111.3 3.5 %backward_light.4 = f32[96,384]{1,0:T(8,128)S(1)} custom-call(s32[11]{0:T(128)S(1)} %copy-done.6, f32[96,384]{1,0:T(8,128)S(1)} %collective-permute-done.24.refs_1_, f32[96,384]{1,0:T(8,128)S(1)} %collective-permute-done.25.refs_2_, f32[4,128,360]{2,1,0:T(8,128)S(1)} %get-tuple-element.87.refs_2_.refs_3_.refs_8_, ...), custom_call_target="tpu_custom_call" | custom-call | tf_op jit(solution)/shard_map/backward_light/pallas_call | solution.py:634
  114.8 0.7 collective-permute-start.26
  115.4 1.8 collective-permute-start.28
  117.3 2.4 %collective-permute-start.30 = (f32[112,384]{1,0:T(8,128)S(1)}, f32[112,384]{1,0:T(8,128)S(1)}, u32[]{:S(2)}, u32[]{:S(2)}) collective-permute-start(f32[112,384]{1,0:T(8,128)S(1)} %get-tuple-element.91), channel_id=1, source_target_pairs={{0,16},{2,18},{8,24},{10,26},{16,0},{18,2},{24,8},{26,10},{1,17},{... | collective-permute-start | bytes 516104 | tf_op jit(solution)/shard_map/ppermute | solution.py:535
  119.6 1.2 collective-permute-start.27
  120.8 3.1 %collective-permute-done.29.l2 = f32[112,384]{1,0:T(8,128)S(1)} collective-permute-done((f32[112,384]{1,0:T(8,128)S(1)}, f32[112,384]{1,0:T(8,128)S(1)}, u32[]{:S(2)}, u32[]{:S(2)}) %collective-permute-start.29) | collective-permute-done | bytes 172064 | tf_op jit(solution)/shard_map/ppermute | solution.py:534
  123.9 3.7 %collective-permute-done.30.l3 = f32[112,384]{1,0:T(8,128)S(1)} collective-permute-done((f32[112,384]{1,0:T(8,128)S(1)}, f32[112,384]{1,0:T(8,128)S(1)}, u32[]{:S(2)}, u32[]{:S(2)}) %collective-permute-start.30) | collective-permute-done | bytes 172064 | tf_op jit(solution)/shard_map/ppermute | solution.py:535
  127.6 3.5 %backward_light.5 = f32[96,384]{1,0:T(8,128)S(1)} custom-call(s32[11]{0:T(128)S(1)} %copy-done.6, f32[96,384]{1,0:T(8,128)S(1)} %collective-permute-done.26.refs_1_.refs_3_, f32[96,384]{1,0:T(8,128)S(1)} %collective-permute-done.27.refs_2_.refs_4_, f32[4,128,360]{2,1,0:T(8,128)S(1)} %get-tuple-element.87.refs_2_.refs_3_.refs_8_, ...), custom_call_target="tpu_custom_call" | custom-call | tf_op jit(solution)/shard_map/backward_light/pallas_call | solution.py:634
  131.1 0.7 collective-permute-start.31
  134.1 4.6 %backward_full.1 = (f32[136,384]{1,0:T(8,128)S(1)}, f32[136,384]{1,0:T(8,128)S(1)}, f32[136,384]{1,0:T(8,128)S(1)}, f32[240,384]{1,0:T(8,128)S(1)}, f32[16,384]{1,0:T(8,128)S(1)}) custom-call(s32[11]{0:T(128)S(1)} %copy-done.6, f32[96,384]{1,0:T(8,128)S(1)} %collective-permute-done.24.refs_1_, f32[96,384]{1,0:T(8,128)S(1)} %collective-permute-done.25.refs_2_, ...), custom_call_target="tpu_custom_call" | custom-call | tf_op jit(solution)/shard_map/backward_full/pallas_call | solution.py:634
  138.7 1.2 collective-permute-start.36
  140.3 0.9 collective-permute-start.38
  141.2 3.8 %collective-permute-done.36.r1 = f32[136,384]{1,0:T(8,128)S(1)} collective-permute-done((f32[136,384]{1,0:T(8,128)S(1)}, f32[136,384]{1,0:T(8,128)S(1)}, u32[]{:S(2)}, u32[]{:S(2)}) %collective-permute-start.36) | collective-permute-done | bytes 208928 | tf_op jit(solution)/shard_map/ppermute | solution.py:533
  145.0 7.4 %collective-permute-start.39 = (f32[136,384]{1,0:T(8,128)S(1)}, f32[136,384]{1,0:T(8,128)S(1)}, u32[]{:S(2)}, u32[]{:S(2)}) collective-permute-start(f32[136,384]{1,0:T(8,128)S(1)} %collective-permute-done.36.r1), channel_id=1, source_target_pairs={{0,2},{2,0},{1,3},{3,1},{4,6},{6,4},{5,7},{7,5},{8,10},{10,8},{9,1... | collective-permute-start | bytes 626696 | tf_op jit(solution)/shard_map/ppermute | solution.py:530
  154.2 3.1 %weight_grads.1 = (f32[256,384]{1,0:T(8,128)S(1)}, f32[256,384]{1,0:T(8,128)S(1)}, f32[256,384]{1,0:T(8,128)S(1)}, f32[256,384]{1,0:T(8,128)S(1)}, f32[4,4,384]{...) custom-call(s32[11]{0:T(128)S(1)} %copy-done.6, ...), custom_call_target="tpu_custom_call" | custom-call | tf_op jit(solution)/shard_map/weight_grads/pallas_call | solution.py:655
  157.2 1.7 collective-permute-start.42
  159.0 8.6 %collective-permute-done.42.second = f32[256,384]{1,0:T(8,128)S(1)} collective-permute-done((f32[256,384]{1,0:T(8,128)S(1)}, f32[256,384]{1,0:T(8,128)S(1)}, u32[]{:S(2)}, u32[]{:S(2)}) %collective-permute-start.42) | collective-permute-done | bytes 393248 | tf_op jit(solution)/shard_map/ppermute | solution.py:664
  167.6 2.5 %collective-permute-done.43.far = f32[256,384]{1,0:T(8,128)S(1)} collective-permute-done((f32[256,384]{1,0:T(8,128)S(1)}, f32[256,384]{1,0:T(8,128)S(1)}, u32[]{:S(2)}, u32[]{:S(2)}) %collective-permute-start.43) | collective-permute-done | bytes 393248 | tf_op jit(solution)/shard_map/ppermute | solution.py:665
  170.3 4.8 %collective-permute-start.45 = (f32[4,4,384]{2,1,0:T(4,128)S(1)}, f32[4,4,384]{2,1,0:T(4,128)S(1)}, u32[]{:S(2)}, u32[]{:S(2)}) collective-permute-start(f32[4,4,384]{2,1,0:T(4,128)S(1)} %get-tuple-element.118), channel_id=1, source_target_pairs={{0,0},{1,2},{2,1},{3,3},{32,32},{33,34},{34,33},{35,35},{64,64},{6... | collective-permute-start | bytes 73736 | tf_op jit(solution)/shard_map/ppermute | solution.py:680
  175.1 3.3 %collective-permute-start.46 = (f32[4,4,384]{2,1,0:T(4,128)S(1)}, f32[4,4,384]{2,1,0:T(4,128)S(1)}, u32[]{:S(2)}, u32[]{:S(2)}) collective-permute-start(f32[4,4,384]{2,1,0:T(4,128)S(1)} %get-tuple-element.119), channel_id=1, source_target_pairs={{0,32},{1,34},{2,33},{3,35},{32,64},{33,66},{34,65},{35,67},{64,96... | collective-permute-start | bytes 73736 | tf_op jit(solution)/shard_map/ppermute | solution.py:680
  178.4 4.1 %collective-permute-start.47 = (f32[4,4,384]{2,1,0:T(4,128)S(1)}, f32[4,4,384]{2,1,0:T(4,128)S(1)}, u32[]{:S(2)}, u32[]{:S(2)}) collective-permute-start(f32[4,4,384]{2,1,0:T(4,128)S(1)} %get-tuple-element.120), channel_id=1, source_target_pairs={{0,64},{1,66},{2,65},{3,67},{32,96},{33,98},{34,97},{35,99},{64,0}... | collective-permute-start | bytes 73736 | tf_op jit(solution)/shard_map/ppermute | solution.py:680
  182.5 3.1 %collective-permute-done.47.c2 = f32[4,4,384]{2,1,0:T(4,128)S(1)} collective-permute-done((f32[4,4,384]{2,1,0:T(4,128)S(1)}, f32[4,4,384]{2,1,0:T(4,128)S(1)}, u32[]{:S(2)}, u32[]{:S(2)}) %collective-permute-start.47) | collective-permute-done | bytes 24608 | tf_op jit(solution)/shard_map/ppermute | solution.py:680
  185.6 3.8 %collective-permute-done.48.c3 = f32[4,4,384]{2,1,0:T(4,128)S(1)} collective-permute-done((f32[4,4,384]{2,1,0:T(4,128)S(1)}, f32[4,4,384]{2,1,0:T(4,128)S(1)}, u32[]{:S(2)}, u32[]{:S(2)}) %collective-permute-start.48) | collective-permute-done | bytes 24608 | tf_op jit(solution)/shard_map/ppermute | solution.py:680
  189.4 1.3 final.1
  (66 shorter events, 7.3 us)
Async XLA Ops:
  0.6 57.9 %copy-start.1 = (bf16[1,360,720]{2,1,0:T(8,128)(2,1)S(1)}, bf16[1,360,720]{2,1,0:T(8,128)(2,1)}, u32[]{:S(2)}) copy-start(bf16[1,360,720]{2,1,0:T(8,128)(2,1)} %refs_16_.1) | copy-start | bytes 1555204
  0.6 57.9 %copy-start.2 = (bf16[1,360,360]{2,1,0:T(8,128)(2,1)S(1)}, bf16[1,360,360]{2,1,0:T(8,128)(2,1)}, u32[]{:S(2)}) copy-start(bf16[1,360,360]{2,1,0:T(8,128)(2,1)} %refs_15_.1) | copy-start | bytes 777604
  0.7 57.9 %copy-start = (bf16[1,720,360]{2,1,0:T(8,128)(2,1)S(1)}, bf16[1,720,360]{2,1,0:T(8,128)(2,1)}, u32[]{:S(2)}) copy-start(bf16[1,720,360]{2,1,0:T(8,128)(2,1)} %refs_14_.1) | copy-start | bytes 1555204
  1.5 57.0 %copy-start.6 = (s32[11]{0:T(128)S(1)}, s32[11]{0:T(128)}, u32[]{:S(2)}) copy-start(s32[11]{0:T(128)} %stack.47.where.refs_0_) | copy-start | bytes 136
  4.7 14.3 %collective-permute-start.1 = (f32[64,768]{1,0:T(8,128)}, f32[64,768]{1,0:T(8,128)S(1)}, u32[]{:S(2)}, u32[]{:S(2)}) collective-permute-start(f32[64,768]{1,0:T(8,128)} %get-tuple-element.66), channel_id=1, source_target_pairs={{0,24},{2,10},{8,0},{10,18},{16,8},{18,26},{24,16},{26,2},{1,25},{... | collective-permute-start | bytes 589832 | tf_op jit(solution)/shard_map/ppermute | solution.py:557
  6.4 12.6 %collective-permute-start = (f32[64,768]{1,0:T(8,128)}, f32[64,768]{1,0:T(8,128)S(1)}, u32[]{:S(2)}, u32[]{:S(2)}) collective-permute-start(f32[64,768]{1,0:T(8,128)} %get-tuple-element.66), channel_id=1, source_target_pairs={{0,8},{2,26},{8,16},{10,2},{16,24},{18,10},{24,0},{26,18},{1,9},{3... | collective-permute-start | bytes 589832 | tf_op jit(solution)/shard_map/ppermute | solution.py:557
  8.6 5.9 %collective-permute-start.3 = (f32[64,384]{1,0:T(8,128)}, f32[64,384]{1,0:T(8,128)S(1)}, u32[]{:S(2)}, u32[]{:S(2)}) collective-permute-start(f32[64,384]{1,0:T(8,128)} %get-tuple-element.67), channel_id=1, source_target_pairs={{0,2},{1,0},{2,3},{3,1},{4,6},{5,4},{6,7},{7,5},{8,10},{9,8},{10,1... | collective-permute-start | bytes 294920 | tf_op jit(solution)/shard_map/ppermute | solution.py:554
  11.4 7.6 %collective-permute-start.2 = (f32[64,384]{1,0:T(8,128)}, f32[64,384]{1,0:T(8,128)S(1)}, u32[]{:S(2)}, u32[]{:S(2)}) collective-permute-start(f32[64,384]{1,0:T(8,128)} %get-tuple-element.67), channel_id=1, source_target_pairs={{0,0},{1,2},{2,1},{3,3},{4,4},{5,6},{6,5},{7,7},{8,8},{9,10},{10,9... | collective-permute-start | bytes 294920 | tf_op jit(solution)/shard_map/ppermute | solution.py:553
  19.0 4.5 %collective-permute-start.4 = (f32[64,768]{1,0:T(8,128)S(1)}, f32[64,768]{1,0:T(8,128)S(1)}, u32[]{:S(2)}, u32[]{:S(2)}) collective-permute-start(f32[64,768]{1,0:T(8,128)S(1)} %collective-permute-done.first), channel_id=1, source_target_pairs={{0,8},{2,26},{8,16},{10,2},{16,24},{18,10},{24,0},{26,18},{1,9},{3... | collective-permute-start | bytes 589832 | tf_op jit(solution)/shard_map/ppermute | solution.py:561
  23.5 17.9 %collective-permute-start.6 = (f32[208,768]{1,0:T(8,128)}, f32[208,768]{1,0:T(8,128)S(1)}, u32[]{:S(2)}, u32[]{:S(2)}) collective-permute-start(f32[208,768]{1,0:T(8,128)} %get-tuple-element.72), channel_id=1, source_target_pairs={{0,24},{2,10},{8,0},{10,18},{16,8},{18,26},{24,16},{26,2},{1,25},{... | collective-permute-start | bytes 1916936 | tf_op jit(solution)/shard_map/ppermute | solution.py:557
  23.6 17.9 %collective-permute-start.5 = (f32[208,768]{1,0:T(8,128)}, f32[208,768]{1,0:T(8,128)S(1)}, u32[]{:S(2)}, u32[]{:S(2)}) collective-permute-start(f32[208,768]{1,0:T(8,128)} %get-tuple-element.72), channel_id=1, source_target_pairs={{0,8},{2,26},{8,16},{10,2},{16,24},{18,10},{24,0},{26,18},{1,9},{3... | collective-permute-start | bytes 1916936 | tf_op jit(solution)/shard_map/ppermute | solution.py:557
  26.3 10.3 %collective-permute-start.8 = (f32[192,768]{1,0:T(8,128)S(1)}, f32[192,768]{1,0:T(8,128)S(1)}, u32[]{:S(2)}, u32[]{:S(2)}) collective-permute-start(f32[192,768]{1,0:T(8,128)S(1)} %join_quarters.1.refs_3_), channel_id=1, source_target_pairs={{0,5},{2,6},{4,0},{6,3},{1,4},{3,7},{5,1},{7,2},{8,13},{10,14},{12... | collective-permute-start | bytes 1769480 | tf_op jit(solution)/shard_map/ppermute | solution.py:557
  27.1 14.4 %collective-permute-start.7 = (f32[192,768]{1,0:T(8,128)S(1)}, f32[192,768]{1,0:T(8,128)S(1)}, u32[]{:S(2)}, u32[]{:S(2)}) collective-permute-start(f32[192,768]{1,0:T(8,128)S(1)} %join_quarters.1.refs_3_), channel_id=1, source_target_pairs={{0,4},{2,7},{4,1},{6,2},{1,5},{3,6},{5,0},{7,3},{8,12},{10,15},{12... | collective-permute-start | bytes 1769480 | tf_op jit(solution)/shard_map/ppermute | solution.py:557
  41.4 9.6 %collective-permute-start.9 = (f32[208,768]{1,0:T(8,128)S(1)}, f32[208,768]{1,0:T(8,128)S(1)}, u32[]{:S(2)}, u32[]{:S(2)}) collective-permute-start(f32[208,768]{1,0:T(8,128)S(1)} %collective-permute-done.5.refs_0_), channel_id=1, source_target_pairs={{0,8},{2,26},{8,16},{10,2},{16,24},{18,10},{24,0},{26,18},{1,9},{3... | collective-permute-start | bytes 1916936 | tf_op jit(solution)/shard_map/ppermute | solution.py:576
  43.7 2.5 %collective-permute-start.14 = (f32[192,768]{1,0:T(8,128)S(1)}, f32[192,768]{1,0:T(8,128)S(1)}, u32[]{:S(2)}, u32[]{:S(2)}) collective-permute-start(f32[192,768]{1,0:T(8,128)S(1)} %join_quarters.1.refs_3_), channel_id=1, source_target_pairs={{0,2},{2,0},{1,3},{3,1},{4,6},{6,4},{5,7},{7,5},{8,10},{10,8},{9,1... | collective-permute-start | bytes 1769480 | tf_op jit(solution)/shard_map/ppermute | solution.py:530
  43.7 11.5 %collective-permute-start.16 = (f32[192,768]{1,0:T(8,128)S(1)}, f32[192,768]{1,0:T(8,128)S(1)}, u32[]{:S(2)}, u32[]{:S(2)}) collective-permute-start(f32[192,768]{1,0:T(8,128)S(1)} %collective-permute-done.8.refs_5_), channel_id=1, source_target_pairs={{0,2},{2,0},{1,3},{3,1},{4,6},{6,4},{5,7},{7,5},{8,10},{10,8},{9,1... | collective-permute-start | bytes 1769480 | tf_op jit(solution)/shard_map/ppermute | solution.py:530
  44.2 11.0 %collective-permute-start.10 = (f32[192,768]{1,0:T(8,128)S(1)}, f32[192,768]{1,0:T(8,128)S(1)}, u32[]{:S(2)}, u32[]{:S(2)}) collective-permute-start(f32[192,768]{1,0:T(8,128)S(1)} %collective-permute-done.7.refs_4_), channel_id=1, source_target_pairs={{0,4},{2,7},{4,1},{6,2},{1,5},{3,6},{5,0},{7,3},{8,12},{10,15},{12... | collective-permute-start | bytes 1769480 | tf_op jit(solution)/shard_map/ppermute | solution.py:579
  46.2 11.5 %collective-permute-start.12 = (f32[208,768]{1,0:T(8,128)S(1)}, f32[208,768]{1,0:T(8,128)S(1)}, u32[]{:S(2)}, u32[]{:S(2)}) collective-permute-start(f32[208,768]{1,0:T(8,128)S(1)} %collective-permute-done.6.refs_1_), channel_id=1, source_target_pairs={{0,2},{2,0},{1,3},{3,1},{4,6},{6,4},{5,7},{7,5},{8,10},{10,8},{9,1... | collective-permute-start | bytes 1916936 | tf_op jit(solution)/shard_map/ppermute | solution.py:530
  46.2 11.5 %collective-permute-start.11 = (f32[208,768]{1,0:T(8,128)S(1)}, f32[208,768]{1,0:T(8,128)S(1)}, u32[]{:S(2)}, u32[]{:S(2)}) collective-permute-start(f32[208,768]{1,0:T(8,128)S(1)} %collective-permute-done.5.refs_0_), channel_id=1, source_target_pairs={{0,2},{2,0},{1,3},{3,1},{4,6},{6,4},{5,7},{7,5},{8,10},{10,8},{9,1... | collective-permute-start | bytes 1916936 | tf_op jit(solution)/shard_map/ppermute | solution.py:530
  51.1 7.5 %collective-permute-start.13 = (f32[208,768]{1,0:T(8,128)S(1)}, f32[208,768]{1,0:T(8,128)S(1)}, u32[]{:S(2)}, u32[]{:S(2)}) collective-permute-start(f32[208,768]{1,0:T(8,128)S(1)} %collective-permute-done.9.refs_2_), channel_id=1, source_target_pairs={{0,2},{2,0},{1,3},{3,1},{4,6},{6,4},{5,7},{7,5},{8,10},{10,8},{9,1... | collective-permute-start | bytes 1916936 | tf_op jit(solution)/shard_map/ppermute | solution.py:530
  55.2 2.5 %collective-permute-start.15 = (f32[192,768]{1,0:T(8,128)S(1)}, f32[192,768]{1,0:T(8,128)S(1)}, u32[]{:S(2)}, u32[]{:S(2)}) collective-permute-start(f32[192,768]{1,0:T(8,128)S(1)} %collective-permute-done.7.refs_4_), channel_id=1, source_target_pairs={{0,2},{2,0},{1,3},{3,1},{4,6},{6,4},{5,7},{7,5},{8,10},{10,8},{9,1... | collective-permute-start | bytes 1769480 | tf_op jit(solution)/shard_map/ppermute | solution.py:530
  55.2 3.4 %collective-permute-start.17 = (f32[192,768]{1,0:T(8,128)S(1)}, f32[192,768]{1,0:T(8,128)S(1)}, u32[]{:S(2)}, u32[]{:S(2)}) collective-permute-start(f32[192,768]{1,0:T(8,128)S(1)} %collective-permute-done.10.refs_6_), channel_id=1, source_target_pairs={{0,2},{2,0},{1,3},{3,1},{4,6},{6,4},{5,7},{7,5},{8,10},{10,8},{9,1... | collective-permute-start | bytes 1769480 | tf_op jit(solution)/shard_map/ppermute | solution.py:530
  58.6 0.7 copy-start.7
  65.1 0.7 collective-permute-start.18
  65.8 1.6 collective-permute-start.19
  70.7 0.7 collective-permute-start.20
  71.4 1.5 collective-permute-start.21
  76.0 23.6 %copy-start.3 = (bf16[720,512]{1,0:T(8,128)(2,1)S(1)}, bf16[720,512]{1,0:T(8,128)(2,1)}, u32[]{:S(2)}) copy-start(bf16[720,512]{1,0:T(8,128)(2,1)} %two_ref.1) | copy-start | bytes 2211844
  76.1 23.6 %copy-start.4 = (bf16[360,512]{1,0:T(8,128)(2,1)S(1)}, bf16[360,512]{1,0:T(8,128)(2,1)}, u32[]{:S(2)}) copy-start(bf16[360,512]{1,0:T(8,128)(2,1)} %one_ref.1) | copy-start | bytes 1105924
  76.1 23.6 %copy-start.5 = (bf16[512,150]{0,1:T(8,128)(2,1)S(1)}, bf16[512,150]{0,1:T(8,128)(2,1)}, u32[]{:S(2)}) copy-start(bf16[512,150]{0,1:T(8,128)(2,1)} %param.21) | copy-start | bytes 460804
  76.1 17.7 %collective-permute-start.22 = (f32[96,384]{1,0:T(8,128)S(1)}, f32[96,384]{1,0:T(8,128)S(1)}, u32[]{:S(2)}, u32[]{:S(2)}) collective-permute-start(f32[96,384]{1,0:T(8,128)S(1)} %forward_light.5), channel_id=1, source_target_pairs={{64,96},{65,97},{66,98},{67,99},{68,100},{69,101},{70,102},{71,103... | collective-permute-start | bytes 442376 | tf_op jit(solution)/shard_map/ppermute | solution.py:609
  93.8 1.9 collective-permute-start.23
  104.9 4.3 %collective-permute-start.24 = (f32[96,384]{1,0:T(8,128)S(1)}, f32[96,384]{1,0:T(8,128)S(1)}, u32[]{:S(2)}, u32[]{:S(2)}) collective-permute-start(f32[96,384]{1,0:T(8,128)S(1)} %backward_light.3), channel_id=1, source_target_pairs={{96,64},{97,65},{98,66},{99,67},{100,68},{101,69},{102,70},{103,71... | collective-permute-start | bytes 442376 | tf_op jit(solution)/shard_map/ppermute | solution.py:609
  109.2 2.1 %collective-permute-start.25 = (f32[96,384]{1,0:T(8,128)S(1)}, f32[96,384]{1,0:T(8,128)S(1)}, u32[]{:S(2)}, u32[]{:S(2)}) collective-permute-start(f32[96,384]{1,0:T(8,128)S(1)} %collective-permute-done.24.refs_1_), channel_id=1, source_target_pairs={{0,2},{2,0},{1,3},{3,1},{4,6},{6,4},{5,7},{7,5},{8,10},{10,8},{9,1... | collective-permute-start | bytes 442376 | tf_op jit(solution)/shard_map/ppermute | solution.py:530
  114.8 4.9 %collective-permute-start.26 = (f32[96,384]{1,0:T(8,128)S(1)}, f32[96,384]{1,0:T(8,128)S(1)}, u32[]{:S(2)}, u32[]{:S(2)}) collective-permute-start(f32[96,384]{1,0:T(8,128)S(1)} %backward_light.4), channel_id=1, source_target_pairs={{64,32},{65,33},{66,34},{67,35},{68,36},{69,37},{70,38},{71,39},{7... | collective-permute-start | bytes 442376 | tf_op jit(solution)/shard_map/ppermute | solution.py:609
  115.4 5.4 %collective-permute-start.28 = (f32[112,384]{1,0:T(8,128)S(1)}, f32[112,384]{1,0:T(8,128)S(1)}, u32[]{:S(2)}, u32[]{:S(2)}) collective-permute-start(f32[112,384]{1,0:T(8,128)S(1)} %get-tuple-element.89), channel_id=1, source_target_pairs={{0,8},{2,26},{8,16},{10,2},{16,24},{18,10},{24,0},{26,18},{1,9},{3... | collective-permute-start | bytes 516104 | tf_op jit(solution)/shard_map/ppermute | solution.py:533
  117.3 6.7 %collective-permute-start.29 = (f32[112,384]{1,0:T(8,128)S(1)}, f32[112,384]{1,0:T(8,128)S(1)}, u32[]{:S(2)}, u32[]{:S(2)}) collective-permute-start(f32[112,384]{1,0:T(8,128)S(1)} %get-tuple-element.90), channel_id=1, source_target_pairs={{0,24},{2,10},{8,0},{10,18},{16,8},{18,26},{24,16},{26,2},{1,25},{... | collective-permute-start | bytes 516104 | tf_op jit(solution)/shard_map/ppermute | solution.py:534
  117.3 10.3 %collective-permute-start.30 = (f32[112,384]{1,0:T(8,128)S(1)}, f32[112,384]{1,0:T(8,128)S(1)}, u32[]{:S(2)}, u32[]{:S(2)}) collective-permute-start(f32[112,384]{1,0:T(8,128)S(1)} %get-tuple-element.91), channel_id=1, source_target_pairs={{0,16},{2,18},{8,24},{10,26},{16,0},{18,2},{24,8},{26,10},{1,17},{... | collective-permute-start | bytes 516104 | tf_op jit(solution)/shard_map/ppermute | solution.py:535
  119.6 8.0 %collective-permute-start.27 = (f32[96,384]{1,0:T(8,128)S(1)}, f32[96,384]{1,0:T(8,128)S(1)}, u32[]{:S(2)}, u32[]{:S(2)}) collective-permute-start(f32[96,384]{1,0:T(8,128)S(1)} %collective-permute-done.26.refs_1_.refs_3_), channel_id=1, source_target_pairs={{0,2},{2,0},{1,3},{3,1},{4,6},{6,4},{5,7},{7,5},{8,10},{10,8},{9,1... | collective-permute-start | bytes 442376 | tf_op jit(solution)/shard_map/ppermute | solution.py:530
  131.1 1.7 collective-permute-start.31
  131.8 1.5 collective-permute-start.33
  132.2 1.4 collective-permute-start.34
  132.4 1.5 collective-permute-start.35
  132.8 1.4 collective-permute-start.32
  138.7 6.3 %collective-permute-start.36 = (f32[136,384]{1,0:T(8,128)S(1)}, f32[136,384]{1,0:T(8,128)S(1)}, u32[]{:S(2)}, u32[]{:S(2)}) collective-permute-start(f32[136,384]{1,0:T(8,128)S(1)} %get-tuple-element.104), channel_id=1, source_target_pairs={{0,8},{2,26},{8,16},{10,2},{16,24},{18,10},{24,0},{26,18},{1,9},{3... | collective-permute-start | bytes 626696 | tf_op jit(solution)/shard_map/ppermute | solution.py:533
  139.9 12.5 %collective-permute-start.37 = (f32[136,384]{1,0:T(8,128)S(1)}, f32[136,384]{1,0:T(8,128)S(1)}, u32[]{:S(2)}, u32[]{:S(2)}) collective-permute-start(f32[136,384]{1,0:T(8,128)S(1)} %get-tuple-element.105), channel_id=1, source_target_pairs={{0,24},{2,10},{8,0},{10,18},{16,8},{18,26},{24,16},{26,2},{1,25},{... | collective-permute-start | bytes 626696 | tf_op jit(solution)/shard_map/ppermute | solution.py:534
  140.3 12.1 %collective-permute-start.38 = (f32[136,384]{1,0:T(8,128)S(1)}, f32[136,384]{1,0:T(8,128)S(1)}, u32[]{:S(2)}, u32[]{:S(2)}) collective-permute-start(f32[136,384]{1,0:T(8,128)S(1)} %get-tuple-element.106), channel_id=1, source_target_pairs={{0,16},{2,18},{8,24},{10,26},{16,0},{18,2},{24,8},{26,10},{1,17},{... | collective-permute-start | bytes 626696 | tf_op jit(solution)/shard_map/ppermute | solution.py:535
  145.0 8.5 %collective-permute-start.39 = (f32[136,384]{1,0:T(8,128)S(1)}, f32[136,384]{1,0:T(8,128)S(1)}, u32[]{:S(2)}, u32[]{:S(2)}) collective-permute-start(f32[136,384]{1,0:T(8,128)S(1)} %collective-permute-done.36.r1), channel_id=1, source_target_pairs={{0,2},{2,0},{1,3},{3,1},{4,6},{6,4},{5,7},{7,5},{8,10},{10,8},{9,1... | collective-permute-start | bytes 626696 | tf_op jit(solution)/shard_map/ppermute | solution.py:530
  152.4 1.5 collective-permute-start.40
  152.4 1.8 collective-permute-start.41
  157.2 10.4 %collective-permute-start.42 = (f32[256,384]{1,0:T(8,128)S(1)}, f32[256,384]{1,0:T(8,128)S(1)}, u32[]{:S(2)}, u32[]{:S(2)}) collective-permute-start(f32[256,384]{1,0:T(8,128)S(1)} %get-tuple-element.110), channel_id=1, source_target_pairs={{0,4},{2,7},{4,1},{6,2},{1,5},{3,6},{5,0},{7,3},{8,12},{10,15},{12... | collective-permute-start | bytes 1179656 | tf_op jit(solution)/shard_map/ppermute | solution.py:664
  159.0 11.1 %collective-permute-start.43 = (f32[256,384]{1,0:T(8,128)S(1)}, f32[256,384]{1,0:T(8,128)S(1)}, u32[]{:S(2)}, u32[]{:S(2)}) collective-permute-start(f32[256,384]{1,0:T(8,128)S(1)} %get-tuple-element.111), channel_id=1, source_target_pairs={{0,5},{2,6},{4,0},{6,3},{1,4},{3,7},{5,1},{7,2},{8,13},{10,14},{12... | collective-permute-start | bytes 1179656 | tf_op jit(solution)/shard_map/ppermute | solution.py:665
  170.2 19.2 %collective-permute-start.44 = (f32[256,384]{1,0:T(8,128)S(1)}, f32[256,384]{1,0:T(8,128)S(1)}, u32[]{:S(2)}, u32[]{:S(2)}) collective-permute-start(f32[256,384]{1,0:T(8,128)S(1)} %add_relay.1), channel_id=1, source_target_pairs={{0,4},{2,7},{4,1},{6,2},{1,5},{3,6},{5,0},{7,3},{8,12},{10,15},{12... | collective-permute-start | bytes 1179656 | tf_op jit(solution)/shard_map/ppermute | solution.py:675
  170.3 12.2 %collective-permute-start.45 = (f32[4,4,384]{2,1,0:T(4,128)S(1)}, f32[4,4,384]{2,1,0:T(4,128)S(1)}, u32[]{:S(2)}, u32[]{:S(2)}) collective-permute-start(f32[4,4,384]{2,1,0:T(4,128)S(1)} %get-tuple-element.118), channel_id=1, source_target_pairs={{0,0},{1,2},{2,1},{3,3},{32,32},{33,34},{34,33},{35,35},{64,64},{6... | collective-permute-start | bytes 73736 | tf_op jit(solution)/shard_map/ppermute | solution.py:680
  175.1 7.4 %collective-permute-start.46 = (f32[4,4,384]{2,1,0:T(4,128)S(1)}, f32[4,4,384]{2,1,0:T(4,128)S(1)}, u32[]{:S(2)}, u32[]{:S(2)}) collective-permute-start(f32[4,4,384]{2,1,0:T(4,128)S(1)} %get-tuple-element.119), channel_id=1, source_target_pairs={{0,32},{1,34},{2,33},{3,35},{32,64},{33,66},{34,65},{35,67},{64,96... | collective-permute-start | bytes 73736 | tf_op jit(solution)/shard_map/ppermute | solution.py:680
  178.4 7.2 %collective-permute-start.47 = (f32[4,4,384]{2,1,0:T(4,128)S(1)}, f32[4,4,384]{2,1,0:T(4,128)S(1)}, u32[]{:S(2)}, u32[]{:S(2)}) collective-permute-start(f32[4,4,384]{2,1,0:T(4,128)S(1)} %get-tuple-element.120), channel_id=1, source_target_pairs={{0,64},{1,66},{2,65},{3,67},{32,96},{33,98},{34,97},{35,99},{64,0}... | collective-permute-start | bytes 73736 | tf_op jit(solution)/shard_map/ppermute | solution.py:680
  182.5 6.9 %collective-permute-start.48 = (f32[4,4,384]{2,1,0:T(4,128)S(1)}, f32[4,4,384]{2,1,0:T(4,128)S(1)}, u32[]{:S(2)}, u32[]{:S(2)}) collective-permute-start(f32[4,4,384]{2,1,0:T(4,128)S(1)} %get-tuple-element.121), channel_id=1, source_target_pairs={{0,96},{1,98},{2,97},{3,99},{32,0},{33,2},{34,1},{35,3},{64,32},{6... | collective-permute-start | bytes 73736 | tf_op jit(solution)/shard_map/ppermute | solution.py:680

commit v5 on v4

--- a/solution.py
+++ b/solution.py
@@ -570,13 +570,14 @@
     )(near, away, opposite)
     straights = both_ways(straight, z_axes, z_ring)
     spread = both_ways(quarters, x_axes, x_ring)
+    relays = lax.ppermute(straights[0], z_axes, z_ring(1)), lax.ppermute(spread[0], x_axes, x_ring(1))
     straights, spread, quarters = lax.optimization_barrier((straights, spread, quarters))
     mine = [
         *straights,
-        lax.ppermute(straights[0], z_axes, z_ring(1)),
+        relays[0],
         quarters,
         *spread,
-        lax.ppermute(spread[0], x_axes, x_ring(1)),
+        relays[1],
     ]
     weights = pl.pallas_call(
         columns_kernel,

time: 191 us -> 191 us (level)
  starting transfers between devices: 65.9 us -> 60.4 us
  waiting for transfers between devices: 81.6 us -> 86.1 us
    ppermute x1, waiting for transfers between devices: 0.01 us -> 8.01 us  [shards(): lax.ppermute(spread[0], x_axes, x_ring(1))]
    ppermute x3, waiting for transfers between devices: 7.57 us -> 0.01 us  [both_ways(): lax.ppermute(values, axes, ring(-1))]
    ppermute x3, waiting for transfers between devices: 4.85 us -> 12.2 us  [both_ways(): lax.ppermute(values, axes, ring(1))]
    ppermute x1, waiting for transfers between devices: 4.32 us -> 0.01 us  [shards(): lax.ppermute(straights[0], z_axes, z_ring(1))]
    ppermute x19, starting transfers between devices: 18.9 us -> 16.5 us  [swap(): return lax.ppermute(values, 'core', [(0, 1), (1, 0)])]
    ppermute x1, starting transfers between devices: 2.01 us -> 0.01 us  [shards(): lax.ppermute(spread[0], x_axes, x_ring(1))]
    ppermute x3, starting transfers between devices: 6.82 us -> 4.87 us  [both_ways(): lax.ppermute(values, axes, ring(1))]
where the time goes in v5:
time: 191 us; the launch traced here: 190 us
  waiting for transfers between devices  86.1 us (45%)
  starting transfers between devices  60.4 us (32%)
  Pallas kernels  40.6 us (21%)
    ppermute x6, waiting for transfers between devices, hop(): half = lax.ppermute(half, 'y', pairs)  19.3 us
    ppermute x19, starting transfers between devices, swap(): return lax.ppermute(values, 'core', [(0, 1), (1, 0)])  16.5 us
    pallas_call x4, Pallas kernels, backward(): pl.pallas_call(lambda *refs: backward_kernel(not halves, full, *refs), ou...  15 us
    pallas_call x4, Pallas kernels, forward(): pl.pallas_call(lambda *refs: forward_kernel(not halves, full, *refs), out...  13.5 us
    ppermute x3, waiting for transfers between devices, both_ways(): lax.ppermute(values, axes, ring(1))  12.2 us
    ppermute x4, starting transfers between devices, shards(): lax.ppermute(cells[step], ('y', 'core', 'xh'), stem_pairs(step))  11.5 us
    ppermute x19, waiting for transfers between devices, swap(): return lax.ppermute(values, 'core', [(0, 1), (1, 0)])  10.3 us
    ppermute x1, waiting for transfers between devices, shards(): relay = lax.ppermute(partial[2], x_axes, x_ring(1))  8.86 us
  transfers between devices with their start and end apart: 49, of which 27 were waited for; matrix products, arithmetic and copies ran while one was open for 0% of the time, Pallas kernels for 0%

profile of v5, /device:TPU:25, one launch (start us, length us, event | category | flops | bytes accessed | tf_op | source)
XLA Modules:
  0.0 189.7 jit_solution(15485824197399949681)
XLA Ops:
  0.9 0.7 stack.47.where.refs_0_
  1.5 3.2 %pack.1 = (f32[208,768]{1,0:T(8,128)}, f32[64,768]{1,0:T(8,128)}, f32[64,384]{1,0:T(8,128)}, f32[8,768]{1,0:T(8,128)}) custom-call(s32[11]{0:T(128)} %stack.47.where.refs_0_, bf16[1,720,360]{2,1,0:T(8,128)(2,1)} %refs_14_.1, bf16[1,360,360]{2,1,0:T(8,128)(2,1)} %refs_15_.1, bf16[1,360,720]{2,1,0:T(8,128)(2,1)} %refs_16_.1, bf16[1,9,360]{2,1,0:T(8,128)(2,1)} %refs_3_.1, ...), custom_call_target="tpu_custom_call" | custom-call | tf_op jit(solution)/shard_map/pack/pallas_call | solution.py:539
  4.7 1.7 collective-permute-start.1
  6.4 2.2 %collective-permute-start = (f32[64,768]{1,0:T(8,128)}, f32[64,768]{1,0:T(8,128)S(1)}, u32[]{:S(2)}, u32[]{:S(2)}) collective-permute-start(f32[64,768]{1,0:T(8,128)} %get-tuple-element.66), channel_id=1, source_target_pairs={{0,8},{2,26},{8,16},{10,2},{16,24},{18,10},{24,0},{26,18},{1,9},{3... | collective-permute-start | bytes 589832 | tf_op jit(solution)/shard_map/ppermute | solution.py:557
  8.6 2.7 %collective-permute-start.3 = (f32[64,384]{1,0:T(8,128)}, f32[64,384]{1,0:T(8,128)S(1)}, u32[]{:S(2)}, u32[]{:S(2)}) collective-permute-start(f32[64,384]{1,0:T(8,128)} %get-tuple-element.67), channel_id=1, source_target_pairs={{0,2},{1,0},{2,3},{3,1},{4,6},{5,4},{6,7},{7,5},{8,10},{9,8},{10,1... | collective-permute-start | bytes 294920 | tf_op jit(solution)/shard_map/ppermute | solution.py:554
  11.4 3.2 %collective-permute-start.2 = (f32[64,384]{1,0:T(8,128)}, f32[64,384]{1,0:T(8,128)S(1)}, u32[]{:S(2)}, u32[]{:S(2)}) collective-permute-start(f32[64,384]{1,0:T(8,128)} %get-tuple-element.67), channel_id=1, source_target_pairs={{0,0},{1,2},{2,1},{3,3},{4,4},{5,6},{6,5},{7,7},{8,8},{9,10},{10,9... | collective-permute-start | bytes 294920 | tf_op jit(solution)/shard_map/ppermute | solution.py:553
  14.6 4.5 %collective-permute-done.2.refs_1_.refs_3_.refs_7_.same_ref = f32[64,384]{1,0:T(8,128)S(1)} collective-permute-done((f32[64,384]{1,0:T(8,128)}, f32[64,384]{1,0:T(8,128)S(1)}, u32[]{:S(2)}, u32[]{:S(2)}) %collective-permute-start.2) | collective-permute-done | bytes 98336 | tf_op jit(solution)/shard_map/ppermute | solution.py:553
  19.0 1.4 collective-permute-start.4
  20.4 3.1 %collective-permute-done.4.third = f32[64,768]{1,0:T(8,128)S(1)} collective-permute-done((f32[64,768]{1,0:T(8,128)S(1)}, f32[64,768]{1,0:T(8,128)S(1)}, u32[]{:S(2)}, u32[]{:S(2)}) %collective-permute-start.4) | collective-permute-done | bytes 196640 | tf_op jit(solution)/shard_map/ppermute | solution.py:561
  23.5 2.6 %collective-permute-start.5 = (f32[208,768]{1,0:T(8,128)}, f32[208,768]{1,0:T(8,128)S(1)}, u32[]{:S(2)}, u32[]{:S(2)}) collective-permute-start(f32[208,768]{1,0:T(8,128)} %get-tuple-element.72), channel_id=1, source_target_pairs={{0,8},{2,26},{8,16},{10,2},{16,24},{18,10},{24,0},{26,18},{1,9},{3... | collective-permute-start | bytes 1916936 | tf_op jit(solution)/shard_map/ppermute | solution.py:557
  26.3 1.5 collective-permute-start.8
  27.7 12.2 %collective-permute-done.5.refs_0_ = f32[208,768]{1,0:T(8,128)S(1)} collective-permute-done((f32[208,768]{1,0:T(8,128)}, f32[208,768]{1,0:T(8,128)S(1)}, u32[]{:S(2)}, u32[]{:S(2)}) %collective-permute-start.5) | collective-permute-done | bytes 639008 | tf_op jit(solution)/shard_map/ppermute | solution.py:557
  39.9 3.3 %collective-permute-start.9 = (f32[208,768]{1,0:T(8,128)S(1)}, f32[208,768]{1,0:T(8,128)S(1)}, u32[]{:S(2)}, u32[]{:S(2)}) collective-permute-start(f32[208,768]{1,0:T(8,128)S(1)} %collective-permute-done.5.refs_0_), channel_id=1, source_target_pairs={{0,8},{2,26},{8,16},{10,2},{16,24},{18,10},{24,0},{26,18},{1,9},{3... | collective-permute-start | bytes 1916936 | tf_op jit(solution)/shard_map/ppermute | solution.py:573
  44.3 8.0 %collective-permute-done.10.refs_6_ = f32[192,768]{1,0:T(8,128)S(1)} collective-permute-done((f32[192,768]{1,0:T(8,128)S(1)}, f32[192,768]{1,0:T(8,128)S(1)}, u32[]{:S(2)}, u32[]{:S(2)}) %collective-permute-start.10) | collective-permute-done | bytes 589856 | tf_op jit(solution)/shard_map/ppermute | solution.py:573
  52.3 2.1 %collective-permute-start.12 = (f32[208,768]{1,0:T(8,128)S(1)}, f32[208,768]{1,0:T(8,128)S(1)}, u32[]{:S(2)}, u32[]{:S(2)}) collective-permute-start(f32[208,768]{1,0:T(8,128)S(1)} %collective-permute-done.6.refs_1_), channel_id=1, source_target_pairs={{0,2},{2,0},{1,3},{3,1},{4,6},{6,4},{5,7},{7,5},{8,10},{10,8},{9,1... | collective-permute-start | bytes 1916936 | tf_op jit(solution)/shard_map/ppermute | solution.py:530
  55.0 2.9 %collective-permute-done.16.refs_12_ = f32[192,768]{1,0:T(8,128)S(1)} collective-permute-done((f32[192,768]{1,0:T(8,128)S(1)}, f32[192,768]{1,0:T(8,128)S(1)}, u32[]{:S(2)}, u32[]{:S(2)}) %collective-permute-start.16) | collective-permute-done | bytes 589856 | tf_op jit(solution)/shard_map/ppermute | solution.py:530
  57.9 0.8 collective-permute-done.17.refs_13_
  58.7 0.7 copy-done.7
  59.5 2.6 %columns.1 = (bf16[4,720,360]{2,1,0:T(8,128)(2,1)S(1)}, bf16[4,360,360]{2,1,0:T(8,128)(2,1)S(1)}, bf16[4,360,720]{2,1,0:T(8,128)(2,1)S(1)}, f32[4,8,768]{2,1,0:T(8,128)S(1)}) custom-call(s32[11]{0:T(128)S(1)} %copy-done.6, f32[208,768]{1,0:T(8,128)S(1)} %collective-permute-done.5.refs_0_, f32[208,768]{1,0:T(8,128)S(1)} %collective-permute-done.6.refs_1_, ...), custom_call_target="tpu_custom_call" | custom-call | tf_op jit(solution)/shard_map/columns/pallas_call | solution.py:582
  62.0 3.2 %forward_light.3 = f32[96,384]{1,0:T(8,128)S(1)} custom-call(s32[11]{0:T(128)S(1)} %copy-done.6, f32[64,384]{1,0:T(8,128)S(1)} %collective-permute-done.2.refs_1_.refs_3_.refs_7_.same_ref, f32[64,384]{1,0:T(8,128)S(1)} %collective-permute-done.3.refs_2_.refs_4_.refs_8_.cross_ref, ...), custom_call_target="tpu_custom_call" | custom-call | tf_op jit(solution)/shard_map/forward_light/pallas_call | solution.py:599
  65.3 0.7 collective-permute-start.18
  65.9 0.6 collective-permute-start.19
  66.6 1.0 collective-permute-done.19.refs_2_
  67.6 3.2 %forward_light.4 = f32[96,384]{1,0:T(8,128)S(1)} custom-call(s32[11]{0:T(128)S(1)} %copy-done.6, f32[96,384]{1,0:T(8,128)S(1)} %collective-permute-done.18.refs_1_, f32[96,384]{1,0:T(8,128)S(1)} %collective-permute-done.19.refs_2_, f32[64,384]{1,0:T(8,128)S(1)} %collective-permute-done.2.refs_1_.refs_3_.refs_7_.same_ref, ...), custom_call_target="tpu_custom_call" | custom-call | tf_op jit(solution)/shard_map/forward_light/pallas_call | solution.py:599
  70.8 0.7 collective-permute-start.20
  71.9 1.0 collective-permute-done.21.refs_2_.refs_4_
  73.0 3.2 %forward_light.5 = f32[96,384]{1,0:T(8,128)S(1)} custom-call(s32[11]{0:T(128)S(1)} %copy-done.6, f32[96,384]{1,0:T(8,128)S(1)} %collective-permute-done.20.refs_1_.refs_3_, f32[96,384]{1,0:T(8,128)S(1)} %collective-permute-done.21.refs_2_.refs_4_, f32[64,384]{1,0:T(8,128)S(1)} %collective-permute-done.2.refs_1_.refs_3_.refs_7_.same_ref, ...), custom_call_target="tpu_custom_call" | custom-call | tf_op jit(solution)/shard_map/forward_light/pallas_call | solution.py:599
  76.2 1.4 collective-permute-start.22
  77.6 16.3 %collective-permute-done.22.refs_5_ = f32[96,384]{1,0:T(8,128)S(1)} collective-permute-done((f32[96,384]{1,0:T(8,128)S(1)}, f32[96,384]{1,0:T(8,128)S(1)}, u32[]{:S(2)}, u32[]{:S(2)}) %collective-permute-start.22) | collective-permute-done | bytes 147488 | tf_op jit(solution)/shard_map/ppermute | solution.py:610
  94.0 0.9 collective-permute-start.23
  94.8 1.0 collective-permute-done.23.refs_6_
  95.8 3.9 %forward_full.1 = (f32[192,384]{1,0:T(8,128)S(1)}, f32[4,128,360]{2,1,0:T(8,128)S(1)}, f32[4,128,360]{2,1,0:T(8,128)S(1)}, f32[4,32,720]{2,1,0:T(8,128)S(1)}, f3...) custom-call(s32[11]{0:T(128)S(1)} %copy-done.6, ...), custom_call_target="tpu_custom_call" | custom-call | tf_op jit(solution)/shard_map/forward_full/pallas_call | solution.py:599
  99.8 1.8 head.1.refs_1_.refs_7_
  101.6 3.5 %backward_light.3 = f32[96,384]{1,0:T(8,128)S(1)} custom-call(s32[11]{0:T(128)S(1)} %copy-done.6, f32[192,384]{1,0:T(8,128)S(1)} %head.1.refs_1_.refs_7_, f32[4,128,360]{2,1,0:T(8,128)S(1)} %get-tuple-element.87.refs_2_.refs_3_.refs_8_, f32[4,32,720]{2,1,0:T(8,128)S(1)} %get-tuple-element.88.refs_3_.refs_4_.refs_9_, ...), custom_call_target="tpu_custom_call" | custom-call | tf_op jit(solution)/shard_map/backward_light/pallas_call | solution.py:635
  105.1 1.3 collective-permute-start.24
  106.4 3.0 %collective-permute-done.24.refs_1_ = f32[96,384]{1,0:T(8,128)S(1)} collective-permute-done((f32[96,384]{1,0:T(8,128)S(1)}, f32[96,384]{1,0:T(8,128)S(1)}, u32[]{:S(2)}, u32[]{:S(2)}) %collective-permute-start.24) | collective-permute-done | bytes 147488 | tf_op jit(solution)/shard_map/ppermute | solution.py:610
  109.3 1.1 collective-permute-start.25
  110.4 1.0 collective-permute-done.25.refs_2_
  111.4 3.5 %backward_light.4 = f32[96,384]{1,0:T(8,128)S(1)} custom-call(s32[11]{0:T(128)S(1)} %copy-done.6, f32[96,384]{1,0:T(8,128)S(1)} %collective-permute-done.24.refs_1_, f32[96,384]{1,0:T(8,128)S(1)} %collective-permute-done.25.refs_2_, f32[4,128,360]{2,1,0:T(8,128)S(1)} %get-tuple-element.87.refs_2_.refs_3_.refs_8_, ...), custom_call_target="tpu_custom_call" | custom-call | tf_op jit(solution)/shard_map/backward_light/pallas_call | solution.py:635
  114.9 0.7 collective-permute-start.26
  115.6 2.8 %collective-permute-start.28 = (f32[112,384]{1,0:T(8,128)S(1)}, f32[112,384]{1,0:T(8,128)S(1)}, u32[]{:S(2)}, u32[]{:S(2)}) collective-permute-start(f32[112,384]{1,0:T(8,128)S(1)} %get-tuple-element.89), channel_id=1, source_target_pairs={{0,8},{2,26},{8,16},{10,2},{16,24},{18,10},{24,0},{26,18},{1,9},{3... | collective-permute-start | bytes 516104 | tf_op jit(solution)/shard_map/ppermute | solution.py:533
  118.3 1.5 collective-permute-start.30
  119.8 0.6 collective-permute-start.27
  120.4 0.9 collective-permute-done.28.l1
  121.4 2.4 %collective-permute-done.29.l2 = f32[112,384]{1,0:T(8,128)S(1)} collective-permute-done((f32[112,384]{1,0:T(8,128)S(1)}, f32[112,384]{1,0:T(8,128)S(1)}, u32[]{:S(2)}, u32[]{:S(2)}) %collective-permute-start.29) | collective-permute-done | bytes 172064 | tf_op jit(solution)/shard_map/ppermute | solution.py:534
  123.8 4.2 %collective-permute-done.30.l3 = f32[112,384]{1,0:T(8,128)S(1)} collective-permute-done((f32[112,384]{1,0:T(8,128)S(1)}, f32[112,384]{1,0:T(8,128)S(1)}, u32[]{:S(2)}, u32[]{:S(2)}) %collective-permute-start.30) | collective-permute-done | bytes 172064 | tf_op jit(solution)/shard_map/ppermute | solution.py:535
  128.0 3.5 %backward_light.5 = f32[96,384]{1,0:T(8,128)S(1)} custom-call(s32[11]{0:T(128)S(1)} %copy-done.6, f32[96,384]{1,0:T(8,128)S(1)} %collective-permute-done.26.refs_1_.refs_3_, f32[96,384]{1,0:T(8,128)S(1)} %collective-permute-done.27.refs_2_.refs_4_, f32[4,128,360]{2,1,0:T(8,128)S(1)} %get-tuple-element.87.refs_2_.refs_3_.refs_8_, ...), custom_call_target="tpu_custom_call" | custom-call | tf_op jit(solution)/shard_map/backward_light/pallas_call | solution.py:635
  131.5 0.7 collective-permute-start.31
  132.1 0.9 collective-permute-start.33
  135.0 4.6 %backward_full.1 = (f32[136,384]{1,0:T(8,128)S(1)}, f32[136,384]{1,0:T(8,128)S(1)}, f32[136,384]{1,0:T(8,128)S(1)}, f32[240,384]{1,0:T(8,128)S(1)}, f32[16,384]{1,0:T(8,128)S(1)}) custom-call(s32[11]{0:T(128)S(1)} %copy-done.6, f32[96,384]{1,0:T(8,128)S(1)} %collective-permute-done.24.refs_1_, f32[96,384]{1,0:T(8,128)S(1)} %collective-permute-done.25.refs_2_, ...), custom_call_target="tpu_custom_call" | custom-call | tf_op jit(solution)/shard_map/backward_full/pallas_call | solution.py:635
  139.6 1.3 collective-permute-start.36
  141.1 1.0 collective-permute-start.38
  142.1 3.9 %collective-permute-done.36.r1 = f32[136,384]{1,0:T(8,128)S(1)} collective-permute-done((f32[136,384]{1,0:T(8,128)S(1)}, f32[136,384]{1,0:T(8,128)S(1)}, u32[]{:S(2)}, u32[]{:S(2)}) %collective-permute-start.36) | collective-permute-done | bytes 208928 | tf_op jit(solution)/shard_map/ppermute | solution.py:533
  146.0 7.1 %collective-permute-start.39 = (f32[136,384]{1,0:T(8,128)S(1)}, f32[136,384]{1,0:T(8,128)S(1)}, u32[]{:S(2)}, u32[]{:S(2)}) collective-permute-start(f32[136,384]{1,0:T(8,128)S(1)} %collective-permute-done.36.r1), channel_id=1, source_target_pairs={{0,2},{2,0},{1,3},{3,1},{4,6},{6,4},{5,7},{7,5},{8,10},{10,8},{9,1... | collective-permute-start | bytes 626696 | tf_op jit(solution)/shard_map/ppermute | solution.py:530
  154.9 3.1 %weight_grads.1 = (f32[256,384]{1,0:T(8,128)S(1)}, f32[256,384]{1,0:T(8,128)S(1)}, f32[256,384]{1,0:T(8,128)S(1)}, f32[256,384]{1,0:T(8,128)S(1)}, f32[4,4,384]{...) custom-call(s32[11]{0:T(128)S(1)} %copy-done.6, ...), custom_call_target="tpu_custom_call" | custom-call | tf_op jit(solution)/shard_map/weight_grads/pallas_call | solution.py:656
  158.1 1.5 collective-permute-start.43
  159.5 8.9 %collective-permute-done.42.second = f32[256,384]{1,0:T(8,128)S(1)} collective-permute-done((f32[256,384]{1,0:T(8,128)S(1)}, f32[256,384]{1,0:T(8,128)S(1)}, u32[]{:S(2)}, u32[]{:S(2)}) %collective-permute-start.42) | collective-permute-done | bytes 393248 | tf_op jit(solution)/shard_map/ppermute | solution.py:665
  168.4 1.5 collective-permute-done.43.far
  170.0 4.2 %collective-permute-start.45 = (f32[4,4,384]{2,1,0:T(4,128)S(1)}, f32[4,4,384]{2,1,0:T(4,128)S(1)}, u32[]{:S(2)}, u32[]{:S(2)}) collective-permute-start(f32[4,4,384]{2,1,0:T(4,128)S(1)} %get-tuple-element.118), channel_id=1, source_target_pairs={{0,0},{1,2},{2,1},{3,3},{32,32},{33,34},{34,33},{35,35},{64,64},{6... | collective-permute-start | bytes 73736 | tf_op jit(solution)/shard_map/ppermute | solution.py:681
  174.2 2.9 %collective-permute-start.46 = (f32[4,4,384]{2,1,0:T(4,128)S(1)}, f32[4,4,384]{2,1,0:T(4,128)S(1)}, u32[]{:S(2)}, u32[]{:S(2)}) collective-permute-start(f32[4,4,384]{2,1,0:T(4,128)S(1)} %get-tuple-element.119), channel_id=1, source_target_pairs={{0,32},{1,34},{2,33},{3,35},{32,64},{33,66},{34,65},{35,67},{64,96... | collective-permute-start | bytes 73736 | tf_op jit(solution)/shard_map/ppermute | solution.py:681
  177.1 4.5 %collective-permute-start.47 = (f32[4,4,384]{2,1,0:T(4,128)S(1)}, f32[4,4,384]{2,1,0:T(4,128)S(1)}, u32[]{:S(2)}, u32[]{:S(2)}) collective-permute-start(f32[4,4,384]{2,1,0:T(4,128)S(1)} %get-tuple-element.120), channel_id=1, source_target_pairs={{0,64},{1,66},{2,65},{3,67},{32,96},{33,98},{34,97},{35,99},{64,0}... | collective-permute-start | bytes 73736 | tf_op jit(solution)/shard_map/ppermute | solution.py:681
  181.6 2.7 %collective-permute-done.47.c2 = f32[4,4,384]{2,1,0:T(4,128)S(1)} collective-permute-done((f32[4,4,384]{2,1,0:T(4,128)S(1)}, f32[4,4,384]{2,1,0:T(4,128)S(1)}, u32[]{:S(2)}, u32[]{:S(2)}) %collective-permute-start.47) | collective-permute-done | bytes 24608 | tf_op jit(solution)/shard_map/ppermute | solution.py:681
  184.2 4.2 %collective-permute-done.48.c3 = f32[4,4,384]{2,1,0:T(4,128)S(1)} collective-permute-done((f32[4,4,384]{2,1,0:T(4,128)S(1)}, f32[4,4,384]{2,1,0:T(4,128)S(1)}, u32[]{:S(2)}, u32[]{:S(2)}) %collective-permute-start.48) | collective-permute-done | bytes 24608 | tf_op jit(solution)/shard_map/ppermute | solution.py:681
  188.4 1.3 final.1
  (66 shorter events, 6.4 us)
Async XLA Ops:
  0.6 58.1 %copy-start.1 = (bf16[1,360,720]{2,1,0:T(8,128)(2,1)S(1)}, bf16[1,360,720]{2,1,0:T(8,128)(2,1)}, u32[]{:S(2)}) copy-start(bf16[1,360,720]{2,1,0:T(8,128)(2,1)} %refs_16_.1) | copy-start | bytes 1555204
  0.6 58.1 %copy-start.2 = (bf16[1,360,360]{2,1,0:T(8,128)(2,1)S(1)}, bf16[1,360,360]{2,1,0:T(8,128)(2,1)}, u32[]{:S(2)}) copy-start(bf16[1,360,360]{2,1,0:T(8,128)(2,1)} %refs_15_.1) | copy-start | bytes 777604
  0.7 58.0 %copy-start = (bf16[1,720,360]{2,1,0:T(8,128)(2,1)S(1)}, bf16[1,720,360]{2,1,0:T(8,128)(2,1)}, u32[]{:S(2)}) copy-start(bf16[1,720,360]{2,1,0:T(8,128)(2,1)} %refs_14_.1) | copy-start | bytes 1555204
  1.5 57.2 %copy-start.6 = (s32[11]{0:T(128)S(1)}, s32[11]{0:T(128)}, u32[]{:S(2)}) copy-start(s32[11]{0:T(128)} %stack.47.where.refs_0_) | copy-start | bytes 136
  4.7 14.3 %collective-permute-start.1 = (f32[64,768]{1,0:T(8,128)}, f32[64,768]{1,0:T(8,128)S(1)}, u32[]{:S(2)}, u32[]{:S(2)}) collective-permute-start(f32[64,768]{1,0:T(8,128)} %get-tuple-element.66), channel_id=1, source_target_pairs={{0,24},{2,10},{8,0},{10,18},{16,8},{18,26},{24,16},{26,2},{1,25},{... | collective-permute-start | bytes 589832 | tf_op jit(solution)/shard_map/ppermute | solution.py:557
  6.4 12.6 %collective-permute-start = (f32[64,768]{1,0:T(8,128)}, f32[64,768]{1,0:T(8,128)S(1)}, u32[]{:S(2)}, u32[]{:S(2)}) collective-permute-start(f32[64,768]{1,0:T(8,128)} %get-tuple-element.66), channel_id=1, source_target_pairs={{0,8},{2,26},{8,16},{10,2},{16,24},{18,10},{24,0},{26,18},{1,9},{3... | collective-permute-start | bytes 589832 | tf_op jit(solution)/shard_map/ppermute | solution.py:557
  8.6 5.9 %collective-permute-start.3 = (f32[64,384]{1,0:T(8,128)}, f32[64,384]{1,0:T(8,128)S(1)}, u32[]{:S(2)}, u32[]{:S(2)}) collective-permute-start(f32[64,384]{1,0:T(8,128)} %get-tuple-element.67), channel_id=1, source_target_pairs={{0,2},{1,0},{2,3},{3,1},{4,6},{5,4},{6,7},{7,5},{8,10},{9,8},{10,1... | collective-permute-start | bytes 294920 | tf_op jit(solution)/shard_map/ppermute | solution.py:554
  11.4 7.6 %collective-permute-start.2 = (f32[64,384]{1,0:T(8,128)}, f32[64,384]{1,0:T(8,128)S(1)}, u32[]{:S(2)}, u32[]{:S(2)}) collective-permute-start(f32[64,384]{1,0:T(8,128)} %get-tuple-element.67), channel_id=1, source_target_pairs={{0,0},{1,2},{2,1},{3,3},{4,4},{5,6},{6,5},{7,7},{8,8},{9,10},{10,9... | collective-permute-start | bytes 294920 | tf_op jit(solution)/shard_map/ppermute | solution.py:553
  19.0 4.5 %collective-permute-start.4 = (f32[64,768]{1,0:T(8,128)S(1)}, f32[64,768]{1,0:T(8,128)S(1)}, u32[]{:S(2)}, u32[]{:S(2)}) collective-permute-start(f32[64,768]{1,0:T(8,128)S(1)} %collective-permute-done.first), channel_id=1, source_target_pairs={{0,8},{2,26},{8,16},{10,2},{16,24},{18,10},{24,0},{26,18},{1,9},{3... | collective-permute-start | bytes 589832 | tf_op jit(solution)/shard_map/ppermute | solution.py:561
  23.5 16.4 %collective-permute-start.5 = (f32[208,768]{1,0:T(8,128)}, f32[208,768]{1,0:T(8,128)S(1)}, u32[]{:S(2)}, u32[]{:S(2)}) collective-permute-start(f32[208,768]{1,0:T(8,128)} %get-tuple-element.72), channel_id=1, source_target_pairs={{0,8},{2,26},{8,16},{10,2},{16,24},{18,10},{24,0},{26,18},{1,9},{3... | collective-permute-start | bytes 1916936 | tf_op jit(solution)/shard_map/ppermute | solution.py:557
  26.1 17.1 %collective-permute-start.6 = (f32[208,768]{1,0:T(8,128)}, f32[208,768]{1,0:T(8,128)S(1)}, u32[]{:S(2)}, u32[]{:S(2)}) collective-permute-start(f32[208,768]{1,0:T(8,128)} %get-tuple-element.72), channel_id=1, source_target_pairs={{0,24},{2,10},{8,0},{10,18},{16,8},{18,26},{24,16},{26,2},{1,25},{... | collective-permute-start | bytes 1916936 | tf_op jit(solution)/shard_map/ppermute | solution.py:557
  26.2 17.1 %collective-permute-start.7 = (f32[192,768]{1,0:T(8,128)S(1)}, f32[192,768]{1,0:T(8,128)S(1)}, u32[]{:S(2)}, u32[]{:S(2)}) collective-permute-start(f32[192,768]{1,0:T(8,128)S(1)} %join_quarters.1.refs_3_), channel_id=1, source_target_pairs={{0,4},{2,7},{4,1},{6,2},{1,5},{3,6},{5,0},{7,3},{8,12},{10,15},{12... | collective-permute-start | bytes 1769480 | tf_op jit(solution)/shard_map/ppermute | solution.py:557
  26.3 17.0 %collective-permute-start.8 = (f32[192,768]{1,0:T(8,128)S(1)}, f32[192,768]{1,0:T(8,128)S(1)}, u32[]{:S(2)}, u32[]{:S(2)}) collective-permute-start(f32[192,768]{1,0:T(8,128)S(1)} %join_quarters.1.refs_3_), channel_id=1, source_target_pairs={{0,5},{2,6},{4,0},{6,3},{1,4},{3,7},{5,1},{7,2},{8,13},{10,14},{12... | collective-permute-start | bytes 1769480 | tf_op jit(solution)/shard_map/ppermute | solution.py:557
  39.9 14.5 %collective-permute-start.9 = (f32[208,768]{1,0:T(8,128)S(1)}, f32[208,768]{1,0:T(8,128)S(1)}, u32[]{:S(2)}, u32[]{:S(2)}) collective-permute-start(f32[208,768]{1,0:T(8,128)S(1)} %collective-permute-done.5.refs_0_), channel_id=1, source_target_pairs={{0,8},{2,26},{8,16},{10,2},{16,24},{18,10},{24,0},{26,18},{1,9},{3... | collective-permute-start | bytes 1916936 | tf_op jit(solution)/shard_map/ppermute | solution.py:573
  43.3 9.0 %collective-permute-start.10 = (f32[192,768]{1,0:T(8,128)S(1)}, f32[192,768]{1,0:T(8,128)S(1)}, u32[]{:S(2)}, u32[]{:S(2)}) collective-permute-start(f32[192,768]{1,0:T(8,128)S(1)} %collective-permute-done.7.refs_4_), channel_id=1, source_target_pairs={{0,4},{2,7},{4,1},{6,2},{1,5},{3,6},{5,0},{7,3},{8,12},{10,15},{12... | collective-permute-start | bytes 1769480 | tf_op jit(solution)/shard_map/ppermute | solution.py:573
  43.3 11.1 %collective-permute-start.14 = (f32[192,768]{1,0:T(8,128)S(1)}, f32[192,768]{1,0:T(8,128)S(1)}, u32[]{:S(2)}, u32[]{:S(2)}) collective-permute-start(f32[192,768]{1,0:T(8,128)S(1)} %join_quarters.1.refs_3_), channel_id=1, source_target_pairs={{0,2},{2,0},{1,3},{3,1},{4,6},{6,4},{5,7},{7,5},{8,10},{10,8},{9,1... | collective-permute-start | bytes 1769480 | tf_op jit(solution)/shard_map/ppermute | solution.py:530
  43.8 11.2 %collective-permute-start.15 = (f32[192,768]{1,0:T(8,128)S(1)}, f32[192,768]{1,0:T(8,128)S(1)}, u32[]{:S(2)}, u32[]{:S(2)}) collective-permute-start(f32[192,768]{1,0:T(8,128)S(1)} %collective-permute-done.7.refs_4_), channel_id=1, source_target_pairs={{0,2},{2,0},{1,3},{3,1},{4,6},{6,4},{5,7},{7,5},{8,10},{10,8},{9,1... | collective-permute-start | bytes 1769480 | tf_op jit(solution)/shard_map/ppermute | solution.py:530
  43.9 14.0 %collective-permute-start.11 = (f32[208,768]{1,0:T(8,128)S(1)}, f32[208,768]{1,0:T(8,128)S(1)}, u32[]{:S(2)}, u32[]{:S(2)}) collective-permute-start(f32[208,768]{1,0:T(8,128)S(1)} %collective-permute-done.5.refs_0_), channel_id=1, source_target_pairs={{0,2},{2,0},{1,3},{3,1},{4,6},{6,4},{5,7},{7,5},{8,10},{10,8},{9,1... | collective-permute-start | bytes 1916936 | tf_op jit(solution)/shard_map/ppermute | solution.py:530
  52.3 5.6 %collective-permute-start.12 = (f32[208,768]{1,0:T(8,128)S(1)}, f32[208,768]{1,0:T(8,128)S(1)}, u32[]{:S(2)}, u32[]{:S(2)}) collective-permute-start(f32[208,768]{1,0:T(8,128)S(1)} %collective-permute-done.6.refs_1_), channel_id=1, source_target_pairs={{0,2},{2,0},{1,3},{3,1},{4,6},{6,4},{5,7},{7,5},{8,10},{10,8},{9,1... | collective-permute-start | bytes 1916936 | tf_op jit(solution)/shard_map/ppermute | solution.py:530
  54.4 4.3 %collective-permute-start.13 = (f32[208,768]{1,0:T(8,128)S(1)}, f32[208,768]{1,0:T(8,128)S(1)}, u32[]{:S(2)}, u32[]{:S(2)}) collective-permute-start(f32[208,768]{1,0:T(8,128)S(1)} %collective-permute-done.9.refs_2_), channel_id=1, source_target_pairs={{0,2},{2,0},{1,3},{3,1},{4,6},{6,4},{5,7},{7,5},{8,10},{10,8},{9,1... | collective-permute-start | bytes 1916936 | tf_op jit(solution)/shard_map/ppermute | solution.py:530
  54.4 3.4 %collective-permute-start.16 = (f32[192,768]{1,0:T(8,128)S(1)}, f32[192,768]{1,0:T(8,128)S(1)}, u32[]{:S(2)}, u32[]{:S(2)}) collective-permute-start(f32[192,768]{1,0:T(8,128)S(1)} %collective-permute-done.8.refs_5_), channel_id=1, source_target_pairs={{0,2},{2,0},{1,3},{3,1},{4,6},{6,4},{5,7},{7,5},{8,10},{10,8},{9,1... | collective-permute-start | bytes 1769480 | tf_op jit(solution)/shard_map/ppermute | solution.py:530
  54.9 3.8 %collective-permute-start.17 = (f32[192,768]{1,0:T(8,128)S(1)}, f32[192,768]{1,0:T(8,128)S(1)}, u32[]{:S(2)}, u32[]{:S(2)}) collective-permute-start(f32[192,768]{1,0:T(8,128)S(1)} %collective-permute-done.10.refs_6_), channel_id=1, source_target_pairs={{0,2},{2,0},{1,3},{3,1},{4,6},{6,4},{5,7},{7,5},{8,10},{10,8},{9,1... | collective-permute-start | bytes 1769480 | tf_op jit(solution)/shard_map/ppermute | solution.py:530
  58.7 0.7 copy-start.7
  65.3 0.7 collective-permute-start.18
  65.9 1.6 collective-permute-start.19
  70.8 0.7 collective-permute-start.20
  71.5 1.5 collective-permute-start.21
  76.2 23.6 %copy-start.3 = (bf16[720,512]{1,0:T(8,128)(2,1)S(1)}, bf16[720,512]{1,0:T(8,128)(2,1)}, u32[]{:S(2)}) copy-start(bf16[720,512]{1,0:T(8,128)(2,1)} %two_ref.1) | copy-start | bytes 2211844
  76.2 23.6 %copy-start.4 = (bf16[360,512]{1,0:T(8,128)(2,1)S(1)}, bf16[360,512]{1,0:T(8,128)(2,1)}, u32[]{:S(2)}) copy-start(bf16[360,512]{1,0:T(8,128)(2,1)} %one_ref.1) | copy-start | bytes 1105924
  76.2 23.6 %copy-start.5 = (bf16[512,150]{0,1:T(8,128)(2,1)S(1)}, bf16[512,150]{0,1:T(8,128)(2,1)}, u32[]{:S(2)}) copy-start(bf16[512,150]{0,1:T(8,128)(2,1)} %param.21) | copy-start | bytes 460804
  76.2 17.7 %collective-permute-start.22 = (f32[96,384]{1,0:T(8,128)S(1)}, f32[96,384]{1,0:T(8,128)S(1)}, u32[]{:S(2)}, u32[]{:S(2)}) collective-permute-start(f32[96,384]{1,0:T(8,128)S(1)} %forward_light.5), channel_id=1, source_target_pairs={{64,96},{65,97},{66,98},{67,99},{68,100},{69,101},{70,102},{71,103... | collective-permute-start | bytes 442376 | tf_op jit(solution)/shard_map/ppermute | solution.py:610
  94.0 1.9 collective-permute-start.23
  105.1 4.3 %collective-permute-start.24 = (f32[96,384]{1,0:T(8,128)S(1)}, f32[96,384]{1,0:T(8,128)S(1)}, u32[]{:S(2)}, u32[]{:S(2)}) collective-permute-start(f32[96,384]{1,0:T(8,128)S(1)} %backward_light.3), channel_id=1, source_target_pairs={{96,64},{97,65},{98,66},{99,67},{100,68},{101,69},{102,70},{103,71... | collective-permute-start | bytes 442376 | tf_op jit(solution)/shard_map/ppermute | solution.py:610
  109.3 2.1 %collective-permute-start.25 = (f32[96,384]{1,0:T(8,128)S(1)}, f32[96,384]{1,0:T(8,128)S(1)}, u32[]{:S(2)}, u32[]{:S(2)}) collective-permute-start(f32[96,384]{1,0:T(8,128)S(1)} %collective-permute-done.24.refs_1_), channel_id=1, source_target_pairs={{0,2},{2,0},{1,3},{3,1},{4,6},{6,4},{5,7},{7,5},{8,10},{10,8},{9,1... | collective-permute-start | bytes 442376 | tf_op jit(solution)/shard_map/ppermute | solution.py:530
  114.9 4.9 %collective-permute-start.26 = (f32[96,384]{1,0:T(8,128)S(1)}, f32[96,384]{1,0:T(8,128)S(1)}, u32[]{:S(2)}, u32[]{:S(2)}) collective-permute-start(f32[96,384]{1,0:T(8,128)S(1)} %backward_light.4), channel_id=1, source_target_pairs={{64,32},{65,33},{66,34},{67,35},{68,36},{69,37},{70,38},{71,39},{7... | collective-permute-start | bytes 442376 | tf_op jit(solution)/shard_map/ppermute | solution.py:610
  115.6 5.8 %collective-permute-start.28 = (f32[112,384]{1,0:T(8,128)S(1)}, f32[112,384]{1,0:T(8,128)S(1)}, u32[]{:S(2)}, u32[]{:S(2)}) collective-permute-start(f32[112,384]{1,0:T(8,128)S(1)} %get-tuple-element.89), channel_id=1, source_target_pairs={{0,8},{2,26},{8,16},{10,2},{16,24},{18,10},{24,0},{26,18},{1,9},{3... | collective-permute-start | bytes 516104 | tf_op jit(solution)/shard_map/ppermute | solution.py:533
  118.3 5.5 %collective-permute-start.29 = (f32[112,384]{1,0:T(8,128)S(1)}, f32[112,384]{1,0:T(8,128)S(1)}, u32[]{:S(2)}, u32[]{:S(2)}) collective-permute-start(f32[112,384]{1,0:T(8,128)S(1)} %get-tuple-element.90), channel_id=1, source_target_pairs={{0,24},{2,10},{8,0},{10,18},{16,8},{18,26},{24,16},{26,2},{1,25},{... | collective-permute-start | bytes 516104 | tf_op jit(solution)/shard_map/ppermute | solution.py:534
  118.3 9.6 %collective-permute-start.30 = (f32[112,384]{1,0:T(8,128)S(1)}, f32[112,384]{1,0:T(8,128)S(1)}, u32[]{:S(2)}, u32[]{:S(2)}) collective-permute-start(f32[112,384]{1,0:T(8,128)S(1)} %get-tuple-element.91), channel_id=1, source_target_pairs={{0,16},{2,18},{8,24},{10,26},{16,0},{18,2},{24,8},{26,10},{1,17},{... | collective-permute-start | bytes 516104 | tf_op jit(solution)/shard_map/ppermute | solution.py:535
  119.8 8.2 %collective-permute-start.27 = (f32[96,384]{1,0:T(8,128)S(1)}, f32[96,384]{1,0:T(8,128)S(1)}, u32[]{:S(2)}, u32[]{:S(2)}) collective-permute-start(f32[96,384]{1,0:T(8,128)S(1)} %collective-permute-done.26.refs_1_.refs_3_), channel_id=1, source_target_pairs={{0,2},{2,0},{1,3},{3,1},{4,6},{6,4},{5,7},{7,5},{8,10},{10,8},{9,1... | collective-permute-start | bytes 442376 | tf_op jit(solution)/shard_map/ppermute | solution.py:530
  131.5 2.1 %collective-permute-start.31 = (f32[96,384]{1,0:T(8,128)S(1)}, f32[96,384]{1,0:T(8,128)S(1)}, u32[]{:S(2)}, u32[]{:S(2)}) collective-permute-start(f32[96,384]{1,0:T(8,128)S(1)} %backward_light.5), channel_id=1, source_target_pairs={{32,0},{33,1},{34,2},{35,3},{36,4},{37,5},{38,6},{39,7},{40,8},{41... | collective-permute-start | bytes 442376 | tf_op jit(solution)/shard_map/ppermute | solution.py:610
  132.1 2.0 %collective-permute-start.33 = (f32[112,384]{1,0:T(8,128)S(1)}, f32[112,384]{1,0:T(8,128)S(1)}, u32[]{:S(2)}, u32[]{:S(2)}) collective-permute-start(f32[112,384]{1,0:T(8,128)S(1)} %collective-permute-done.28.l1), channel_id=1, source_target_pairs={{0,2},{2,0},{1,3},{3,1},{4,6},{6,4},{5,7},{7,5},{8,10},{10,8},{9,1... | collective-permute-start | bytes 516104 | tf_op jit(solution)/shard_map/ppermute | solution.py:530
  133.1 1.4 collective-permute-start.34
  133.2 1.6 collective-permute-start.35
  133.6 1.4 collective-permute-start.32
  139.6 6.5 %collective-permute-start.36 = (f32[136,384]{1,0:T(8,128)S(1)}, f32[136,384]{1,0:T(8,128)S(1)}, u32[]{:S(2)}, u32[]{:S(2)}) collective-permute-start(f32[136,384]{1,0:T(8,128)S(1)} %get-tuple-element.104), channel_id=1, source_target_pairs={{0,8},{2,26},{8,16},{10,2},{16,24},{18,10},{24,0},{26,18},{1,9},{3... | collective-permute-start | bytes 626696 | tf_op jit(solution)/shard_map/ppermute | solution.py:533
  140.8 12.3 %collective-permute-start.37 = (f32[136,384]{1,0:T(8,128)S(1)}, f32[136,384]{1,0:T(8,128)S(1)}, u32[]{:S(2)}, u32[]{:S(2)}) collective-permute-start(f32[136,384]{1,0:T(8,128)S(1)} %get-tuple-element.105), channel_id=1, source_target_pairs={{0,24},{2,10},{8,0},{10,18},{16,8},{18,26},{24,16},{26,2},{1,25},{... | collective-permute-start | bytes 626696 | tf_op jit(solution)/shard_map/ppermute | solution.py:534
  141.1 12.1 %collective-permute-start.38 = (f32[136,384]{1,0:T(8,128)S(1)}, f32[136,384]{1,0:T(8,128)S(1)}, u32[]{:S(2)}, u32[]{:S(2)}) collective-permute-start(f32[136,384]{1,0:T(8,128)S(1)} %get-tuple-element.106), channel_id=1, source_target_pairs={{0,16},{2,18},{8,24},{10,26},{16,0},{18,2},{24,8},{26,10},{1,17},{... | collective-permute-start | bytes 626696 | tf_op jit(solution)/shard_map/ppermute | solution.py:535
  146.0 8.2 %collective-permute-start.39 = (f32[136,384]{1,0:T(8,128)S(1)}, f32[136,384]{1,0:T(8,128)S(1)}, u32[]{:S(2)}, u32[]{:S(2)}) collective-permute-start(f32[136,384]{1,0:T(8,128)S(1)} %collective-permute-done.36.r1), channel_id=1, source_target_pairs={{0,2},{2,0},{1,3},{3,1},{4,6},{6,4},{5,7},{7,5},{8,10},{10,8},{9,1... | collective-permute-start | bytes 626696 | tf_op jit(solution)/shard_map/ppermute | solution.py:530
  153.1 1.5 collective-permute-start.40
  153.1 1.8 collective-permute-start.41
  158.0 10.4 %collective-permute-start.42 = (f32[256,384]{1,0:T(8,128)S(1)}, f32[256,384]{1,0:T(8,128)S(1)}, u32[]{:S(2)}, u32[]{:S(2)}) collective-permute-start(f32[256,384]{1,0:T(8,128)S(1)} %get-tuple-element.110), channel_id=1, source_target_pairs={{0,4},{2,7},{4,1},{6,2},{1,5},{3,6},{5,0},{7,3},{8,12},{10,15},{12... | collective-permute-start | bytes 1179656 | tf_op jit(solution)/shard_map/ppermute | solution.py:665
  158.1 11.8 %collective-permute-start.43 = (f32[256,384]{1,0:T(8,128)S(1)}, f32[256,384]{1,0:T(8,128)S(1)}, u32[]{:S(2)}, u32[]{:S(2)}) collective-permute-start(f32[256,384]{1,0:T(8,128)S(1)} %get-tuple-element.111), channel_id=1, source_target_pairs={{0,5},{2,6},{4,0},{6,3},{1,4},{3,7},{5,1},{7,2},{8,13},{10,14},{12... | collective-permute-start | bytes 1179656 | tf_op jit(solution)/shard_map/ppermute | solution.py:666
  169.9 18.5 %collective-permute-start.44 = (f32[256,384]{1,0:T(8,128)S(1)}, f32[256,384]{1,0:T(8,128)S(1)}, u32[]{:S(2)}, u32[]{:S(2)}) collective-permute-start(f32[256,384]{1,0:T(8,128)S(1)} %add_relay.1), channel_id=1, source_target_pairs={{0,4},{2,7},{4,1},{6,2},{1,5},{3,6},{5,0},{7,3},{8,12},{10,15},{12... | collective-permute-start | bytes 1179656 | tf_op jit(solution)/shard_map/ppermute | solution.py:676
  170.0 11.6 %collective-permute-start.45 = (f32[4,4,384]{2,1,0:T(4,128)S(1)}, f32[4,4,384]{2,1,0:T(4,128)S(1)}, u32[]{:S(2)}, u32[]{:S(2)}) collective-permute-start(f32[4,4,384]{2,1,0:T(4,128)S(1)} %get-tuple-element.118), channel_id=1, source_target_pairs={{0,0},{1,2},{2,1},{3,3},{32,32},{33,34},{34,33},{35,35},{64,64},{6... | collective-permute-start | bytes 73736 | tf_op jit(solution)/shard_map/ppermute | solution.py:681
  174.2 7.4 %collective-permute-start.46 = (f32[4,4,384]{2,1,0:T(4,128)S(1)}, f32[4,4,384]{2,1,0:T(4,128)S(1)}, u32[]{:S(2)}, u32[]{:S(2)}) collective-permute-start(f32[4,4,384]{2,1,0:T(4,128)S(1)} %get-tuple-element.119), channel_id=1, source_target_pairs={{0,32},{1,34},{2,33},{3,35},{32,64},{33,66},{34,65},{35,67},{64,96... | collective-permute-start | bytes 73736 | tf_op jit(solution)/shard_map/ppermute | solution.py:681
  177.1 7.2 %collective-permute-start.47 = (f32[4,4,384]{2,1,0:T(4,128)S(1)}, f32[4,4,384]{2,1,0:T(4,128)S(1)}, u32[]{:S(2)}, u32[]{:S(2)}) collective-permute-start(f32[4,4,384]{2,1,0:T(4,128)S(1)} %get-tuple-element.120), channel_id=1, source_target_pairs={{0,64},{1,66},{2,65},{3,67},{32,96},{33,98},{34,97},{35,99},{64,0}... | collective-permute-start | bytes 73736 | tf_op jit(solution)/shard_map/ppermute | solution.py:681
  181.5 6.9 %collective-permute-start.48 = (f32[4,4,384]{2,1,0:T(4,128)S(1)}, f32[4,4,384]{2,1,0:T(4,128)S(1)}, u32[]{:S(2)}, u32[]{:S(2)}) collective-permute-start(f32[4,4,384]{2,1,0:T(4,128)S(1)} %get-tuple-element.121), channel_id=1, source_target_pairs={{0,96},{1,98},{2,97},{3,99},{32,0},{33,2},{34,1},{35,3},{64,32},{6... | collective-permute-start | bytes 73736 | tf_op jit(solution)/shard_map/ppermute | solution.py:681
